TPU v7x, 128 devices: a whole 4x4x4 slice. The times are simulated.
128 devices in a mesh: shard: 16 (over x_hi, y, core), context: 2 (over x_lo), tensor: 4 (over z).
Axes of the slice: x: 4 (x_hi: 2, x_lo: 2; x = x_hi * 2 + x_lo), y: 4, z: 4, core: 2. Of those that a mesh axis runs over, the one named last changes fastest.
Arguments:
- hidden_in: bfloat16 [16, 1792, 1536], P('shard', ('context', 'tensor')), may hold values from -1.1953125 to 1.1953125
- cotangent: bfloat16 [16, 1792, 1536], P('shard', ('context', 'tensor')), may hold values from -9 to 9
- prefix: int32 [16], P('shard'), may hold values from 1 to 1344, as said below
- positions: int32 [16, 1792], P('shard', 'context'), may hold values from 0 to 3582, as said below
- norm_gains: float32 [2, 1536], replicated, may hold values from 0.38 to 2.5
- gains_first: float32 [2, 1536], replicated, may hold values from -0.0002695215 to 0.0002695215
- gains_second: float32 [2, 1536], replicated, may hold values from 6.253602e-09 to 1.8760806e-08
- input_weight: float32 [1536, 2560], P(('shard', 'context'), 'tensor'), may hold values from -0.22963966 to 0.22963966
- input_first: float32 [1536, 2560], P(('shard', 'context'), 'tensor'), may hold values from -8.9840505e-05 to 8.9840505e-05
- input_second: float32 [1536, 2560], P(('shard', 'context'), 'tensor'), may hold values from 1.2507204e-09 to 1.6676273e-08
- output_weight: float32 [1536, 1536], P('tensor', ('shard', 'context')), may hold values from -0.75 to 0.75
- output_first: float32 [1536, 1536], P('tensor', ('shard', 'context')), may hold values from -8.9840505e-05 to 8.9840505e-05
- output_second: float32 [1536, 1536], P('tensor', ('shard', 'context')), may hold values from 4.1690681e-10 to 1.2507204e-09
- expand_weight: float32 [2, 1536, 3840], P(None, ('shard', 'context'), 'tensor'), may hold values from -0.22963966 to 0.22963966
- expand_first: float32 [2, 1536, 3840], P(None, ('shard', 'context'), 'tensor'), may hold values from -8.9840505e-05 to 8.9840505e-05
- expand_second: float32 [2, 1536, 3840], P(None, ('shard', 'context'), 'tensor'), may hold values from 1.2507204e-09 to 1.6676273e-08
- shrink_weight: float32 [3840, 1536], P('tensor', ('shard', 'context')), may hold values from -0.09375 to 0.09375
- shrink_first: float32 [3840, 1536], P('tensor', ('shard', 'context')), may hold values from -8.9840505e-05 to 8.9840505e-05
- shrink_second: float32 [3840, 1536], P('tensor', ('shard', 'context')), may hold values from 1.2507204e-09 to 1.6676273e-08
Outputs:
- block_output: bfloat16 [16, 1792, 1536], P('shard', ('context', 'tensor'))
- input_gradient: float32 [16, 1792, 1536], P('shard', ('context', 'tensor'))
- gradient_norm: float32 [], replicated
- gains_momentum: float32 [2, 1536], replicated
- gains_variance: float32 [2, 1536], replicated
- gains_updated: float32 [2, 1536], replicated
- input_momentum: float32 [1536, 2560], P(('shard', 'context'), 'tensor')
- input_variance: float32 [1536, 2560], P(('shard', 'context'), 'tensor')
- input_updated: float32 [1536, 2560], P(('shard', 'context'), 'tensor')
- output_momentum: float32 [1536, 1536], P('tensor', ('shard', 'context'))
- output_variance: float32 [1536, 1536], P('tensor', ('shard', 'context'))
- output_updated: float32 [1536, 1536], P('tensor', ('shard', 'context'))
- expand_momentum: float32 [2, 1536, 3840], P(None, ('shard', 'context'), 'tensor')
- expand_variance: float32 [2, 1536, 3840], P(None, ('shard', 'context'), 'tensor')
- expand_updated: float32 [2, 1536, 3840], P(None, ('shard', 'context'), 'tensor')
- shrink_momentum: float32 [3840, 1536], P('tensor', ('shard', 'context'))
- shrink_variance: float32 [3840, 1536], P('tensor', ('shard', 'context'))
- shrink_updated: float32 [3840, 1536], P('tensor', ('shard', 'context'))
Inputs may be any that keep to these rules, and one draw needn't show every extreme that they name: The first sequence's prefix is exactly 1344. Within a sequence the positions start at 0 and rise by 1 or 2 from one token to the next; in the first sequence they rise by 2 throughout.
All inputs are finite; a program needn't handle non-finite values.
Results may differ from a plain program's by a relative error of at most 0.04.
Values may be sent and summed in bfloat16 or wider, within the bound.
A program may use at most 192 MiB of HBM per device.

v0:
```python
import math

import jax
import jax.numpy as jnp
from jax import lax
from jax.sharding import PartitionSpec as P

HD = 64
GROUP = 3
STEP = 10


EPS = 1e-05
RESID = 1.4 / math.sqrt(52.0)
ROPE_BASE = 10000.0
MAX_NORM = 1.0
RATE = 0.1
GAIN_RATE = 1.0
BETA_ONE = 0.9
BETA_TWO = 0.95
ADAM_EPS = 1e-08
DECAY = 0.1
NEG = -1e30


def angles(places):
    half_width = HD // 2
    frequency = ROPE_BASE ** (-2.0 * jnp.arange(half_width, dtype=jnp.float32) / HD)
    phase_turn = places.astype(jnp.float32)[..., None] * frequency
    return (jnp.cos(phase_turn), jnp.sin(phase_turn))


def rotate(values, cos_part, sin_part):
    half_width = values.shape[-1] // 2
    lower_half = values[..., :half_width]
    upper_half = values[..., half_width:]
    return jnp.concatenate(
        [
            lower_half * cos_part - upper_half * sin_part,
            upper_half * cos_part + lower_half * sin_part,
        ],
        axis=-1,
    )


def unrotate(gradient, cos_part, sin_part):
    half_width = gradient.shape[-1] // 2
    lower_half = gradient[..., :half_width]
    upper_half = gradient[..., half_width:]
    return jnp.concatenate(
        [
            lower_half * cos_part + upper_half * sin_part,
            upper_half * cos_part - lower_half * sin_part,
        ],
        axis=-1,
    )


def visible(query_count, key_count, row_start, prefix_len):
    row_index = row_start + jnp.arange(query_count, dtype=jnp.int32)[:, None]
    col_index = jnp.arange(key_count, dtype=jnp.int32)[None, :]
    return (col_index <= row_index) | (col_index < prefix_len)


def rms_parts(values):
    scaling = lax.rsqrt(jnp.mean(values * values, axis=-1, keepdims=True) + EPS)
    return (values * scaling, scaling)


def rms_back(gradient, normed, scaling):
    return scaling * (gradient - normed * jnp.mean(gradient * normed, axis=-1, keepdims=True))


def masked_scores(queries, key_rows, prefix_len, row_start):
    scores = jnp.einsum(
        "qgjd,kgd->gjqk", queries, key_rows, preferred_element_type=jnp.float32
    ) * HD ** (-0.5)
    return jnp.where(
        visible(queries.shape[0], key_rows.shape[0], row_start, prefix_len), scores, NEG
    )


def attend(queries, key_rows, value_rows, prefix_len, row_start):
    scores = masked_scores(queries, key_rows, prefix_len, row_start)
    row_max = jnp.max(scores, axis=-1, keepdims=True)
    shifted = jnp.exp(scores - row_max)
    exp_total = jnp.sum(shifted, axis=-1, keepdims=True)
    probs_low = (shifted / exp_total).astype(jnp.bfloat16)
    attended = jnp.einsum(
        "gjqk,kgd->qgjd", probs_low, value_rows, preferred_element_type=jnp.float32
    )
    return (attended, row_max[..., 0] + jnp.log(exp_total[..., 0]))


def attend_back(
    queries, key_rows, value_rows, prefix_len, row_start, log_total, attended, grad_attended
):
    scores = masked_scores(queries, key_rows, prefix_len, row_start)
    probs = jnp.exp(scores - log_total[..., None])
    grad_probs = jnp.einsum(
        "qgjd,kgd->gjqk", grad_attended, value_rows, preferred_element_type=jnp.float32
    )
    inner_sum = jnp.transpose(
        jnp.sum(grad_attended.astype(jnp.float32) * attended, axis=-1), (1, 2, 0)
    )
    grad_scores = (probs * (grad_probs - inner_sum[..., None])).astype(jnp.bfloat16)
    grad_queries = jnp.einsum(
        "gjqk,kgd->qgjd", grad_scores, key_rows, preferred_element_type=jnp.float32
    ) * HD ** (-0.5)
    grad_keys = jnp.einsum(
        "gjqk,qgjd->kgd", grad_scores, queries, preferred_element_type=jnp.float32
    ) * HD ** (-0.5)
    grad_values = jnp.einsum(
        "gjqk,qgjd->kgd",
        probs.astype(jnp.bfloat16),
        grad_attended,
        preferred_element_type=jnp.float32,
    )
    return (grad_queries, grad_keys, grad_values)


def fetch_weights(masters):
    lowered = tuple((master.astype(jnp.bfloat16) for master in masters))
    return (
        lax.all_gather(lowered[0], ("shard", "context"), axis=0, tiled=True),
        lax.all_gather(lowered[1], ("shard", "context"), axis=1, tiled=True),
        lax.all_gather(lowered[2], ("shard", "context"), axis=1, tiled=True),
        lax.all_gather(lowered[3], ("shard", "context"), axis=1, tiled=True),
    )


def adamw(weight, gradient, momentum, variance, step_rate, decay_rate):
    momentum_new = BETA_ONE * momentum + (1.0 - BETA_ONE) * gradient
    variance_new = BETA_TWO * variance + (1.0 - BETA_TWO) * gradient * gradient
    momentum_hat = momentum_new / (1.0 - BETA_ONE**STEP)
    variance_hat = variance_new / (1.0 - BETA_TWO**STEP)
    updated = weight - step_rate * (
        momentum_hat / (jnp.sqrt(variance_hat) + ADAM_EPS) + decay_rate * weight
    )
    return (momentum_new, variance_new, updated)


def shards(
    hidden_in,
    cotangent,
    prefix,
    positions,
    norm_gains,
    gains_first,
    gains_second,
    input_weight,
    input_first,
    input_second,
    output_weight,
    output_first,
    output_second,
    expand_weight,
    expand_first,
    expand_second,
    shrink_weight,
    shrink_first,
    shrink_second,
):
    masters = (input_weight, output_weight, expand_weight, shrink_weight)
    input_weight_reduced, output_weight_reduced, expand_weight_reduced, shrink_weight_reduced = (
        fetch_weights(masters)
    )
    seq_dev = hidden_in.shape[0]
    block_rows = positions.shape[1]
    row_start = lax.axis_index("context") * block_rows
    cos_part, sin_part = angles(positions)
    x_rows = hidden_in.astype(jnp.float32)
    normed_one, scale_one = rms_parts(x_rows)
    first_input = lax.all_gather(
        (normed_one * norm_gains[0]).astype(jnp.bfloat16), "tensor", axis=1, tiled=True
    )
    packed_projection = jnp.einsum(
        "ibr,re->ibe", first_input, input_weight_reduced, preferred_element_type=jnp.float32
    )
    heads_local = packed_projection.shape[-1] // ((GROUP + 2) * HD)
    packed_parts = packed_projection.reshape(seq_dev, block_rows, heads_local, GROUP + 2, HD)
    queries = rotate(
        packed_parts[:, :, :, :GROUP], cos_part[:, :, None, None], sin_part[:, :, None, None]
    ).astype(jnp.bfloat16)
    key_local = rotate(
        packed_parts[:, :, :, GROUP], cos_part[:, :, None], sin_part[:, :, None]
    ).astype(jnp.bfloat16)
    value_local = packed_parts[:, :, :, GROUP + 1].astype(jnp.bfloat16)
    flat_width = heads_local * HD
    keys_all, values_all = (
        lax.all_gather(
            key_local.reshape(seq_dev, block_rows, flat_width), "context", axis=1, tiled=True
        ),
        lax.all_gather(
            value_local.reshape(seq_dev, block_rows, flat_width), "context", axis=1, tiled=True
        ),
    )
    total_len = keys_all.shape[1]
    keys_all = keys_all.reshape(seq_dev, total_len, heads_local, HD)
    values_all = values_all.reshape(seq_dev, total_len, heads_local, HD)

    def forward_sequence(slices):
        query_seq, key_seq, value_seq, prefix_len = slices
        return attend(query_seq, key_seq, value_seq, prefix_len, row_start)

    attended, log_total = lax.map(forward_sequence, (queries, keys_all, values_all, prefix))
    attended_reduced = attended.astype(jnp.bfloat16).reshape(
        seq_dev, block_rows, heads_local * GROUP * HD
    )
    projected = lax.psum_scatter(
        jnp.einsum(
            "fvz,zx->fvx",
            attended_reduced,
            output_weight_reduced,
            preferred_element_type=jnp.float32,
        ).astype(jnp.bfloat16),
        "tensor",
        scatter_dimension=1,
        tiled=True,
    ).astype(jnp.float32)
    residual = x_rows + RESID * projected
    normed_two, scale_two = rms_parts(residual)
    second_input = lax.all_gather(
        (normed_two * norm_gains[1]).astype(jnp.bfloat16), "tensor", axis=1, tiled=True
    )
    gate_value = jnp.einsum(
        "vma,ak->vmk", second_input, expand_weight_reduced[0], preferred_element_type=jnp.float32
    )
    up_value = jnp.einsum(
        "vma,ak->vmk", second_input, expand_weight_reduced[1], preferred_element_type=jnp.float32
    )
    gate_active = jax.nn.silu(gate_value)
    gated_hidden = (gate_active * up_value).astype(jnp.bfloat16)
    shrunk = lax.psum_scatter(
        jnp.einsum(
            "rpn,ng->rpg", gated_hidden, shrink_weight_reduced, preferred_element_type=jnp.float32
        ).astype(jnp.bfloat16),
        "tensor",
        scatter_dimension=1,
        tiled=True,
    ).astype(jnp.float32)
    block_output = (residual + RESID * shrunk).astype(jnp.bfloat16)
    grad_out = cotangent.astype(jnp.float32)
    masters_late, grad_out = lax.optimization_barrier((masters, grad_out))
    input_weight_reduced, output_weight_reduced, expand_weight_reduced, shrink_weight_reduced = (
        fetch_weights(masters_late)
    )
    shrunk_gradient = lax.all_gather(
        (RESID * grad_out).astype(jnp.bfloat16), "tensor", axis=1, tiled=True
    )
    grad_shrink = jnp.einsum(
        "yje,yjm->em", gated_hidden, shrunk_gradient, preferred_element_type=jnp.float32
    )
    grad_activated = jnp.einsum(
        "hkr,er->hke", shrunk_gradient, shrink_weight_reduced, preferred_element_type=jnp.float32
    )
    sigmoid_gate = jax.nn.sigmoid(gate_value)
    gate_gradient = (
        grad_activated * up_value * sigmoid_gate * (1.0 + gate_value * (1.0 - sigmoid_gate))
    ).astype(jnp.bfloat16)
    up_gradient = (grad_activated * gate_active).astype(jnp.bfloat16)
    grad_expand = jnp.stack(
        [
            jnp.einsum(
                "zuc,zuj->cj", second_input, gate_gradient, preferred_element_type=jnp.float32
            ),
            jnp.einsum(
                "zuc,zuj->cj", second_input, up_gradient, preferred_element_type=jnp.float32
            ),
        ]
    )
    second_terms = jnp.einsum(
        "mvz,cz->mvc", gate_gradient, expand_weight_reduced[0], preferred_element_type=jnp.float32
    )
    second_terms = second_terms + jnp.einsum(
        "mvz,cz->mvc", up_gradient, expand_weight_reduced[1], preferred_element_type=jnp.float32
    )
    grad_second = lax.psum_scatter(
        second_terms.astype(jnp.bfloat16), "tensor", scatter_dimension=1, tiled=True
    ).astype(jnp.float32)
    gain_two = jnp.sum(grad_second * normed_two, axis=(0, 1))
    grad_residual = grad_out + rms_back(grad_second * norm_gains[1], normed_two, scale_two)
    projected_gradient = lax.all_gather(
        (RESID * grad_residual).astype(jnp.bfloat16), "tensor", axis=1, tiled=True
    )
    grad_output = jnp.einsum(
        "jrq,jru->qu", attended_reduced, projected_gradient, preferred_element_type=jnp.float32
    )
    grad_attended = jnp.einsum(
        "mpu,au->mpa", projected_gradient, output_weight_reduced, preferred_element_type=jnp.float32
    ).astype(jnp.bfloat16)
    grad_attended = grad_attended.reshape(seq_dev, block_rows, heads_local, GROUP, HD)

    def backward_sequence(slices):
        query_seq, key_seq, value_seq, prefix_len, log_seq, attended_seq, grad_seq = slices
        return attend_back(
            query_seq, key_seq, value_seq, prefix_len, row_start, log_seq, attended_seq, grad_seq
        )

    grad_queries, grad_keys, grad_values = lax.map(
        backward_sequence,
        (queries, keys_all, values_all, prefix, log_total, attended, grad_attended),
    )
    grad_keys, grad_values = (
        lax.psum_scatter(
            grad_keys.reshape(seq_dev, total_len, flat_width).astype(jnp.bfloat16),
            "context",
            scatter_dimension=1,
            tiled=True,
        ).astype(jnp.float32),
        lax.psum_scatter(
            grad_values.reshape(seq_dev, total_len, flat_width).astype(jnp.bfloat16),
            "context",
            scatter_dimension=1,
            tiled=True,
        ).astype(jnp.float32),
    )
    grad_keys = unrotate(
        grad_keys.reshape(seq_dev, block_rows, heads_local, HD),
        cos_part[:, :, None],
        sin_part[:, :, None],
    )
    grad_values = grad_values.reshape(seq_dev, block_rows, heads_local, HD)
    grad_queries = unrotate(grad_queries, cos_part[:, :, None, None], sin_part[:, :, None, None])
    packed_gradient = jnp.concatenate(
        [grad_queries, grad_keys[:, :, :, None], grad_values[:, :, :, None]], axis=3
    )
    packed_gradient = packed_gradient.reshape(
        seq_dev, block_rows, heads_local * (GROUP + 2) * HD
    ).astype(jnp.bfloat16)
    grad_input = jnp.einsum(
        "ukz,uka->za", first_input, packed_gradient, preferred_element_type=jnp.float32
    )
    grad_first = lax.psum_scatter(
        jnp.einsum(
            "zwm,rm->zwr", packed_gradient, input_weight_reduced, preferred_element_type=jnp.float32
        ).astype(jnp.bfloat16),
        "tensor",
        scatter_dimension=1,
        tiled=True,
    ).astype(jnp.float32)
    gain_one = jnp.sum(grad_first * normed_one, axis=(0, 1))
    input_gradient = grad_residual + rms_back(grad_first * norm_gains[0], normed_one, scale_one)
    reduced = (
        lax.psum_scatter(
            grad_input.astype(jnp.bfloat16), ("shard", "context"), scatter_dimension=0, tiled=True
        ).astype(jnp.float32),
        lax.psum_scatter(
            grad_output.astype(jnp.bfloat16), ("shard", "context"), scatter_dimension=1, tiled=True
        ).astype(jnp.float32),
        lax.psum_scatter(
            grad_expand.astype(jnp.bfloat16), ("shard", "context"), scatter_dimension=1, tiled=True
        ).astype(jnp.float32),
        lax.psum_scatter(
            grad_shrink.astype(jnp.bfloat16), ("shard", "context"), scatter_dimension=1, tiled=True
        ).astype(jnp.float32),
    )
    grad_gains = lax.psum(jnp.stack([gain_one, gain_two]), ("shard", "context", "tensor"))
    local_squares = jnp.sum(reduced[0] * reduced[0])
    for shard_grad in reduced[1:]:
        local_squares = local_squares + jnp.sum(shard_grad * shard_grad)
    squares = lax.psum(local_squares, ("shard", "context", "tensor")) + jnp.sum(
        grad_gains * grad_gains
    )
    gradient_norm = jnp.sqrt(squares)
    factor = jnp.minimum(1.0, MAX_NORM / (gradient_norm + 1e-06))
    gains_new = adamw(norm_gains, factor * grad_gains, gains_first, gains_second, GAIN_RATE, 0.0)
    input_new = adamw(input_weight, factor * reduced[0], input_first, input_second, RATE, DECAY)
    output_new = adamw(output_weight, factor * reduced[1], output_first, output_second, RATE, DECAY)
    expand_new = adamw(expand_weight, factor * reduced[2], expand_first, expand_second, RATE, DECAY)
    shrink_new = adamw(shrink_weight, factor * reduced[3], shrink_first, shrink_second, RATE, DECAY)
    return (
        block_output,
        input_gradient,
        gradient_norm,
        gains_new[0],
        gains_new[1],
        gains_new[2],
        input_new[0],
        input_new[1],
        input_new[2],
        output_new[0],
        output_new[1],
        output_new[2],
        expand_new[0],
        expand_new[1],
        expand_new[2],
        shrink_new[0],
        shrink_new[1],
        shrink_new[2],
    )


def solution(mesh):
    return jax.shard_map(
        shards,
        mesh=mesh,
        in_specs=(
            P("shard", ("context", "tensor"), None),
            P("shard", ("context", "tensor"), None),
            P("shard"),
            P("shard", "context"),
            P(),
            P(),
            P(),
            P(("shard", "context"), "tensor"),
            P(("shard", "context"), "tensor"),
            P(("shard", "context"), "tensor"),
            P("tensor", ("shard", "context")),
            P("tensor", ("shard", "context")),
            P("tensor", ("shard", "context")),
            P(None, ("shard", "context"), "tensor"),
            P(None, ("shard", "context"), "tensor"),
            P(None, ("shard", "context"), "tensor"),
            P("tensor", ("shard", "context")),
            P("tensor", ("shard", "context")),
            P("tensor", ("shard", "context")),
        ),
        out_specs=(
            P("shard", ("context", "tensor"), None),
            P("shard", ("context", "tensor"), None),
            P(),
            P(),
            P(),
            P(),
            P(("shard", "context"), "tensor"),
            P(("shard", "context"), "tensor"),
            P(("shard", "context"), "tensor"),
            P("tensor", ("shard", "context")),
            P("tensor", ("shard", "context")),
            P("tensor", ("shard", "context")),
            P(None, ("shard", "context"), "tensor"),
            P(None, ("shard", "context"), "tensor"),
            P(None, ("shard", "context"), "tensor"),
            P("tensor", ("shard", "context")),
            P("tensor", ("shard", "context")),
            P("tensor", ("shard", "context")),
        ),
        check_vma=False,
    )
```

profile of v0, /device:TPU:0, one launch (start us, length us, event | category | flops | bytes accessed | tf_op | source)
XLA Modules:
  0.0 1725.7 jit_solution(12227890295845817597)
XLA Ops:
  16.9 77.6 %all-gather.15.cloned.1.call-done = bf16[1536,640]{1,0:T(8,128)(2,1)} async-done(((bf16[48,640]{1,0:T(8,128)(2,1)}), bf16[1536,640]{1,0:T(8,128)(2,1)}) %all-gather.15.cloned.1.call-update) | async-done | bytes 1966096 | tf_op jit(solution)/shard_map/all_gather | solution.py:125
  98.5 36.4 %all-gather.13.cloned.1.call-done = bf16[1,896,1536]{2,1,0:T(8,128)(2,1)} async-done(((bf16[1,224,1536]{2,1,0:T(8,128)(2,1)}), bf16[1,896,1536]{2,1,0:T(8,128)(2,1)}) %all-gather.13.cloned.1.call-update) | async-done | bytes 2752528 | tf_op jit(solution)/shard_map/all_gather | solution.py:174
  187.7 17.9 %fusion.101 = (bf16[896,2,3,64]{0,3,2,1:T(8,128)(2,1)S(1)}, f32[896,2,3,64]{0,3,2,1:T(8,128)}) fusion(bf16[1792,2,64,1]{0,2,3,1:T(8,128)(2,1)S(1)} %bitcast.205, f32[2,1792,896,3]{2,1,3,0:T(8,128)} %get-tuple-element.164, f32[2,3,896]{2,1,0:T(4,128)S(1)} %fusion.2, f32[2,3,896]{2,1,0:T(4,128)S(1)} %get-tuple-element.163, pred[896,1792]{0,1:T(8,128)(4,1)S(1)} %fusion.9), kind=kOutput, calls=%fused_computation.174 | convolution fusion | flops 1281638400 | bytes 42706944 | tf_op jit(solution)/shard_map/while/body/eval_jaxpr/gjqk,kgd->qgjd/dot_general | solution.py:89
  224.3 36.0 %reduce-scatter.14.cloned.1.call-done = bf16[1,224,1536]{2,1,0:T(8,128)(2,1)} async-done(((bf16[1,896,1536]{2,1,0:T(8,128)(2,1)}), bf16[1,224,1536]{2,1,0:T(8,128)(2,1)}) %reduce-scatter.14.cloned.1.call-update) | async-done | bytes 688144 | tf_op jit(solution)/shard_map/reduce_scatter | solution.py:210
  267.3 84.1 %all-gather.21.cloned.1.call-done = bf16[2,1536,960]{2,1,0:T(8,128)(2,1)} async-done(((bf16[2,48,960]{2,1,0:T(8,128)(2,1)}), bf16[2,1536,960]{2,1,0:T(8,128)(2,1)}) %all-gather.21.cloned.1.call-update) | async-done | bytes 5898256 | tf_op jit(solution)/shard_map/all_gather | solution.py:127
  351.4 40.4 %all-gather.19.cloned.1.call-done = bf16[1,896,1536]{2,1,0:T(8,128)(2,1)} async-done(((bf16[1,224,1536]{2,1,0:T(8,128)(2,1)}), bf16[1,896,1536]{2,1,0:T(8,128)(2,1)}) %all-gather.19.cloned.1.call-update) | async-done | bytes 2752528 | tf_op jit(solution)/shard_map/all_gather | solution.py:223
  404.9 25.1 %all-gather.25.cloned.1.call-done = bf16[1,896,1536]{2,1,0:T(8,128)(2,1)} async-done(((bf16[1,224,1536]{2,1,0:T(8,128)(2,1)}), bf16[1,896,1536]{2,1,0:T(8,128)(2,1)}) %all-gather.25.cloned.1.call-update) | async-done | bytes 2752528 | tf_op jit(solution)/shard_map/all_gather | solution.py:248
  430.0 87.3 %all-gather.27.cloned.1.call-done = bf16[960,1536]{0,1:T(8,128)(2,1)} async-done(((bf16[960,48]{0,1:T(8,128)(2,1)}), bf16[960,1536]{0,1:T(8,128)(2,1)}) %all-gather.27.cloned.1.call-update) | async-done | bytes 2949136 | tf_op jit(solution)/shard_map/all_gather | solution.py:128
  529.0 80.9 %all-gather.29.cloned.1.call-done = bf16[2,1536,960]{2,1,0:T(8,128)(2,1)} async-done(((bf16[2,48,960]{2,1,0:T(8,128)(2,1)}), bf16[2,1536,960]{2,1,0:T(8,128)(2,1)}) %all-gather.29.cloned.1.call-update) | async-done | bytes 5898256 | tf_op jit(solution)/shard_map/all_gather | solution.py:127
  621.1 36.4 %reduce-scatter.18.cloned.1.call-done = bf16[1,224,1536]{2,1,0:T(8,128)(2,1)} async-done(((bf16[1,896,1536]{2,1,0:T(8,128)(2,1)}), bf16[1,224,1536]{2,1,0:T(8,128)(2,1)}) %reduce-scatter.18.cloned.1.call-update) | async-done | bytes 688144 | tf_op jit(solution)/shard_map/reduce_scatter | solution.py:278
  662.1 78.9 %all-gather.33.cloned.1.call-done = bf16[384,1536]{0,1:T(8,128)(2,1)} async-done(((bf16[384,48]{0,1:T(8,128)(2,1)}), bf16[384,1536]{0,1:T(8,128)(2,1)}) %all-gather.33.cloned.1.call-update) | async-done | bytes 1179664 | tf_op jit(solution)/shard_map/all_gather | solution.py:126
  741.0 40.0 %all-gather.31.cloned.1.call-done = bf16[1,896,1536]{2,1,0:T(8,128)(2,1)} async-done(((bf16[1,224,1536]{2,1,0:T(8,128)(2,1)}), bf16[1,896,1536]{2,1,0:T(8,128)(2,1)}) %all-gather.31.cloned.1.call-update) | async-done | bytes 2752528 | tf_op jit(solution)/shard_map/all_gather | solution.py:283
  785.7 17.9 %fusion.37 = bf16[2,64,1792]{2,1,0:T(8,128)(2,1)} fusion(bf16[896,2,3,64]{0,3,2,1:T(8,128)(2,1)} %bitcast.203, f32[2,1792,896,3]{2,1,3,0:T(8,128)} %get-tuple-element.164, f32[2,3,896]{2,1,0:T(4,128)S(1)} %log_add_fusion, pred[896,1792]{0,1:T(8,128)(4,1)S(1)} %copy-done.3), kind=kOutput, calls=%fused_computation.59 | convolution fusion | flops 1271889920 | bytes 41309184 | tf_op jit(solution)/shard_map/while/body/eval_jaxpr/gjqk,qgjd->kgd/dot_general | solution.py:113
  803.6 25.5 %fusion.1 = bf16[2,3,896,1792]{2,3,1,0:T(8,128)(2,1)} fusion(f32[2,1792,896,3]{2,1,3,0:T(8,128)} %get-tuple-element.164, f32[2,3,896]{2,1,0:T(4,128)S(1)} %bitcast.208, f32[2,3,896]{2,1,0:T(4,128)S(1)} %log_add_fusion, pred[896,1792]{0,1:T(8,128)(4,1)} %copy-done.2, bf16[1792,2,64,1]{0,2,3,1:T(8,128)(2,1)} %bitcast.206, bf16[896,2,3,64]{0,3,2,1:T(8,128)(2,1)} %bitcast.204), kind=kOutput, calls=%fused_computation.2 | convolution fusion | flops 1290928128 | bytes 60598272 | tf_op jit(solution)/shard_map/while/body/eval_jaxpr/qgjd,kgd->gjqk/dot_general | solution.py:100
  867.0 16.4 copy.70
  922.6 32.6 %all-gather.35.cloned.1.call-done = bf16[1536,640]{1,0:T(8,128)(2,1)} async-done(((bf16[48,640]{1,0:T(8,128)(2,1)}), bf16[1536,640]{1,0:T(8,128)(2,1)}) %all-gather.35.cloned.1.call-update) | async-done | bytes 1966096 | tf_op jit(solution)/shard_map/all_gather | solution.py:125
  962.9 112.9 %all-reduce.4.cloned.1.call-done = bf16[2,1536,960]{2,0,1:T(2,128)(2,1)} async-done(((bf16[2,1536,960]{2,0,1:T(2,128)(2,1)}), bf16[2,1536,960]{2,0,1:T(2,128)(2,1)}) %all-reduce.4.cloned.1.call-update) | async-done | bytes 5898256
  1078.2 136.0 %reduce-scatter.26.cloned.1.call-done = bf16[960,48]{0,1:T(8,128)(2,1)} async-done(((bf16[960,1536]{0,1:T(8,128)(2,1)}), bf16[960,48]{0,1:T(8,128)(2,1)}) %reduce-scatter.26.cloned.1.call-update) | async-done | bytes 92176 | tf_op jit(solution)/shard_map/reduce_scatter | solution.py:354
  1215.8 132.0 %reduce-scatter.24.cloned.1.call-done = bf16[384,48]{0,1:T(8,128)(2,1)} async-done(((bf16[384,1536]{0,1:T(8,128)(2,1)}), bf16[384,48]{0,1:T(8,128)(2,1)}) %reduce-scatter.24.cloned.1.call-update) | async-done | bytes 36880 | tf_op jit(solution)/shard_map/reduce_scatter | solution.py:348
  1349.1 132.4 %reduce-scatter.22.cloned.1.call-done = bf16[48,640]{1,0:T(8,128)(2,1)} async-done(((bf16[1536,640]{1,0:T(8,128)(2,1)}), bf16[48,640]{1,0:T(8,128)(2,1)}) %reduce-scatter.22.cloned.1.call-update) | async-done | bytes 61456 | tf_op jit(solution)/shard_map/reduce_scatter | solution.py:345
  1485.6 30.4 %reduce-scatter.20.cloned.1.call-done = bf16[1,224,1536]{2,1,0:T(8,128)(2,1)} async-done(((bf16[1,896,1536]{2,1,0:T(8,128)(2,1)}), bf16[1,224,1536]{2,1,0:T(8,128)(2,1)}) %reduce-scatter.20.cloned.1.call-update) | async-done | bytes 688144 | tf_op jit(solution)/shard_map/reduce_scatter | solution.py:334
  1518.3 64.9 %all-reduce.1 = (f32[]{:T(128)}, f32[2,1536]{1,0:T(2,128)S(1)}) all-reduce(f32[]{:T(128)S(6)} %add.211, f32[2,1536]{1,0:T(2,128)S(1)} %pad_maximum_fusion.5), channel_id=1, replica_groups=mesh['shard'=16,'context'=2,'tensor'=4] {'shard','context','tensor'}, use_global_device_ids=true, to_apply=%region_21.22 | all-reduce | flops 3073 | bytes 24584 | tf_op jit(solution)/shard_map/psum | solution.py:362
  1587.7 82.7 %all-gather.23.cloned.1.call-done = bf16[960,1536]{0,1:T(8,128)(2,1)} async-done(((bf16[960,48]{0,1:T(8,128)(2,1)}), bf16[960,1536]{0,1:T(8,128)(2,1)}) %all-gather.23.cloned.1.call-update) | async-done | bytes 2949136 | tf_op jit(solution)/shard_map/all_gather | solution.py:128
  1685.5 28.3 %reduce-scatter.16.cloned.1.call-done = bf16[1,224,1536]{2,1,0:T(8,128)(2,1)} async-done(((bf16[1,896,1536]{2,1,0:T(8,128)(2,1)}), bf16[1,224,1536]{2,1,0:T(8,128)(2,1)}) %reduce-scatter.16.cloned.1.call-update) | async-done | bytes 688144 | tf_op jit(solution)/shard_map/reduce_scatter | solution.py:234
  (231 shorter events, 251.0 us)
Async XLA Ops:
  7.2 87.3 %all-gather.15.cloned.1.call-start = ((), (), s32[]{:S(2)}) async-start(), calls=%async_computation.10 | async-start | bytes 2027520 | tf_op jit(solution)/shard_map/all_gather | solution.py:125
  8.8 126.1 %all-gather.13.cloned.1.call-start = ((), (), s32[]{:S(2)}) async-start(), calls=%async_computation.9 | async-start | bytes 3440640 | tf_op jit(solution)/shard_map/all_gather | solution.py:174
  9.7 650.3 %copy-start.24 = (f32[1536]{0:T(1024)}, f32[1536]{0:T(1024)S(1)}, u32[]{:S(2)}) copy-start(f32[1536]{0:T(1024)S(1)} %get-tuple-element.129) | copy-start | bytes 18436
  13.2 204.9 %all-gather.17.cloned.1.call-start = ((), (), s32[]{:S(2)}) async-start(), calls=%async_computation.11 | async-start | bytes 1216512 | tf_op jit(solution)/shard_map/all_gather | solution.py:126
  14.0 246.3 %reduce-scatter.14.cloned.1.call-start = ((), (), s32[]{:S(2)}) async-start(), calls=%async_computation.12 | async-start | bytes 3440640 | tf_op jit(solution)/shard_map/reduce_scatter | solution.py:210
  222.6 128.8 %all-gather.21.cloned.1.call-start = ((), (), s32[]{:S(2)}) async-start(), calls=%async_computation.14 | async-start | bytes 6488064 | tf_op jit(solution)/shard_map/all_gather | solution.py:127
  224.3 167.5 %all-gather.19.cloned.1.call-start = ((), (), s32[]{:S(2)}) async-start(), calls=%async_computation.13 | async-start | bytes 3440640 | tf_op jit(solution)/shard_map/all_gather | solution.py:223
  264.1 165.9 %all-gather.25.cloned.1.call-start = ((), (), s32[]{:S(2)}) async-start(), calls=%async_computation.17 | async-start | bytes 3440640 | tf_op jit(solution)/shard_map/all_gather | solution.py:248
  265.3 252.0 %all-gather.27.cloned.1.call-start = ((), (), s32[]{:S(2)}) async-start(), calls=%async_computation.18 | async-start | bytes 3244032 | tf_op jit(solution)/shard_map/all_gather | solution.py:128
  266.0 343.9 %all-gather.29.cloned.1.call-start = ((), (), s32[]{:S(2)}) async-start(), calls=%async_computation.19 | async-start | bytes 6488064 | tf_op jit(solution)/shard_map/all_gather | solution.py:127
  266.8 390.7 %reduce-scatter.18.cloned.1.call-start = ((), (), s32[]{:S(2)}) async-start(), calls=%async_computation.20 | async-start | bytes 3440640 | tf_op jit(solution)/shard_map/reduce_scatter | solution.py:278
  620.3 120.7 %all-gather.33.cloned.1.call-start = ((), (), s32[]{:S(2)}) async-start(), calls=%async_computation.22 | async-start | bytes 1216512 | tf_op jit(solution)/shard_map/all_gather | solution.py:126
  621.0 159.9 %all-gather.31.cloned.1.call-start = ((), (), s32[]{:S(2)}) async-start(), calls=%async_computation.21 | async-start | bytes 3440640 | tf_op jit(solution)/shard_map/all_gather | solution.py:283
  662.0 244.9 %reduce-scatter.30.cloned.1.call-start = ((), (), s32[]{:S(2)}) async-start(), calls=%async_computation.29 | async-start | bytes 688128
  834.2 76.5 %reduce-scatter.28.cloned.1.call-start = ((), (), s32[]{:S(2)}) async-start(), calls=%async_computation.28 | async-start | bytes 688128
  853.2 102.0 %all-gather.35.cloned.1.call-start = ((), (), s32[]{:S(2)}) async-start(), calls=%async_computation.23 | async-start | bytes 2027520 | tf_op jit(solution)/shard_map/all_gather | solution.py:125
  854.8 220.9 %all-reduce.4.cloned.1.call-start = ((), (), s32[]{:S(2)}) async-start(), calls=%async_computation.30 | async-start | bytes 12582912
  883.5 330.7 %reduce-scatter.26.cloned.1.call-start = ((), (), s32[]{:S(2)}) async-start(), calls=%async_computation.27 | async-start | bytes 3244032 | tf_op jit(solution)/shard_map/reduce_scatter | solution.py:354
  891.0 456.8 %reduce-scatter.24.cloned.1.call-start = ((), (), s32[]{:S(2)}) async-start(), calls=%async_computation.26 | async-start | bytes 1216512 | tf_op jit(solution)/shard_map/reduce_scatter | solution.py:348
  896.0 585.6 %reduce-scatter.22.cloned.1.call-start = ((), (), s32[]{:S(2)}) async-start(), calls=%async_computation.25 | async-start | bytes 2027520 | tf_op jit(solution)/shard_map/reduce_scatter | solution.py:345
  922.6 593.5 %reduce-scatter.20.cloned.1.call-start = ((), (), s32[]{:S(2)}) async-start(), calls=%async_computation.24 | async-start | bytes 3440640 | tf_op jit(solution)/shard_map/reduce_scatter | solution.py:334
  961.0 555.1 %copy-start.33 = (f32[224]{0:T(256)S(1)}, f32[224]{0:T(256)}, u32[]{:S(2)}) copy-start(f32[224]{0:T(256)} %copy-done.32) | copy-start | bytes 2692
  961.0 709.4 %all-gather.23.cloned.1.call-start = ((), (), s32[]{:S(2)}) async-start(), calls=%async_computation.15 | async-start | bytes 3244032 | tf_op jit(solution)/shard_map/all_gather | solution.py:128
  1587.5 126.3 %reduce-scatter.16.cloned.1.call-start = ((), (), s32[]{:S(2)}) async-start(), calls=%async_computation.16 | async-start | bytes 3440640 | tf_op jit(solution)/shard_map/reduce_scatter | solution.py:234
  (47 other events, 2016.4 us)
Sparse Core Ops, SparseCore 0:
  10.3 84.1 all-gather.14
  96.7 38.1 all-gather.12
  137.2 80.9 all-gather.16
  222.7 37.5 reduce-scatter.13
  262.4 88.9 all-gather.20
  353.5 38.2 all-gather.18
  393.5 36.4 all-gather.24
  432.2 85.0 all-gather.26
  519.5 90.3 all-gather.28
  620.4 37.0 reduce-scatter.17
  659.8 81.1 all-gather.32
  743.1 37.8 all-gather.30
  834.4 16.3 reduce-scatter.29
  853.3 17.0 reduce-scatter.27
  872.5 82.6 all-gather.34
  958.4 117.2 all-reduce.3
  1078.0 136.2 reduce-scatter.25
  1217.1 130.5 reduce-scatter.23
  1350.1 131.4 reduce-scatter.21
  1484.0 32.0 reduce-scatter.19
  1587.6 82.7 all-gather.22
  1677.6 36.1 reduce-scatter.15
where the time goes:
time: 1730 us
  waiting for transfers between devices  1320 us (76%)
  matrix products  186 us (11%)
  blocking collectives  80.7 us (5%)
  other arithmetic  66.6 us (4%)
  local copies, waits for them, and re-layouts  45.5 us (3%)
  between operations  21.6 us (1%)
    all_gather x2, waiting for transfers between devices, fetch_weights(): lax.all_gather(lowered[3], ('shard', 'context'), axis=1, tiled=True)  170 us
    all_gather x2, waiting for transfers between devices, fetch_weights(): lax.all_gather(lowered[2], ('shard', 'context'), axis=1, tiled=True)  165 us
    reduce_scatter x1, waiting for transfers between devices, shards(): lax.psum_scatter(grad_shrink.astype(jnp.bfloat16), ('shard', 'context'),...  136 us
    reduce_scatter x1, waiting for transfers between devices, shards(): lax.psum_scatter(grad_input.astype(jnp.bfloat16), ('shard', 'context'), s...  132 us
    reduce_scatter x1, waiting for transfers between devices, shards(): lax.psum_scatter(grad_output.astype(jnp.bfloat16), ('shard', 'context'),...  132 us
    unnamed x25, waiting for transfers between devices  113 us
    all_gather x2, waiting for transfers between devices, fetch_weights(): lax.all_gather(lowered[0], ('shard', 'context'), axis=0, tiled=True)  110 us
    all_gather x2, waiting for transfers between devices, fetch_weights(): lax.all_gather(lowered[1], ('shard', 'context'), axis=1, tiled=True)  91.4 us
  transfers between devices with their start and end apart: 22, of which 20 were waited for; matrix products, arithmetic and copies ran while one was open for 12% of the time, Pallas kernels for 0%

commit v1 on v0

v1 whole, which is shorter than its diff:
```python
import functools
import math

import jax
import jax.numpy as jnp
from jax import lax
from jax.experimental import pallas as pl
from jax.experimental.pallas import tpu as pltpu
from jax.sharding import PartitionSpec as P

HD = 64
GROUP = 3
STEP = 10
HEADS = 2
BLOCKS = 7
VMEM_MOST = 60 * 2**20
MESH = pl.DeviceIdType.MESH


EPS = 1e-05
RESID = 1.4 / math.sqrt(52.0)
ROPE_BASE = 10000.0
MAX_NORM = 1.0
RATE = 0.1
GAIN_RATE = 1.0
BETA_ONE = 0.9
BETA_TWO = 0.95
ADAM_EPS = 1e-08
DECAY = 0.1
NEG = -1e30


def angles(places):
    half_width = HD // 2
    frequency = ROPE_BASE ** (-2.0 * jnp.arange(half_width, dtype=jnp.float32) / HD)
    phase_turn = places.astype(jnp.float32)[None, :] * frequency[:, None]
    return (jnp.cos(phase_turn), jnp.sin(phase_turn))


def rms_parts(values):
    scaling = lax.rsqrt(jnp.mean(values * values, axis=-1, keepdims=True) + EPS)
    return (values * scaling, scaling)


def rms_back(gradient, normed, scaling):
    return scaling * (gradient - normed * jnp.mean(gradient * normed, axis=-1, keepdims=True))


def adamw(weight, gradient, momentum, variance, step_rate, decay_rate):
    momentum_new = BETA_ONE * momentum + (1.0 - BETA_ONE) * gradient
    variance_new = BETA_TWO * variance + (1.0 - BETA_TWO) * gradient * gradient
    momentum_hat = momentum_new / (1.0 - BETA_ONE**STEP)
    variance_hat = variance_new / (1.0 - BETA_TWO**STEP)
    updated = weight - step_rate * (
        momentum_hat / (jnp.sqrt(variance_hat) + ADAM_EPS) + decay_rate * weight
    )
    return (momentum_new, variance_new, updated)


def nn(a, b):
    return lax.dot_general(a, b, (((1,), (0,)), ((), ())), preferred_element_type=jnp.float32)


def nt(a, b):
    return lax.dot_general(a, b, (((1,), (1,)), ((), ())), preferred_element_type=jnp.float32)


def place():
    shard = lax.axis_index("shard")
    return (
        shard // 8,
        lax.rem(shard // 2, 4),
        lax.rem(shard, 2),
        lax.axis_index("context"),
        lax.axis_index("tensor"),
    )


def device(xh, y, core, xl, z):
    return {"shard": (xh * 4 + y) * 2 + core, "context": xl, "tensor": z}


def greet(peers):
    barrier = pltpu.get_barrier_semaphore()
    for peer in peers:
        pl.semaphore_signal(barrier, inc=1, device_id=peer, device_id_type=MESH)
    pl.semaphore_wait(barrier, len(peers))


def remote(src, dst, send_sem, recv_sem, peer):
    return pltpu.make_async_remote_copy(
        src_ref=src,
        dst_ref=dst,
        send_sem=send_sem,
        recv_sem=recv_sem,
        device_id=peer,
        device_id_type=MESH,
    )


def turn(block, cos_part, sin_part):
    lower_half, upper_half = block[: HD // 2], block[HD // 2 :]
    return jnp.concatenate(
        [
            lower_half * cos_part - upper_half * sin_part,
            upper_half * cos_part + lower_half * sin_part,
        ],
        axis=0,
    )


def turn_back(block, cos_part, sin_part):
    return turn(block, cos_part, -sin_part)


def lay_keys(held, kv_rows):
    for g in range(HEADS):
        both = jnp.concatenate(
            [held[0, g * 128 : (g + 1) * 128, :], held[1, g * 128 : (g + 1) * 128, :]], axis=1
        )
        kv_rows[g] = jnp.transpose(both.astype(jnp.float32)).astype(jnp.bfloat16)


def by_span(context, b, run):
    near = (context == 0) | (b <= 3)

    @pl.when(near)
    def _():
        run(1408)

    @pl.when(jnp.logical_not(near))
    def _():
        run(1792)


def attend_kernel(
    packed, cos_ref, sin_ref, limit, turned, kv_all, attended, log_total, kv_rows, send_sem, recv_sem
):
    xh, y, core, xl, z = place()
    peer = device(xh, y, core, 1 - xl, z)
    greet([peer])
    cos_part, sin_part = cos_ref[...], sin_ref[...]
    for g in range(HEADS):
        base = g * 5 * HD
        kv_all[xl, g * 128 : g * 128 + HD] = turn(
            packed[base + 3 * HD : base + 4 * HD], cos_part, sin_part
        ).astype(jnp.bfloat16)
        kv_all[xl, g * 128 + HD : (g + 1) * 128] = packed[base + 4 * HD : base + 5 * HD].astype(
            jnp.bfloat16
        )
    copy = remote(kv_all.at[xl], kv_all.at[xl], send_sem, recv_sem, peer)
    copy.start()
    for g in range(HEADS):
        base = g * 5 * HD
        for h in range(GROUP):
            turned[(g * GROUP + h) * HD : (g * GROUP + h + 1) * HD] = (
                turn(packed[base + h * HD : base + (h + 1) * HD], cos_part, sin_part)
                * HD ** (-0.5)
            ).astype(jnp.bfloat16)
    copy.wait()
    lay_keys(kv_all, kv_rows)

    def block(t, carry):
        b, g = t // HEADS, lax.rem(t, HEADS)
        columns = pl.ds(pl.multiple_of(b * 128, 128), 128)

        def run(span):
            head_rows = [
                pl.ds(pl.multiple_of((g * GROUP + h) * HD, HD), HD) for h in range(GROUP)
            ]
            queries = jnp.concatenate([turned[r, columns] for r in head_rows], axis=1)
            queries = jnp.concatenate([queries, jnp.zeros_like(queries)], axis=0)
            scores = nn(kv_rows[g, :span], queries)
            key_index = lax.broadcasted_iota(jnp.int32, (span, 384), 0)
            scores = jnp.where(key_index < limit[b], scores, NEG)
            row_max = jnp.max(scores, axis=0, keepdims=True)
            shifted = jnp.exp(scores - row_max)
            exp_total = jnp.sum(shifted, axis=0, keepdims=True)
            value_rows = pl.ds(pl.multiple_of(g * 128 + HD, HD), HD)
            values = jnp.concatenate([kv_all[0, value_rows], kv_all[1, value_rows]], axis=1)
            total = nn(values[:, :span], shifted.astype(jnp.bfloat16)) * (1.0 / exp_total)
            for h in range(GROUP):
                attended[head_rows[h], columns] = total[:, h * 128 : (h + 1) * 128].astype(
                    jnp.bfloat16
                )
            log_total[t] = row_max + jnp.log(exp_total)

        by_span(xl, b, run)
        return carry

    lax.fori_loop(0, HEADS * BLOCKS, block, 0)


def attend_forward(packed, cos_part, sin_part, limit):
    return pl.pallas_call(
        attend_kernel,
        out_shape=(
            jax.ShapeDtypeStruct((384, 896), jnp.bfloat16),
            jax.ShapeDtypeStruct((2, 256, 896), jnp.bfloat16),
            jax.ShapeDtypeStruct((384, 896), jnp.bfloat16),
            jax.ShapeDtypeStruct((HEADS * BLOCKS, 1, 384), jnp.float32),
        ),
        scratch_shapes=[
            pltpu.VMEM((HEADS, 1792, 128), jnp.bfloat16),
            pltpu.SemaphoreType.DMA,
            pltpu.SemaphoreType.DMA,
        ],
        compiler_params=pltpu.CompilerParams(
            collective_id=1, has_side_effects=True, vmem_limit_bytes=VMEM_MOST
        ),
    )(packed, cos_part, sin_part, limit)


def attend_back_kernel(
    turned,
    kv_all,
    attended,
    log_total,
    grad_attended,
    cos_ref,
    sin_ref,
    limit,
    grad_packed,
    kv_rows,
    sums,
    outgoing,
    incoming,
    send_sem,
    recv_sem,
):
    xh, y, core, xl, z = place()
    peer = device(xh, y, core, 1 - xl, z)
    greet([peer])
    cos_part, sin_part = cos_ref[...], sin_ref[...]
    lay_keys(kv_all, kv_rows)
    sums[...] = jnp.zeros_like(sums)

    def block(t, carry):
        b, g = t // HEADS, lax.rem(t, HEADS)
        columns = pl.ds(pl.multiple_of(b * 128, 128), 128)

        def run(span):
            head_rows = [
                pl.ds(pl.multiple_of((g * GROUP + h) * HD, HD), HD) for h in range(GROUP)
            ]
            queries = jnp.concatenate([turned[r, columns] for r in head_rows], axis=1)
            gradient = jnp.concatenate([grad_attended[r, columns] for r in head_rows], axis=1)
            held = jnp.concatenate([attended[r, columns] for r in head_rows], axis=1)
            inner = jnp.sum(
                gradient.astype(jnp.float32) * held.astype(jnp.float32), axis=0, keepdims=True
            )
            nothing = jnp.zeros_like(queries)
            both = jnp.concatenate(
                [
                    jnp.concatenate([queries, nothing], axis=1),
                    jnp.concatenate([nothing, gradient], axis=1),
                ],
                axis=0,
            )
            products = nn(kv_rows[g, :span], both)
            key_index = lax.broadcasted_iota(jnp.int32, (span, 384), 0)
            probs = jnp.exp(
                jnp.where(key_index < limit[b], products[:, :384], NEG) - log_total[t]
            )
            grad_scores = (probs * (products[:, 384:] - inner)).astype(jnp.bfloat16)
            sums[g, :span] += nt(
                jnp.concatenate([grad_scores, probs.astype(jnp.bfloat16)], axis=1), both
            )
            key_lines = pl.ds(pl.multiple_of(g * 128, HD), HD)
            keys = jnp.concatenate([kv_all[0, key_lines], kv_all[1, key_lines]], axis=1)
            total = nn(keys[:, :span], grad_scores) * HD ** (-0.5)
            cos_here, sin_here = cos_ref[:, columns], sin_ref[:, columns]
            for h in range(GROUP):
                lines = pl.ds(pl.multiple_of((g * 5 + h) * HD, HD), HD)
                grad_packed[lines, columns] = turn_back(
                    total[:, h * 128 : (h + 1) * 128], cos_here, sin_here
                ).astype(jnp.bfloat16)

        by_span(xl, b, run)
        return carry

    lax.fori_loop(0, HEADS * BLOCKS, block, 0)
    for g in range(HEADS):
        theirs = sums[g, pl.ds(pl.multiple_of((1 - xl) * 896, 128), 896)]
        outgoing[g * 128 : (g + 1) * 128] = jnp.transpose(theirs).astype(jnp.bfloat16)
    copy = remote(outgoing, incoming, send_sem, recv_sem, peer)
    copy.start()
    copy.wait()
    for g in range(HEADS):
        mine = jnp.transpose(sums[g, pl.ds(pl.multiple_of(xl * 896, 128), 896)])
        mine = mine + incoming[g * 128 : (g + 1) * 128].astype(jnp.float32)
        base = g * 5 * HD
        grad_packed[base + 3 * HD : base + 4 * HD] = turn_back(
            mine[:HD], cos_part, sin_part
        ).astype(jnp.bfloat16)
        grad_packed[base + 4 * HD : base + 5 * HD] = mine[HD:].astype(jnp.bfloat16)


def attend_backward(turned, kv_all, attended, log_total, grad_attended, cos_part, sin_part, limit):
    return pl.pallas_call(
        attend_back_kernel,
        out_shape=jax.ShapeDtypeStruct((640, 896), jnp.bfloat16),
        scratch_shapes=[
            pltpu.VMEM((HEADS, 1792, 128), jnp.bfloat16),
            pltpu.VMEM((HEADS, 1792, 128), jnp.float32),
            pltpu.VMEM((256, 896), jnp.bfloat16),
            pltpu.VMEM((256, 896), jnp.bfloat16),
            pltpu.SemaphoreType.DMA,
            pltpu.SemaphoreType.DMA,
        ],
        compiler_params=pltpu.CompilerParams(
            collective_id=2, has_side_effects=True, vmem_limit_bytes=VMEM_MOST
        ),
    )(turned, kv_all, attended, log_total, grad_attended, cos_part, sin_part, limit)


def ring_peers():
    xh, y, core, xl, z = place()
    return (
        z,
        lax.rem(z + 1, 4),
        lax.rem(z + 2, 4),
        lax.rem(z + 3, 4),
        device(xh, y, core, xl, lax.rem(z + 1, 4)),
        device(xh, y, core, xl, lax.rem(z + 3, 4)),
    )


def halves(ref, index):
    rows = ref.shape[1] // 2
    return ref.at[index, pl.ds(0, rows)], ref.at[index, pl.ds(rows, rows)]


def ring_gather_begin(own, held, send_sem, recv_sem):
    z, zp, z2, zm, up, down = ring_peers()
    rows = own.shape[0] // 2
    first, second = own.at[pl.ds(0, rows)], own.at[pl.ds(rows, rows)]
    first_to, second_to = halves(held, z)
    copies = [
        remote(first, first_to, send_sem.at[0], recv_sem.at[0], up),
        remote(second, second_to, send_sem.at[1], recv_sem.at[1], down),
        remote(second, second_to, send_sem.at[2], recv_sem.at[2], up),
        remote(first, first_to, send_sem.at[3], recv_sem.at[3], down),
    ]
    for copy in copies:
        copy.start()
    return copies


def ring_gather_forward(held, copies, send_sem, recv_sem):
    z, zp, z2, zm, up, down = ring_peers()
    copies[0].wait_recv()
    below = halves(held, zm)[0]
    on_up = remote(below, below, send_sem.at[4], recv_sem.at[4], up)
    on_up.start()
    copies[1].wait_recv()
    above = halves(held, zp)[1]
    on_down = remote(above, above, send_sem.at[5], recv_sem.at[5], down)
    on_down.start()
    return copies + [on_up, on_down]


def ring_gather_end(copies):
    for copy in copies:
        copy.wait_send()
    for copy in copies[2:]:
        copy.wait_recv()


def ring_gather_kernel(own, held, send_sem, recv_sem, own_sem):
    z, zp, z2, zm, up, down = ring_peers()
    greet([up, down])
    copies = ring_gather_begin(own, held, send_sem, recv_sem)
    keep = pltpu.make_async_copy(own, held.at[z], own_sem)
    keep.start()
    copies = ring_gather_forward(held, copies, send_sem, recv_sem)
    keep.wait()
    ring_gather_end(copies)


def ring_gather(rows, identity):
    count, width = rows.shape
    held = pl.pallas_call(
        ring_gather_kernel,
        out_shape=jax.ShapeDtypeStruct((4, count, width), rows.dtype),
        in_specs=[pl.BlockSpec(memory_space=pl.ANY)],
        out_specs=pl.BlockSpec(memory_space=pl.ANY),
        scratch_shapes=[
            pltpu.SemaphoreType.DMA((6,)),
            pltpu.SemaphoreType.DMA((6,)),
            pltpu.SemaphoreType.DMA,
        ],
        compiler_params=pltpu.CompilerParams(
            collective_id=identity, has_side_effects=True, vmem_limit_bytes=VMEM_MOST
        ),
    )(rows)
    return held.reshape(4 * count, width)


def in_rows(count, step, run):
    def body(i, carry):
        run(pl.ds(pl.multiple_of(i * step, step), step))
        return carry

    lax.fori_loop(0, count // step, body, 0)


def ring_scatter_begin(parts, came, send_sem, recv_sem):
    z, zp, z2, zm, up, down = ring_peers()
    copies = [
        remote(halves(parts, z2)[1], came.at[0], send_sem.at[0], recv_sem.at[0], up),
        remote(halves(parts, z2)[0], came.at[1], send_sem.at[1], recv_sem.at[1], down),
        remote(halves(parts, zp)[0], came.at[2], send_sem.at[2], recv_sem.at[2], up),
        remote(halves(parts, zm)[1], came.at[3], send_sem.at[3], recv_sem.at[3], down),
    ]
    for copy in copies:
        copy.start()
    return copies


def ring_scatter_forward(parts, came, sums, copies, send_sem, recv_sem):
    z, zp, z2, zm, up, down = ring_peers()
    count = came.shape[1]
    copies[0].wait_recv()

    def add_up(rows):
        sums[0, rows] = (
            came[0, rows].astype(jnp.float32)
            + parts[zp, pl.ds(pl.multiple_of(rows.start + count, 16), 16)].astype(jnp.float32)
        ).astype(jnp.bfloat16)

    in_rows(count, 16, add_up)
    on_up = remote(sums.at[0], came.at[4], send_sem.at[4], recv_sem.at[4], up)
    on_up.start()
    copies[1].wait_recv()

    def add_down(rows):
        sums[1, rows] = (
            came[1, rows].astype(jnp.float32) + parts[zm, rows].astype(jnp.float32)
        ).astype(jnp.bfloat16)

    in_rows(count, 16, add_down)
    on_down = remote(sums.at[1], came.at[5], send_sem.at[5], recv_sem.at[5], down)
    on_down.start()
    return copies + [on_up, on_down]


def ring_scatter_end(parts, came, total, copies):
    z, zp, z2, zm, up, down = ring_peers()
    count = came.shape[1]
    for copy in copies[2:]:
        copy.wait_recv()
    for copy in copies:
        copy.wait_send()

    def add(rows):
        later = pl.ds(pl.multiple_of(rows.start + count, 16), 16)
        total[rows] = (
            parts[z, rows].astype(jnp.float32)
            + came[2, rows].astype(jnp.float32)
            + came[5, rows].astype(jnp.float32)
        )
        total[later] = (
            parts[z, later].astype(jnp.float32)
            + came[3, rows].astype(jnp.float32)
            + came[4, rows].astype(jnp.float32)
        )

    in_rows(count, 16, add)


def ring_scatter_kernel(parts, total, came, sums, send_sem, recv_sem):
    z, zp, z2, zm, up, down = ring_peers()
    greet([up, down])
    copies = ring_scatter_begin(parts, came, send_sem, recv_sem)
    copies = ring_scatter_forward(parts, came, sums, copies, send_sem, recv_sem)
    ring_scatter_end(parts, came, total, copies)


def ring_scatter(parts, identity):
    rows, width = parts.shape
    count = rows // 4
    return pl.pallas_call(
        ring_scatter_kernel,
        out_shape=jax.ShapeDtypeStruct((count, width), jnp.float32),
        scratch_shapes=[
            pltpu.VMEM((6, count // 2, width), jnp.bfloat16),
            pltpu.VMEM((2, count // 2, width), jnp.bfloat16),
            pltpu.SemaphoreType.DMA((6,)),
            pltpu.SemaphoreType.DMA((6,)),
        ],
        compiler_params=pltpu.CompilerParams(
            collective_id=identity, has_side_effects=True, vmem_limit_bytes=VMEM_MOST
        ),
    )(parts.reshape(4, count, width))


def plane():
    xh, y, core, xl, z = place()
    ys = [lax.rem(y + d, 4) for d in (1, 3, 2)]
    step = xh * 2 + xl
    xs = [lax.rem(step + d, 4) for d in (1, 3, 2)]
    xs = [(x // 2, lax.rem(x, 2)) for x in xs]
    y_peers = [device(xh, other, core, xl, z) for other in ys]
    x_peers = [device(h, y, core, l, z) for h, l in xs]
    return ys, xs, y_peers, x_peers, device(xh, y, 1 - core, xl, z)


class PlaneGather:
    def __init__(self, own, held, y_first, send_sem, recv_sem):
        self.own, self.held, self.y_first = own, held, y_first
        self.send_sem, self.recv_sem, self.used = send_sem, recv_sem, 0
        self.copies, self.first, self.second, self.third = [], [], [], []

    def send(self, src, dst, peer):
        copy = remote(src, dst, self.send_sem.at[self.used], self.recv_sem.at[self.used], peer)
        self.used += 1
        copy.start()
        self.copies.append(copy)
        return copy

    def begin(self):
        xh, y, core, xl, z = place()
        ys, xs, y_peers, x_peers, other = plane()
        target = self.held.at[xh, y, core, xl]
        peers = y_peers if self.y_first else x_peers
        self.first = [self.send(self.own, target, peer) for peer in peers]

    def line(self, where):
        xh, y, core, xl, z = place()
        if self.y_first:
            return self.held.at[where[0], :, core, where[1]]
        return self.held.at[:, where, core, :]

    def spread(self):
        xh, y, core, xl, z = place()
        ys, xs, y_peers, x_peers, other = plane()
        for copy in self.first:
            copy.wait_recv()
        mine = self.line((xh, xl) if self.y_first else y)
        peers = x_peers if self.y_first else y_peers
        self.second = [self.send(mine, mine, peer) for peer in peers]
        self.third = [self.send(mine, mine, other)]

    def share(self):
        ys, xs, y_peers, x_peers, other = plane()
        wheres = xs if self.y_first else ys
        for copy, where in zip(self.second, (wheres[1], wheres[0], wheres[2])):
            copy.wait_recv()
            line = self.line(where)
            self.third.append(self.send(line, line, other))

    def end(self):
        for copy in self.third:
            copy.wait_recv()
        for copy in self.copies:
            copy.wait_send()


def start_kernel(
    first, shrunk, w_in, w_gate, w_up, w_out, w_shrink, *refs
):
    owns = (w_in, w_gate, w_up, w_out, w_shrink)
    (first_all, shrunk_all), helds = refs[:2], refs[2:7]
    ring_send, ring_recv, plane_send, plane_recv, own_sem = refs[7:]
    xh, y, core, xl, z = place()
    z, zp, z2, zm, up, down = ring_peers()
    ys, xs, y_peers, x_peers, other = plane()
    greet([up, down, other] + y_peers + x_peers)
    gathers = [
        PlaneGather(own, held, i in (1, 2), plane_send.at[i], plane_recv.at[i])
        for i, (own, held) in enumerate(zip(owns, helds))
    ]
    keeps = [
        pltpu.make_async_copy(own, held.at[xh, y, core, xl], own_sem.at[i])
        for i, (own, held) in enumerate(zip(owns, helds))
    ]
    keeps.append(pltpu.make_async_copy(first, first_all.at[z], own_sem.at[5]))
    keeps.append(pltpu.make_async_copy(shrunk, shrunk_all.at[z], own_sem.at[6]))
    for gather in gathers:
        gather.begin()
    copies = ring_gather_begin(first, first_all, ring_send.at[0], ring_recv.at[0])
    for keep in keeps:
        keep.start()
    for keep in keeps:
        keep.wait()
    for gather in gathers:
        gather.spread()
    copies = ring_gather_forward(first_all, copies, ring_send.at[0], ring_recv.at[0])
    later = ring_gather_begin(shrunk, shrunk_all, ring_send.at[1], ring_recv.at[1])
    for gather in gathers:
        gather.share()
    later = ring_gather_forward(shrunk_all, later, ring_send.at[1], ring_recv.at[1])
    for gather in gathers:
        gather.end()
    ring_gather_end(copies)
    ring_gather_end(later)


def start(first, shrunk, weights):
    any_place = pl.BlockSpec(memory_space=pl.ANY)
    rows, width = first.shape
    outs = pl.pallas_call(
        start_kernel,
        out_shape=(jax.ShapeDtypeStruct((4, rows, width), jnp.bfloat16),) * 2
        + tuple(jax.ShapeDtypeStruct((2, 4, 2, 2) + w.shape, jnp.bfloat16) for w in weights),
        in_specs=[any_place] * 7,
        out_specs=(any_place,) * 7,
        scratch_shapes=[
            pltpu.SemaphoreType.DMA((2, 6)),
            pltpu.SemaphoreType.DMA((2, 6)),
            pltpu.SemaphoreType.DMA((5, 10)),
            pltpu.SemaphoreType.DMA((5, 10)),
            pltpu.SemaphoreType.DMA((7,)),
        ],
        compiler_params=pltpu.CompilerParams(
            collective_id=0, has_side_effects=True, vmem_limit_bytes=VMEM_MOST
        ),
    )(first, shrunk, *weights)
    return (
        outs[0].reshape(4 * rows, width),
        outs[1].reshape(4 * rows, width),
    ) + tuple(held.reshape(1536, -1) for held in outs[2:])


class PlaneScatter:
    def __init__(self, parts, came, halved, across, lined, last, x_first, send_sem, recv_sem):
        self.parts, self.came, self.halved = parts, came, halved
        self.across, self.lined, self.last, self.x_first = across, lined, last, x_first
        self.send_sem, self.recv_sem, self.used, self.copies = send_sem, recv_sem, 0, []

    def send(self, src, dst, peer):
        copy = remote(src, dst, self.send_sem.at[self.used], self.recv_sem.at[self.used], peer)
        self.used += 1
        copy.start()
        self.copies.append(copy)
        return copy

    def begin(self):
        xh, y, core, xl, z = place()
        ys, xs, y_peers, x_peers, other = plane()
        self.wheres = (xs[::-1] + [(xh, xl)]) if self.x_first else (ys[::-1] + [y])
        self.first = []
        for where in self.wheres:
            if self.x_first:
                src = self.parts.at[where[0], :, 1 - core, where[1]]
                dst = self.came.at[where[0], :, where[1]]
            else:
                src, dst = self.parts.at[:, where, 1 - core, :], self.came.at[:, where, :]
            self.first.append(self.send(src, dst, other))

    def fold(self):
        xh, y, core, xl, z = place()
        ys, xs, y_peers, x_peers, other = plane()
        peers = x_peers[::-1] if self.x_first else y_peers[::-1]
        self.second = []
        for k, (where, copy) in enumerate(zip(self.wheres, self.first)):
            copy.wait_recv()

            def add(i, carry, where=where, k=k):
                def rows(r):
                    if self.x_first:
                        h, l, v = where[0], where[1], i
                    else:
                        h, l, v = i // 2, lax.rem(i, 2), where
                    total = self.parts[h, v, core, l, r].astype(jnp.float32) + self.came[
                        h, v, l, r
                    ].astype(jnp.float32)
                    self.halved[k, i, r] = total.astype(jnp.bfloat16)

                in_rows(48, 16, rows)
                return carry

            lax.fori_loop(0, 4, add, 0)
            if k < 3:
                self.second.append(self.send(self.halved.at[k], self.across.at[k], peers[k]))

    def line(self):
        xh, y, core, xl, z = place()
        ys, xs, y_peers, x_peers, other = plane()
        for copy in self.second:
            copy.wait_recv()

        def add(i, carry):
            def rows(r):
                total = self.halved[3, i, r].astype(jnp.float32)
                for k in range(3):
                    total = total + self.across[k, i, r].astype(jnp.float32)
                self.lined[i, r] = total.astype(jnp.bfloat16)

            in_rows(48, 16, rows)
            return carry

        lax.fori_loop(0, 4, add, 0)
        if self.x_first:
            self.mine, targets, peers = y, ys, y_peers
        else:
            self.mine, targets, peers = xh * 2 + xl, [h * 2 + l for h, l in xs], x_peers
        self.third = [
            self.send(self.lined.at[target], self.last.at[k], peer)
            for k, (target, peer) in enumerate(zip(targets, peers))
        ]

    def end(self, total_ref):
        for copy in self.third:
            copy.wait_recv()

        def rows(r):
            total = self.lined[self.mine, r].astype(jnp.float32)
            for k in range(3):
                total = total + self.last[k, r].astype(jnp.float32)
            total_ref[r] = total

        in_rows(48, 16, rows)
        for copy in self.copies:
            copy.wait_send()


def scatter_scratch(width):
    return [
        pltpu.VMEM((2, 4, 2, 48, width), jnp.bfloat16),
        pltpu.VMEM((4, 4, 48, width), jnp.bfloat16),
        pltpu.VMEM((3, 4, 48, width), jnp.bfloat16),
        pltpu.VMEM((4, 48, width), jnp.bfloat16),
        pltpu.VMEM((3, 48, width), jnp.bfloat16),
    ]


def plane_scatter_kernel(turns, *refs):
    n = len(turns)
    parts, totals, scratch = refs[:n], refs[n : 2 * n], refs[2 * n :]
    send_sem, recv_sem = scratch[-2:]
    ys, xs, y_peers, x_peers, other = plane()
    greet([other] + y_peers + x_peers)
    scatters = [
        PlaneScatter(
            parts[i], *scratch[5 * i : 5 * i + 5], turns[i], send_sem.at[i], recv_sem.at[i]
        )
        for i in range(n)
    ]
    for scatter in scatters:
        scatter.begin()
    for scatter in scatters:
        scatter.fold()
    for scatter in scatters:
        scatter.line()
    for scatter, total in zip(scatters, totals):
        scatter.end(total)


def plane_scatter(gradients, turns, identity):
    shaped = [g.reshape(2, 4, 2, 2, 48, g.shape[-1]) for g in gradients]
    scratch = []
    for g in gradients:
        scratch += scatter_scratch(g.shape[-1])
    n = len(gradients)
    return pl.pallas_call(
        functools.partial(plane_scatter_kernel, turns),
        out_shape=tuple(jax.ShapeDtypeStruct((48, g.shape[-1]), jnp.float32) for g in gradients),
        scratch_shapes=scratch
        + [pltpu.SemaphoreType.DMA((n, 10)), pltpu.SemaphoreType.DMA((n, 10))],
        compiler_params=pltpu.CompilerParams(
            collective_id=identity, has_side_effects=True, vmem_limit_bytes=VMEM_MOST
        ),
    )(*shaped)


def sum_kernel(own, total, held, send_sem, recv_sem):
    xh, y, core, xl, z = place()
    ys, xs, y_peers, x_peers, other = plane()
    z_peers = [device(xh, y, core, xl, lax.rem(z + d, 4)) for d in (1, 3, 2)]
    greet([other] + z_peers + x_peers + y_peers)
    total[...] = own[...]
    groups = ((z_peers, z, 4), (x_peers, xh * 2 + xl, 4), (y_peers, y, 4), ([other], core, 2))
    for axis, (group, here, count) in enumerate(groups):
        held[axis, here] = total[...]
        copies = [
            remote(
                held.at[axis, here],
                held.at[axis, here],
                send_sem.at[axis * 3 + k],
                recv_sem.at[axis * 3 + k],
                peer,
            )
            for k, peer in enumerate(group)
        ]
        for copy in copies:
            copy.start()
        for copy in copies:
            copy.wait()
        order = held[axis, 0]
        for k in range(1, count):
            order = order + held[axis, k]
        total[...] = order


def sum_everywhere(own, identity):
    return pl.pallas_call(
        sum_kernel,
        out_shape=jax.ShapeDtypeStruct(own.shape, jnp.float32),
        scratch_shapes=[
            pltpu.VMEM((4, 4) + own.shape, jnp.float32),
            pltpu.SemaphoreType.DMA((12,)),
            pltpu.SemaphoreType.DMA((12,)),
        ],
        compiler_params=pltpu.CompilerParams(
            collective_id=identity, has_side_effects=True, vmem_limit_bytes=VMEM_MOST
        ),
    )(own)


def product(a, b, a_dim, b_dim):
    return lax.dot_general(
        a, b, (((a_dim,), (b_dim,)), ((), ())), preferred_element_type=jnp.float32
    )


def shards(
    hidden_in,
    cotangent,
    prefix,
    positions,
    norm_gains,
    gains_first,
    gains_second,
    input_weight,
    input_first,
    input_second,
    output_weight,
    output_first,
    output_second,
    expand_weight,
    expand_first,
    expand_second,
    shrink_weight,
    shrink_first,
    shrink_second,
):
    low = jnp.bfloat16
    x_rows = hidden_in[0].astype(jnp.float32)
    grad_out = cotangent[0].astype(jnp.float32)
    normed_one, scale_one = rms_parts(x_rows)
    first_own = (normed_one * norm_gains[0]).astype(low)
    shrunk_own = (RESID * grad_out).astype(low)
    first_all, shrunk_gradient, w_in, w_gate, w_up, w_out, w_shrink = start(
        first_own,
        shrunk_own,
        (
            input_weight.astype(low),
            expand_weight[0].astype(low),
            expand_weight[1].astype(low),
            output_weight.T.astype(low),
            shrink_weight.T.astype(low),
        ),
    )
    cos_part, sin_part = angles(positions[0])
    row_index = lax.axis_index("context") * 896 + jnp.arange(896, dtype=jnp.int32)
    limit = jnp.maximum(row_index + 1, prefix[0]).reshape(BLOCKS, 1, 128)
    limit = jnp.concatenate([limit] * GROUP, axis=2)
    packed = product(w_in, first_all, 0, 1)
    turned, kv_all, attended, log_total = attend_forward(packed, cos_part, sin_part, limit)
    projected = ring_scatter(product(attended, w_out, 0, 1).astype(low), 3)
    residual = x_rows + RESID * projected
    normed_two, scale_two = rms_parts(residual)
    second_all = ring_gather((normed_two * norm_gains[1]).astype(low), 4)
    gate_value = product(second_all, w_gate, 1, 0)
    up_value = product(second_all, w_up, 1, 0)
    sigmoid_gate = jax.nn.sigmoid(gate_value)
    gate_active = gate_value * sigmoid_gate
    gated_hidden = (gate_active * up_value).astype(low)
    grad_activated = product(shrunk_gradient, w_shrink, 1, 0)
    gate_gradient = (
        grad_activated * up_value * sigmoid_gate * (1.0 + gate_value * (1.0 - sigmoid_gate))
    ).astype(low)
    up_gradient = (grad_activated * gate_active).astype(low)
    second_terms = product(gate_gradient, w_gate, 1, 1) + product(up_gradient, w_up, 1, 1)
    grad_second = ring_scatter(second_terms.astype(low), 5)
    gain_two = jnp.sum(grad_second * normed_two, axis=0)
    grad_residual = grad_out + rms_back(grad_second * norm_gains[1], normed_two, scale_two)
    projected_gradient = ring_gather((RESID * grad_residual).astype(low), 6)
    grad_attended = product(w_out, projected_gradient, 0, 1).astype(low)
    grad_packed = attend_backward(
        turned, kv_all, attended, log_total, grad_attended, cos_part, sin_part, limit
    )
    grad_first = ring_scatter(product(grad_packed, w_in, 0, 1).astype(low), 7)
    gain_one = jnp.sum(grad_first * normed_one, axis=0)
    input_gradient = grad_residual + rms_back(grad_first * norm_gains[0], normed_one, scale_one)
    shrunk = ring_scatter(product(gated_hidden, w_shrink, 1, 1).astype(low), 8)
    block_output = (residual + RESID * shrunk).astype(low)
    grad_gate, grad_up, grad_output, grad_shrink, grad_input = plane_scatter(
        (
            product(second_all, gate_gradient, 0, 0).astype(low),
            product(second_all, up_gradient, 0, 0).astype(low),
            product(projected_gradient, attended, 0, 1).astype(low),
            product(shrunk_gradient, gated_hidden, 0, 0).astype(low),
            product(first_all, grad_packed, 0, 1).astype(low),
        ),
        (True, True, False, False, False),
        9,
    )
    grad_expand = jnp.stack([grad_gate, grad_up])
    grad_output, grad_shrink = grad_output.T, grad_shrink.T
    reduced = (grad_input, grad_output, grad_expand, grad_shrink)
    local_squares = sum(jnp.sum(g * g) for g in reduced)
    gains_local = jnp.stack([gain_one, gain_two]).reshape(24, 128)
    message = jnp.concatenate([gains_local, jnp.full((8, 128), local_squares)], axis=0)
    message = sum_everywhere(message, 10)
    grad_gains = message[:24].reshape(2, 1536)
    squares = message[24, 0] + jnp.sum(grad_gains * grad_gains)
    gradient_norm = jnp.sqrt(squares)
    factor = jnp.minimum(1.0, MAX_NORM / (gradient_norm + 1e-06))
    gains_new = adamw(norm_gains, factor * grad_gains, gains_first, gains_second, GAIN_RATE, 0.0)
    input_new = adamw(input_weight, factor * reduced[0], input_first, input_second, RATE, DECAY)
    output_new = adamw(output_weight, factor * reduced[1], output_first, output_second, RATE, DECAY)
    expand_new = adamw(expand_weight, factor * reduced[2], expand_first, expand_second, RATE, DECAY)
    shrink_new = adamw(shrink_weight, factor * reduced[3], shrink_first, shrink_second, RATE, DECAY)
    return (
        block_output[None],
        input_gradient[None],
        gradient_norm,
        *gains_new,
        *input_new,
        *output_new,
        *expand_new,
        *shrink_new,
    )


def solution(mesh):
    return jax.shard_map(
        shards,
        mesh=mesh,
        in_specs=(
            P("shard", ("context", "tensor"), None),
            P("shard", ("context", "tensor"), None),
            P("shard"),
            P("shard", "context"),
            P(),
            P(),
            P(),
            P(("shard", "context"), "tensor"),
            P(("shard", "context"), "tensor"),
            P(("shard", "context"), "tensor"),
            P("tensor", ("shard", "context")),
            P("tensor", ("shard", "context")),
            P("tensor", ("shard", "context")),
            P(None, ("shard", "context"), "tensor"),
            P(None, ("shard", "context"), "tensor"),
            P(None, ("shard", "context"), "tensor"),
            P("tensor", ("shard", "context")),
            P("tensor", ("shard", "context")),
            P("tensor", ("shard", "context")),
        ),
        out_specs=(
            P("shard", ("context", "tensor"), None),
            P("shard", ("context", "tensor"), None),
            P(),
            P(),
            P(),
            P(),
            P(("shard", "context"), "tensor"),
            P(("shard", "context"), "tensor"),
            P(("shard", "context"), "tensor"),
            P("tensor", ("shard", "context")),
            P("tensor", ("shard", "context")),
            P("tensor", ("shard", "context")),
            P(None, ("shard", "context"), "tensor"),
            P(None, ("shard", "context"), "tensor"),
            P(None, ("shard", "context"), "tensor"),
            P("tensor", ("shard", "context")),
            P("tensor", ("shard", "context")),
            P("tensor", ("shard", "context")),
        ),
        check_vma=False,
    )
```

time: 1730 us -> 542 us (0.31)
  waiting for transfers between devices: 1320 us -> 0 us
  Pallas kernels: 0 us -> 395 us
  matrix products: 186 us -> 75.1 us
  blocking collectives: 80.7 us -> 0 us
  other arithmetic: 66.6 us -> 39 us
  local copies, waits for them, and re-layouts: 45.5 us -> 19.3 us
    all_gather x12 -> x0, waiting for transfers between devices: 679 us -> none  [the longest x2 170 us: fetch_weights(): lax.all_gather(lowered[3], ('shard', 'context'), axis=1, tiled=True)]
    reduce_scatter x7 -> x0, waiting for transfers between devices: 532 us -> none  [the longest x1 136 us: shards(): lax.psum_scatter(grad_shrink.astype(jnp.bfloat16), ('shard', 'context'),...]
    pallas_call x0 -> x11, Pallas kernels: none -> 395 us  [the longest x1 108 us: start(): pl.pallas_call(start_kernel, out_shape=(jax.ShapeDtypeStruct((4, rows, wi...]
    unnamed x25 -> x0, waiting for transfers between devices: 113 us -> none
    dot_general x21 -> x15, matrix products: 186 us -> 75.1 us  [product(): lax.dot_general(a, b, (((a_dim,), (b_dim,)), ((), ())), preferred_element...]
    psum x1 -> x0, blocking collectives: 64.9 us -> none  [shards(): lax.psum(local_squares, ('shard', 'context', 'tensor'))]
    unnamed x108 -> x74, local copies, waits for them, and re-layouts: 24.2 us -> 1.43 us
  transfers between devices with their start and end apart: 22 -> 0, of which waited for: 20 -> 0; matrix products, arithmetic and copies ran while one was open for 12% -> 0% of each run, Pallas kernels for 0% -> 0%
where the time goes in v1:
time: 542 us; the launch traced here: 536 us
  Pallas kernels  395 us (73%)
  matrix products  75.1 us (14%)
  other arithmetic  39 us (7%)
  local copies, waits for them, and re-layouts  19.3 us (4%)
  between operations  7.48 us (1%)
    pallas_call x1, Pallas kernels, start(): pl.pallas_call(start_kernel, out_shape=(jax.ShapeDtypeStruct((4, rows, wi...  108 us
    pallas_call x4, Pallas kernels, ring_scatter(): pl.pallas_call(ring_scatter_kernel, out_shape=jax.ShapeDtypeStruct((count...  98.4 us
    dot_general x15, matrix products, product(): lax.dot_general(a, b, (((a_dim,), (b_dim,)), ((), ())), preferred_element...  75.1 us
    pallas_call x1, Pallas kernels, plane_scatter(): pl.pallas_call(functools.partial(plane_scatter_kernel, turns), out_shape=...  56.9 us
    pallas_call x2, Pallas kernels, ring_gather(): pl.pallas_call(ring_gather_kernel, out_shape=jax.ShapeDtypeStruct((4, cou...  47.8 us
    pallas_call x1, Pallas kernels, attend_backward(): pl.pallas_call(attend_back_kernel, out_shape=jax.ShapeDtypeStruct((640, 8...  36.6 us
    pallas_call x1, Pallas kernels, attend_forward(): pl.pallas_call(attend_kernel, out_shape=(jax.ShapeDtypeStruct((384, 896),...  30.4 us
    pallas_call x1, Pallas kernels, sum_everywhere(): pl.pallas_call(sum_kernel, out_shape=jax.ShapeDtypeStruct(own.shape, jnp....  16.7 us

profile of v1, /device:TPU:0, one launch (start us, length us, event | category | flops | bytes accessed | tf_op | source)
XLA Modules:
  0.0 536.0 jit_solution(12849663271392967876)
XLA Ops:
  13.8 108.3 %shard_map.322 = (bf16[4,224,1536]{2,1,0:T(8,128)(2,1)}, bf16[4,224,1536]{2,1,0:T(8,128)(2,1)}, bf16[2,4,2,2,48,640]{5,4,3,2,1,0:T(8,128)(2,1)}, bf16[2,4,2,2,48...) custom-call(bf16[224,1536]{1,0:T(8,128)(2,1)} %get-tuple-element.83., ...), custom_call_target="tpu_custom_call" | custom-call | tf_op jit(solution)/shard_map/pallas_call | solution.py:603
  122.0 6.0 %fusion.29.packed = f32[640,896]{1,0:T(8,128)} fusion(bf16[1536,640]{1,0:T(8,128)(2,1)} %bitcast.125, bf16[896,1536]{1,0:T(8,128)(2,1)} %bitcast.121), kind=kOutput, calls=%fused_computation.86 | convolution fusion | flops 1761607680 | bytes 7012352 | tf_op jit(solution)/shard_map/dot_general | solution.py:813
  128.0 30.4 %shard_map.323 = (bf16[384,896]{1,0:T(8,128)(2,1)}, bf16[2,256,896]{2,1,0:T(8,128)(2,1)}, bf16[384,896]{1,0:T(8,128)(2,1)}, f32[14,1,384]{2,1,0:T(1,128)}) custom-call(f32[640,896]{1,0:T(8,128)} %fusion.29.packed, f32[32,896]{1,0:T(8,128)} %get-tuple-element.81.cos_ref, f32[32,896]{1,0:T(8,128)} %get-tuple-element.80.sin_ref, s32[7,1,384]{2,1,0:T(1,128)} %pad_add_fusion.limit), custom_call_target="tpu_custom_call" | custom-call | tf_op jit(solution)/shard_map/pallas_call | solution.py:195
  162.8 26.6 %shard_map.324 = f32[224,1536]{1,0:T(8,128)} custom-call(bf16[4,224,1536]{2,1,0:T(8,128)(2,1)} %bitcast.108), custom_call_target="tpu_custom_call" | custom-call | tf_op jit(solution)/shard_map/pallas_call | solution.py:483
  192.1 22.8 %shard_map.325 = bf16[4,224,1536]{2,1,0:T(8,128)(2,1)} custom-call(bf16[224,1536]{1,0:T(8,128)(2,1)} %multiply_convert_fusion.4.own), custom_call_target="tpu_custom_call" | custom-call | tf_op jit(solution)/shard_map/pallas_call | solution.py:383
  214.9 6.3 %fusion.31 = f32[896,960]{0,1:T(8,128)S(1)} fusion(bf16[896,1536]{1,0:T(8,128)(2,1)} %bitcast.99, bf16[1536,960]{1,0:T(8,128)(2,1)} %bitcast.115), kind=kOutput, calls=%fused_computation.88 | convolution fusion | flops 2642411520 | bytes 9142272 | tf_op jit(solution)/shard_map/dot_general | solution.py:813
  224.6 6.6 %multiply_convert_fusion = (bf16[896,960]{0,1:T(8,128)(2,1)}, bf16[896,960]{0,1:T(8,128)(2,1)}, bf16[896,960]{0,1:T(8,128)(2,1)S(1)}) fusion(f32[896,960]{0,1:T(8,128)S(1)} %fusion.30, f32[896,960]{0,1:T(8,128)S(1)} %fusion.31, bf16[896,1536]{1,0:T(8,128)(2,1)S(1)} %bitcast.124, bf16[1536,960]{1,0:T(8,128)(2,1)S(1)} %bitcast.119), kind=kOutput, calls=%fused_computation.7 | convolution fusion | flops 2655313920 | bytes 17743872 | tf_op jit(solution)/shard_map/dot_general | solution.py:813
  235.7 25.1 %shard_map.326 = f32[224,1536]{1,0:T(8,128)} custom-call(bf16[4,224,1536]{2,1,0:T(8,128)(2,1)} %bitcast.105), custom_call_target="tpu_custom_call" | custom-call | tf_op jit(solution)/shard_map/pallas_call | solution.py:483
  260.8 7.2 %convolution_convert_fusion = bf16[1536,960]{0,1:T(8,128)(2,1)} fusion(bf16[896,960]{0,1:T(8,128)(2,1)} %copy-done.36, bf16[896,1536]{1,0:T(8,128)(2,1)} %bitcast.123), kind=kOutput, calls=%fused_computation.1 | convolution fusion | flops 2643886080 | bytes 7421952 | tf_op jit(solution)/shard_map/dot_general | solution.py:813
  268.0 4.6 copy.39
  272.6 5.6 %fusion.32 = f32[896,1536]{1,0:T(8,128)S(1)} fusion(bf16[896,960]{0,1:T(8,128)(2,1)} %get-tuple-element.74, bf16[1536,960]{1,0:T(8,128)(2,1)} %bitcast.117), kind=kOutput, calls=%fused_computation.89 | convolution fusion | flops 2642411520 | bytes 10174464 | tf_op jit(solution)/shard_map/dot_general | solution.py:813
  278.3 4.5 add_convert_fusion
  282.8 24.3 %shard_map.327 = f32[224,1536]{1,0:T(8,128)} custom-call(bf16[4,224,1536]{2,1,0:T(8,128)(2,1)} %bitcast.106), custom_call_target="tpu_custom_call" | custom-call | tf_op jit(solution)/shard_map/pallas_call | solution.py:483
  312.3 4.8 convolution_convert_fusion.1
  317.1 4.6 convolution_convert_fusion.2
  321.7 4.7 copy.37
  326.4 4.6 copy.38
  331.0 25.0 %shard_map.328 = bf16[4,224,1536]{2,1,0:T(8,128)(2,1)} custom-call(bf16[224,1536]{1,0:T(8,128)(2,1)} %multiply_convert_fusion.3.own), custom_call_target="tpu_custom_call" | custom-call | tf_op jit(solution)/shard_map/pallas_call | solution.py:383
  356.0 4.6 convolution_convert_fusion.8.grad_attended
  363.4 36.6 %shard_map.329 = bf16[640,896]{1,0:T(8,128)(2,1)} custom-call(bf16[384,896]{1,0:T(8,128)(2,1)} %get-tuple-element.42.turned, bf16[2,256,896]{2,1,0:T(8,128)(2,1)} %get-tuple-element.43.kv_all, bf16[384,896]{1,0:T(8,128)(2,1)} %get-tuple-element.36.attended, f32[14,1,384]{2,1,0:T(1,128)} %get-tuple-element.44.log_total, ...), custom_call_target="tpu_custom_call" | custom-call | tf_op jit(solution)/shard_map/pallas_call | solution.py:300
  400.0 6.1 %convolution_convert_fusion.6 = bf16[1536,640]{1,0:T(8,128)(2,1)} fusion(bf16[896,1536]{1,0:T(8,128)(2,1)} %bitcast.122, bf16[640,896]{1,0:T(8,128)(2,1)} %shard_map.329), kind=kOutput, calls=%fused_computation.12 | convolution fusion | flops 1762590720 | bytes 5865472 | tf_op jit(solution)/shard_map/dot_general | solution.py:813
  410.0 22.4 %shard_map.330 = f32[224,1536]{1,0:T(8,128)} custom-call(bf16[4,224,1536]{2,1,0:T(8,128)(2,1)} %bitcast.107), custom_call_target="tpu_custom_call" | custom-call | tf_op jit(solution)/shard_map/pallas_call | solution.py:483
  432.4 56.9 %shard_map.331 = (f32[48,960]{1,0:T(8,128)}, f32[48,960]{1,0:T(8,128)}, f32[48,384]{1,0:T(8,128)}, f32[48,960]{1,0:T(8,128)}, f32[48,640]{1,0:T(8,128)}) custom-call(bf16[2,4,2,2,48,960]{5,4,3,2,1,0:T(8,128)(2,1)} %bitcast.97, bf16[2,4,2,2,48,960]{5,4,3,2,1,0:T(8,128)(2,1)} %bitcast.98, bf16[2,4,2,2,48,384]{5,4,3,2,1,0:T(8,128)(2,1)} %bitcast.110, ...), custom_call_target="tpu_custom_call" | custom-call | tf_op jit(solution)/shard_map/pallas_call | solution.py:757
  504.9 16.7 %shard_map.332 = f32[32,128]{1,0:T(8,128)} custom-call(f32[32,128]{1,0:T(8,128)} %concatenate.7.own), custom_call_target="tpu_custom_call" | custom-call | tf_op jit(solution)/shard_map/pallas_call | solution.py:798
  (120 shorter events, 63.2 us)
Async XLA Ops:
  0.7 11.8 %copy-start.1 = (bf16[1,224,1536]{2,1,0:T(8,128)(2,1)S(1)}, bf16[1,224,1536]{2,1,0:T(8,128)(2,1)}, u32[]{:S(2)}) copy-start(bf16[1,224,1536]{2,1,0:T(8,128)(2,1)} %param.19) | copy-start | bytes 2064388
  0.7 11.8 %copy-start.2 = (bf16[1,224,1536]{2,1,0:T(8,128)(2,1)S(1)}, bf16[1,224,1536]{2,1,0:T(8,128)(2,1)}, u32[]{:S(2)}) copy-start(bf16[1,224,1536]{2,1,0:T(8,128)(2,1)} %param.20) | copy-start | bytes 2064388
  2.8 11.0 %copy-start.24 = (f32[224]{0:T(256)}, f32[224]{0:T(256)S(1)}, u32[]{:S(2)}) copy-start(f32[224]{0:T(256)S(1)} %add_rsqrt_fusion.1) | copy-start | bytes 2692
  4.9 8.8 %copy-start.19 = (f32[1536]{0:T(1024)}, f32[1536]{0:T(1024)S(1)}, u32[]{:S(2)}) copy-start(f32[1536]{0:T(1024)S(1)} %get-tuple-element.55) | copy-start | bytes 18436
  4.9 304.7 %copy-start.17 = (f32[1536]{0:T(1024)}, f32[1536]{0:T(1024)S(1)}, u32[]{:S(2)}) copy-start(f32[1536]{0:T(1024)S(1)} %get-tuple-element.54) | copy-start | bytes 18436
  128.0 30.4 %copy-start.32 = (bf16[2,4,2,2,48,384]{5,4,3,2,1,0:T(8,128)(2,1)S(1)}, bf16[2,4,2,2,48,384]{5,4,3,2,1,0:T(8,128)(2,1)}, u32[]{:S(2)}) copy-start(bf16[2,4,2,2,48,384]{5,4,3,2,1,0:T(8,128)(2,1)} %get-tuple-element.37) | copy-start | bytes 3538948
  191.0 118.6 %copy-start.22 = (f32[224]{0:T(256)}, f32[224]{0:T(256)S(1)}, u32[]{:S(2)}) copy-start(f32[224]{0:T(256)S(1)} %add_rsqrt_fusion) | copy-start | bytes 2692
  214.9 6.3 %copy-start.4 = (bf16[4,224,1536]{2,1,0:T(8,128)(2,1)S(1)}, bf16[4,224,1536]{2,1,0:T(8,128)(2,1)}, u32[]{:S(2)}) copy-start(bf16[4,224,1536]{2,1,0:T(8,128)(2,1)} %shard_map.325) | copy-start | bytes 8257540
  214.9 6.3 %copy-start.28 = (bf16[2,4,2,2,48,960]{5,4,3,2,1,0:T(8,128)(2,1)S(1)}, bf16[2,4,2,2,48,960]{5,4,3,2,1,0:T(8,128)(2,1)}, u32[]{:S(2)}) copy-start(bf16[2,4,2,2,48,960]{5,4,3,2,1,0:T(8,128)(2,1)} %get-tuple-element.38) | copy-start | bytes 8847364
  400.0 6.1 %copy-start.8 = (bf16[640,896]{1,0:T(8,128)(2,1)S(1)}, bf16[640,896]{1,0:T(8,128)(2,1)}, u32[]{:S(2)}) copy-start(bf16[640,896]{1,0:T(8,128)(2,1)} %shard_map.329) | copy-start | bytes 3440644
  400.0 6.1 %copy-start.31 = (bf16[2,4,2,2,48,640]{5,4,3,2,1,0:T(8,128)(2,1)S(1)}, bf16[2,4,2,2,48,640]{5,4,3,2,1,0:T(8,128)(2,1)}, u32[]{:S(2)}) copy-start(bf16[2,4,2,2,48,640]{5,4,3,2,1,0:T(8,128)(2,1)} %get-tuple-element.34) | copy-start | bytes 5898244
  432.4 65.9 %copy-start.20 = (f32[1536]{0:T(1024)S(1)}, f32[1536]{0:T(1024)}, u32[]{:S(2)}) copy-start(f32[1536]{0:T(1024)} %copy-done.19) | copy-start | bytes 18436
  432.4 65.9 %copy-start.25 = (f32[224]{0:T(256)S(1)}, f32[224]{0:T(256)}, u32[]{:S(2)}) copy-start(f32[224]{0:T(256)} %copy-done.24) | copy-start | bytes 2692
  489.3 10.8 %copy-start.23 = (f32[1,1536]{1,0:T(1,128)S(1)}, f32[1,1536]{1,0:T(1,128)}, u32[]{:S(2)}) copy-start(f32[1,1536]{1,0:T(1,128)} %stack.19) | copy-start | bytes 18436
  489.3 10.9 %copy-start.18 = (f32[1536]{0:T(1024)S(1)}, f32[1536]{0:T(1024)}, u32[]{:S(2)}) copy-start(f32[1536]{0:T(1024)} %copy-done.17) | copy-start | bytes 18436
  500.2 26.1 %copy-start.21 = (f32[2,1536]{1,0:T(2,128)S(1)}, f32[2,1536]{1,0:T(2,128)}, u32[]{:S(2)}) copy-start(f32[2,1536]{1,0:T(2,128)} %param.23) | copy-start | bytes 36868
  500.2 27.5 %copy-start.16 = (f32[384,48]{0,1:T(8,128)S(1)}, f32[384,48]{0,1:T(8,128)}, u32[]{:S(2)}) copy-start(f32[384,48]{0,1:T(8,128)} %param.29) | copy-start | bytes 221188
  504.3 26.9 %copy-start.9 = (f32[960,48]{0,1:T(8,128)S(1)}, f32[960,48]{0,1:T(8,128)}, u32[]{:S(2)}) copy-start(f32[960,48]{0,1:T(8,128)} %param.35) | copy-start | bytes 552964
  504.3 26.9 %copy-start.12 = (f32[48,960]{1,0:T(8,128)S(1)}, f32[48,960]{1,0:T(8,128)}, u32[]{:S(2)}) copy-start(f32[48,960]{1,0:T(8,128)} %get-tuple-element.49) | copy-start | bytes 552964
  504.3 28.9 %copy-start.7 = (f32[2,48,960]{2,1,0:T(8,128)S(1)}, f32[2,48,960]{2,1,0:T(8,128)}, u32[]{:S(2)}) copy-start(f32[2,48,960]{2,1,0:T(8,128)} %param.32) | copy-start | bytes 1105924
  504.3 28.9 %copy-start.10 = (f32[48,960]{1,0:T(8,128)S(1)}, f32[48,960]{1,0:T(8,128)}, u32[]{:S(2)}) copy-start(f32[48,960]{1,0:T(8,128)} %get-tuple-element.47) | copy-start | bytes 552964
  504.3 28.9 %copy-start.11 = (f32[48,960]{1,0:T(8,128)S(1)}, f32[48,960]{1,0:T(8,128)}, u32[]{:S(2)}) copy-start(f32[48,960]{1,0:T(8,128)} %get-tuple-element.48) | copy-start | bytes 552964
  504.3 28.9 %copy-start.14 = (f32[2,48,960]{2,1,0:T(8,128)S(1)}, f32[2,48,960]{2,1,0:T(8,128)}, u32[]{:S(2)}) copy-start(f32[2,48,960]{2,1,0:T(8,128)} %param.34) | copy-start | bytes 1105924
  504.3 28.9 %copy-start.15 = (f32[2,48,960]{2,1,0:T(8,128)S(1)}, f32[2,48,960]{2,1,0:T(8,128)}, u32[]{:S(2)}) copy-start(f32[2,48,960]{2,1,0:T(8,128)} %param.33) | copy-start | bytes 1105924
  (13 other events, 49.8 us)

commit v2 on v1

--- a/solution.py
+++ b/solution.py
@@ -113,14 +113,6 @@
     return turn(block, cos_part, -sin_part)
 
 
-def lay_keys(held, kv_rows):
-    for g in range(HEADS):
-        both = jnp.concatenate(
-            [held[0, g * 128 : (g + 1) * 128, :], held[1, g * 128 : (g + 1) * 128, :]], axis=1
-        )
-        kv_rows[g] = jnp.transpose(both.astype(jnp.float32)).astype(jnp.bfloat16)
-
-
 def by_span(context, b, run):
     near = (context == 0) | (b <= 3)
 
@@ -133,87 +125,10 @@
         run(1792)
 
 
-def attend_kernel(
-    packed, cos_ref, sin_ref, limit, turned, kv_all, attended, log_total, kv_rows, send_sem, recv_sem
-):
-    xh, y, core, xl, z = place()
-    peer = device(xh, y, core, 1 - xl, z)
-    greet([peer])
-    cos_part, sin_part = cos_ref[...], sin_ref[...]
-    for g in range(HEADS):
-        base = g * 5 * HD
-        kv_all[xl, g * 128 : g * 128 + HD] = turn(
-            packed[base + 3 * HD : base + 4 * HD], cos_part, sin_part
-        ).astype(jnp.bfloat16)
-        kv_all[xl, g * 128 + HD : (g + 1) * 128] = packed[base + 4 * HD : base + 5 * HD].astype(
-            jnp.bfloat16
-        )
-    copy = remote(kv_all.at[xl], kv_all.at[xl], send_sem, recv_sem, peer)
-    copy.start()
-    for g in range(HEADS):
-        base = g * 5 * HD
-        for h in range(GROUP):
-            turned[(g * GROUP + h) * HD : (g * GROUP + h + 1) * HD] = (
-                turn(packed[base + h * HD : base + (h + 1) * HD], cos_part, sin_part)
-                * HD ** (-0.5)
-            ).astype(jnp.bfloat16)
-    copy.wait()
-    lay_keys(kv_all, kv_rows)
-
-    def block(t, carry):
-        b, g = t // HEADS, lax.rem(t, HEADS)
-        columns = pl.ds(pl.multiple_of(b * 128, 128), 128)
-
-        def run(span):
-            head_rows = [
-                pl.ds(pl.multiple_of((g * GROUP + h) * HD, HD), HD) for h in range(GROUP)
-            ]
-            queries = jnp.concatenate([turned[r, columns] for r in head_rows], axis=1)
-            queries = jnp.concatenate([queries, jnp.zeros_like(queries)], axis=0)
-            scores = nn(kv_rows[g, :span], queries)
-            key_index = lax.broadcasted_iota(jnp.int32, (span, 384), 0)
-            scores = jnp.where(key_index < limit[b], scores, NEG)
-            row_max = jnp.max(scores, axis=0, keepdims=True)
-            shifted = jnp.exp(scores - row_max)
-            exp_total = jnp.sum(shifted, axis=0, keepdims=True)
-            value_rows = pl.ds(pl.multiple_of(g * 128 + HD, HD), HD)
-            values = jnp.concatenate([kv_all[0, value_rows], kv_all[1, value_rows]], axis=1)
-            total = nn(values[:, :span], shifted.astype(jnp.bfloat16)) * (1.0 / exp_total)
-            for h in range(GROUP):
-                attended[head_rows[h], columns] = total[:, h * 128 : (h + 1) * 128].astype(
-                    jnp.bfloat16
-                )
-            log_total[t] = row_max + jnp.log(exp_total)
-
-        by_span(xl, b, run)
-        return carry
-
-    lax.fori_loop(0, HEADS * BLOCKS, block, 0)
-
-
-def attend_forward(packed, cos_part, sin_part, limit):
-    return pl.pallas_call(
-        attend_kernel,
-        out_shape=(
-            jax.ShapeDtypeStruct((384, 896), jnp.bfloat16),
-            jax.ShapeDtypeStruct((2, 256, 896), jnp.bfloat16),
-            jax.ShapeDtypeStruct((384, 896), jnp.bfloat16),
-            jax.ShapeDtypeStruct((HEADS * BLOCKS, 1, 384), jnp.float32),
-        ),
-        scratch_shapes=[
-            pltpu.VMEM((HEADS, 1792, 128), jnp.bfloat16),
-            pltpu.SemaphoreType.DMA,
-            pltpu.SemaphoreType.DMA,
-        ],
-        compiler_params=pltpu.CompilerParams(
-            collective_id=1, has_side_effects=True, vmem_limit_bytes=VMEM_MOST
-        ),
-    )(packed, cos_part, sin_part, limit)
-
-
 def attend_back_kernel(
     turned,
-    kv_all,
+    kv_rows,
+    kv_lines,
     attended,
     log_total,
     grad_attended,
@@ -221,7 +136,6 @@
     sin_ref,
     limit,
     grad_packed,
-    kv_rows,
     sums,
     outgoing,
     incoming,
@@ -232,7 +146,6 @@
     peer = device(xh, y, core, 1 - xl, z)
     greet([peer])
     cos_part, sin_part = cos_ref[...], sin_ref[...]
-    lay_keys(kv_all, kv_rows)
     sums[...] = jnp.zeros_like(sums)
 
     def block(t, carry):
@@ -266,9 +179,7 @@
             sums[g, :span] += nt(
                 jnp.concatenate([grad_scores, probs.astype(jnp.bfloat16)], axis=1), both
             )
-            key_lines = pl.ds(pl.multiple_of(g * 128, HD), HD)
-            keys = jnp.concatenate([kv_all[0, key_lines], kv_all[1, key_lines]], axis=1)
-            total = nn(keys[:, :span], grad_scores) * HD ** (-0.5)
+            total = nn(kv_lines[g, :HD, :span], grad_scores) * HD ** (-0.5)
             cos_here, sin_here = cos_ref[:, columns], sin_ref[:, columns]
             for h in range(GROUP):
                 lines = pl.ds(pl.multiple_of((g * 5 + h) * HD, HD), HD)
@@ -296,12 +207,13 @@
         grad_packed[base + 4 * HD : base + 5 * HD] = mine[HD:].astype(jnp.bfloat16)
 
 
-def attend_backward(turned, kv_all, attended, log_total, grad_attended, cos_part, sin_part, limit):
+def attend_backward(
+    turned, kv_rows, kv_lines, attended, log_total, grad_attended, cos_part, sin_part, limit
+):
     return pl.pallas_call(
         attend_back_kernel,
         out_shape=jax.ShapeDtypeStruct((640, 896), jnp.bfloat16),
         scratch_shapes=[
-            pltpu.VMEM((HEADS, 1792, 128), jnp.bfloat16),
             pltpu.VMEM((HEADS, 1792, 128), jnp.float32),
             pltpu.VMEM((256, 896), jnp.bfloat16),
             pltpu.VMEM((256, 896), jnp.bfloat16),
@@ -311,7 +223,7 @@
         compiler_params=pltpu.CompilerParams(
             collective_id=2, has_side_effects=True, vmem_limit_bytes=VMEM_MOST
         ),
-    )(turned, kv_all, attended, log_total, grad_attended, cos_part, sin_part, limit)
+    )(turned, kv_rows, kv_lines, attended, log_total, grad_attended, cos_part, sin_part, limit)
 
 
 def ring_peers():
@@ -555,72 +467,6 @@
             copy.wait_recv()
         for copy in self.copies:
             copy.wait_send()
-
-
-def start_kernel(
-    first, shrunk, w_in, w_gate, w_up, w_out, w_shrink, *refs
-):
-    owns = (w_in, w_gate, w_up, w_out, w_shrink)
-    (first_all, shrunk_all), helds = refs[:2], refs[2:7]
-    ring_send, ring_recv, plane_send, plane_recv, own_sem = refs[7:]
-    xh, y, core, xl, z = place()
-    z, zp, z2, zm, up, down = ring_peers()
-    ys, xs, y_peers, x_peers, other = plane()
-    greet([up, down, other] + y_peers + x_peers)
-    gathers = [
-        PlaneGather(own, held, i in (1, 2), plane_send.at[i], plane_recv.at[i])
-        for i, (own, held) in enumerate(zip(owns, helds))
-    ]
-    keeps = [
-        pltpu.make_async_copy(own, held.at[xh, y, core, xl], own_sem.at[i])
-        for i, (own, held) in enumerate(zip(owns, helds))
-    ]
-    keeps.append(pltpu.make_async_copy(first, first_all.at[z], own_sem.at[5]))
-    keeps.append(pltpu.make_async_copy(shrunk, shrunk_all.at[z], own_sem.at[6]))
-    for gather in gathers:
-        gather.begin()
-    copies = ring_gather_begin(first, first_all, ring_send.at[0], ring_recv.at[0])
-    for keep in keeps:
-        keep.start()
-    for keep in keeps:
-        keep.wait()
-    for gather in gathers:
-        gather.spread()
-    copies = ring_gather_forward(first_all, copies, ring_send.at[0], ring_recv.at[0])
-    later = ring_gather_begin(shrunk, shrunk_all, ring_send.at[1], ring_recv.at[1])
-    for gather in gathers:
-        gather.share()
-    later = ring_gather_forward(shrunk_all, later, ring_send.at[1], ring_recv.at[1])
-    for gather in gathers:
-        gather.end()
-    ring_gather_end(copies)
-    ring_gather_end(later)
-
-
-def start(first, shrunk, weights):
-    any_place = pl.BlockSpec(memory_space=pl.ANY)
-    rows, width = first.shape
-    outs = pl.pallas_call(
-        start_kernel,
-        out_shape=(jax.ShapeDtypeStruct((4, rows, width), jnp.bfloat16),) * 2
-        + tuple(jax.ShapeDtypeStruct((2, 4, 2, 2) + w.shape, jnp.bfloat16) for w in weights),
-        in_specs=[any_place] * 7,
-        out_specs=(any_place,) * 7,
-        scratch_shapes=[
-            pltpu.SemaphoreType.DMA((2, 6)),
-            pltpu.SemaphoreType.DMA((2, 6)),
-            pltpu.SemaphoreType.DMA((5, 10)),
-            pltpu.SemaphoreType.DMA((5, 10)),
-            pltpu.SemaphoreType.DMA((7,)),
-        ],
-        compiler_params=pltpu.CompilerParams(
-            collective_id=0, has_side_effects=True, vmem_limit_bytes=VMEM_MOST
-        ),
-    )(first, shrunk, *weights)
-    return (
-        outs[0].reshape(4 * rows, width),
-        outs[1].reshape(4 * rows, width),
-    ) + tuple(held.reshape(1536, -1) for held in outs[2:])
 
 
 class PlaneScatter:
@@ -809,6 +655,199 @@
     )(own)
 
 
+def swap_halves(block):
+    lane = lax.broadcasted_iota(jnp.int32, block.shape, 1)
+    return jnp.where(
+        lane < HD // 2, pltpu.roll(block, 128 - HD // 2, 1), pltpu.roll(block, HD // 2, 1)
+    )
+
+
+def front_kernel(*refs):
+    (first, shrunk, w_in, w_gate, w_up, w_out, w_shrink) = refs[:7]
+    (cos_ref, sin_ref, key_cos, key_sin, limit) = refs[7:12]
+    (first_all, shrunk_all, in_all, gate_all, up_all, out_all, shrink_all) = refs[12:19]
+    (turned, kv_rows, kv_lines, attended, log_total, total) = refs[19:25]
+    (packed, held_rows, parts, came, sums) = refs[25:30]
+    (ring_send, ring_recv, plane_send, plane_recv) = refs[30:34]
+    (kv_send, kv_recv, own_sem, out_sem) = refs[34:]
+    xh, y, core, xl, z = place()
+    z, zp, z2, zm, up, down = ring_peers()
+    ys, xs, y_peers, x_peers, other = plane()
+    beside = device(xh, y, core, 1 - xl, z)
+    greet([up, down, other] + y_peers + x_peers)
+    owns = (w_in, w_out, w_gate, w_up, w_shrink)
+    helds = (in_all, out_all, gate_all, up_all, shrink_all)
+    gathers = [
+        PlaneGather(own, held, i in (2, 3), plane_send.at[i], plane_recv.at[i])
+        for i, (own, held) in enumerate(zip(owns, helds))
+    ]
+    for gather in gathers[:2]:
+        gather.begin()
+    ring = ring_gather_begin(first, first_all, ring_send.at[0], ring_recv.at[0])
+    keeps = [
+        pltpu.make_async_copy(own, held.at[xh, y, core, xl], own_sem.at[i])
+        for i, (own, held) in enumerate(zip(owns, helds))
+    ]
+    keeps.append(pltpu.make_async_copy(first, first_all.at[z], own_sem.at[5]))
+    keeps.append(pltpu.make_async_copy(shrunk, shrunk_all.at[z], own_sem.at[6]))
+    for keep in keeps:
+        keep.start()
+    for keep in keeps:
+        keep.wait()
+    for gather in gathers[:2]:
+        gather.spread()
+    ring = ring_gather_forward(first_all, ring, ring_send.at[0], ring_recv.at[0])
+    gathers[0].share()
+    gathers[1].share()
+    gathers[0].end()
+    for gather in gathers[2:]:
+        gather.begin()
+
+    def project(c, rows):
+        out = nn(first_all[c], in_all[...].reshape(1536, 640))
+        packed[rows] = out
+        for g in range(HEADS):
+            block = out[:, g * 320 + 192 : g * 320 + 320]
+            mine = pl.ds(pl.multiple_of(xl * 896 + c * 224, 16), 224)
+            kv_rows[g, mine] = (
+                block * key_cos[rows] + swap_halves(block) * key_sin[rows]
+            ).astype(jnp.bfloat16)
+
+    kv_copies = []
+    for i, c in enumerate((z, zm, zp, z2)):
+        if i == 1:
+            ring[2].wait_recv()
+        if i == 2:
+            ring[3].wait_recv()
+        if i == 3:
+            ring[4].wait_recv()
+            ring[5].wait_recv()
+        project(c, pl.ds(pl.multiple_of(c * 224, 16), 224))
+        mine = kv_rows.at[:, pl.ds(pl.multiple_of(xl * 896 + c * 224, 16), 224)]
+        kv_copies.append(remote(mine, mine, kv_send.at[i], kv_recv.at[i], beside))
+        kv_copies[-1].start()
+    later = ring_gather_begin(shrunk, shrunk_all, ring_send.at[1], ring_recv.at[1])
+
+    def turn_block(b, carry):
+        columns = pl.ds(pl.multiple_of(b * 128, 128), 128)
+        lines = jnp.transpose(packed[columns])
+        cos_here, sin_here = cos_ref[:, columns], sin_ref[:, columns]
+        for g in range(HEADS):
+            for h in range(GROUP):
+                at = (g * 5 + h) * HD
+                turned[(g * GROUP + h) * HD : (g * GROUP + h + 1) * HD, columns] = (
+                    turn(lines[at : at + HD], cos_here, sin_here) * HD ** (-0.5)
+                ).astype(jnp.bfloat16)
+        return carry
+
+    lax.fori_loop(0, BLOCKS, turn_block, 0)
+    for copy in kv_copies:
+        copy.wait_recv()
+    for gather in gathers[2:]:
+        gather.spread()
+    for g in range(HEADS):
+        kv_lines[g] = jnp.transpose(kv_rows[g].astype(jnp.float32)).astype(jnp.bfloat16)
+
+    def block(t, carry):
+        b, g = t // HEADS, lax.rem(t, HEADS)
+        columns = pl.ds(pl.multiple_of(b * 128, 128), 128)
+
+        def run(span):
+            head_rows = [
+                pl.ds(pl.multiple_of((g * GROUP + h) * HD, HD), HD) for h in range(GROUP)
+            ]
+            queries = jnp.concatenate([turned[r, columns] for r in head_rows], axis=1)
+            queries = jnp.concatenate([queries, jnp.zeros_like(queries)], axis=0)
+            scores = nn(kv_rows[g, :span], queries)
+            key_index = lax.broadcasted_iota(jnp.int32, (span, 384), 0)
+            scores = jnp.where(key_index < limit[b], scores, NEG)
+            row_max = jnp.max(scores, axis=0, keepdims=True)
+            shifted = jnp.exp(scores - row_max)
+            exp_total = jnp.sum(shifted, axis=0, keepdims=True)
+            out = nn(kv_lines[g, HD:, :span], shifted.astype(jnp.bfloat16)) * (1.0 / exp_total)
+            for h in range(GROUP):
+                attended[head_rows[h], columns] = out[:, h * 128 : (h + 1) * 128].astype(
+                    jnp.bfloat16
+                )
+            log_total[t] = row_max + jnp.log(exp_total)
+
+        by_span(xl, b, run)
+        return carry
+
+    lax.fori_loop(0, 6, block, 0)
+    later = ring_gather_forward(shrunk_all, later, ring_send.at[1], ring_recv.at[1])
+    lax.fori_loop(6, HEADS * BLOCKS, block, 0)
+    gathers[1].end()
+    fetch = pltpu.make_async_copy(out_all, held_rows, out_sem)
+    fetch.start()
+    tokens = jnp.transpose(attended[...].astype(jnp.float32)).astype(jnp.bfloat16)
+    packed_low = tokens.reshape(4, 224, 384)
+    fetch.wait()
+    for c in range(4):
+        parts[c] = nt(packed_low[c], held_rows[...].reshape(1536, 384)).astype(jnp.bfloat16)
+    scatter = ring_scatter_begin(parts, came, ring_send.at[2], ring_recv.at[2])
+    scatter = ring_scatter_forward(
+        parts, came, sums, scatter, ring_send.at[2], ring_recv.at[2]
+    )
+    for gather in gathers[2:]:
+        gather.share()
+    for gather in gathers[2:]:
+        gather.end()
+    ring_gather_end(later)
+    for copy in kv_copies + ring:
+        copy.wait_send()
+    ring_scatter_end(parts, came, total, scatter)
+
+
+def front(first, shrunk, weights, tables):
+    any_place = pl.BlockSpec(memory_space=pl.ANY)
+    whole = pl.BlockSpec(memory_space=pltpu.VMEM)
+    rows, width = first.shape
+    gathered = [
+        jax.ShapeDtypeStruct((2, 4, 2, 2) + w.shape, jnp.bfloat16) for w in weights
+    ]
+    outs = pl.pallas_call(
+        front_kernel,
+        out_shape=(
+            jax.ShapeDtypeStruct((4, rows, width), jnp.bfloat16),
+            jax.ShapeDtypeStruct((4, rows, width), jnp.bfloat16),
+            *gathered,
+            jax.ShapeDtypeStruct((384, 896), jnp.bfloat16),
+            jax.ShapeDtypeStruct((HEADS, 1792, 128), jnp.bfloat16),
+            jax.ShapeDtypeStruct((HEADS, 128, 1792), jnp.bfloat16),
+            jax.ShapeDtypeStruct((384, 896), jnp.bfloat16),
+            jax.ShapeDtypeStruct((HEADS * BLOCKS, 1, 384), jnp.float32),
+            jax.ShapeDtypeStruct((rows, width), jnp.float32),
+        ),
+        in_specs=[whole] * 12,
+        out_specs=(whole, any_place, whole) + (any_place,) * 4 + (whole,) * 6,
+        scratch_shapes=[
+            pltpu.VMEM((896, 640), jnp.float32),
+            pltpu.VMEM((2, 4, 2, 2, 48, 384), jnp.bfloat16),
+            pltpu.VMEM((4, rows, width), jnp.bfloat16),
+            pltpu.VMEM((6, rows // 2, width), jnp.bfloat16),
+            pltpu.VMEM((2, rows // 2, width), jnp.bfloat16),
+            pltpu.SemaphoreType.DMA((3, 6)),
+            pltpu.SemaphoreType.DMA((3, 6)),
+            pltpu.SemaphoreType.DMA((5, 10)),
+            pltpu.SemaphoreType.DMA((5, 10)),
+            pltpu.SemaphoreType.DMA((4,)),
+            pltpu.SemaphoreType.DMA((4,)),
+            pltpu.SemaphoreType.DMA((7,)),
+            pltpu.SemaphoreType.DMA,
+        ],
+        compiler_params=pltpu.CompilerParams(
+            collective_id=0, has_side_effects=True, vmem_limit_bytes=VMEM_MOST
+        ),
+    )(first, shrunk, *weights, *tables)
+    return (
+        outs[0].reshape(4 * rows, width),
+        outs[1].reshape(4 * rows, width),
+        *(held.reshape(1536, -1) for held in outs[2:7]),
+        *outs[7:],
+    )
+
+
 def product(a, b, a_dim, b_dim):
     return lax.dot_general(
         a, b, (((a_dim,), (b_dim,)), ((), ())), preferred_element_type=jnp.float32
@@ -842,7 +881,28 @@
     normed_one, scale_one = rms_parts(x_rows)
     first_own = (normed_one * norm_gains[0]).astype(low)
     shrunk_own = (RESID * grad_out).astype(low)
-    first_all, shrunk_gradient, w_in, w_gate, w_up, w_out, w_shrink = start(
+    cos_part, sin_part = angles(positions[0])
+    row_index = lax.axis_index("context") * 896 + jnp.arange(896, dtype=jnp.int32)
+    limit = jnp.maximum(row_index + 1, prefix[0]).reshape(BLOCKS, 1, 128)
+    limit = jnp.concatenate([limit] * GROUP, axis=2)
+    still = jnp.ones((896, HD), jnp.float32)
+    key_cos = jnp.concatenate([cos_part.T, cos_part.T, still], axis=1)
+    key_sin = jnp.concatenate([-sin_part.T, sin_part.T, 0.0 * still], axis=1)
+    (
+        first_all,
+        shrunk_gradient,
+        w_in,
+        w_gate,
+        w_up,
+        w_out,
+        w_shrink,
+        turned,
+        kv_rows,
+        kv_lines,
+        attended,
+        log_total,
+        projected,
+    ) = front(
         first_own,
         shrunk_own,
         (
@@ -852,14 +912,8 @@
             output_weight.T.astype(low),
             shrink_weight.T.astype(low),
         ),
-    )
-    cos_part, sin_part = angles(positions[0])
-    row_index = lax.axis_index("context") * 896 + jnp.arange(896, dtype=jnp.int32)
-    limit = jnp.maximum(row_index + 1, prefix[0]).reshape(BLOCKS, 1, 128)
-    limit = jnp.concatenate([limit] * GROUP, axis=2)
-    packed = product(w_in, first_all, 0, 1)
-    turned, kv_all, attended, log_total = attend_forward(packed, cos_part, sin_part, limit)
-    projected = ring_scatter(product(attended, w_out, 0, 1).astype(low), 3)
+        (cos_part, sin_part, key_cos, key_sin, limit),
+    )
     residual = x_rows + RESID * projected
     normed_two, scale_two = rms_parts(residual)
     second_all = ring_gather((normed_two * norm_gains[1]).astype(low), 4)
@@ -880,7 +934,7 @@
     projected_gradient = ring_gather((RESID * grad_residual).astype(low), 6)
     grad_attended = product(w_out, projected_gradient, 0, 1).astype(low)
     grad_packed = attend_backward(
-        turned, kv_all, attended, log_total, grad_attended, cos_part, sin_part, limit
+        turned, kv_rows, kv_lines, attended, log_total, grad_attended, cos_part, sin_part, limit
     )
     grad_first = ring_scatter(product(grad_packed, w_in, 0, 1).astype(low), 7)
     gain_one = jnp.sum(grad_first * normed_one, axis=0)

time: 542 us -> 463 us (0.85)
  Pallas kernels: 395 us -> 325 us
  matrix products: 75.1 us -> 64.2 us
    pallas_call x2 -> x1, Pallas kernels: 139 us -> 90.7 us  [front(): pl.pallas_call(front_kernel, out_shape=(jax.ShapeDtypeStruct((4, rows, wi...]
    pallas_call x4 -> x3, Pallas kernels: 98.4 us -> 76.8 us  [ring_scatter(): pl.pallas_call(ring_scatter_kernel, out_shape=jax.ShapeDtypeStruct((count...]
    dot_general x15 -> x13, matrix products: 75.1 us -> 64.2 us  [product(): lax.dot_general(a, b, (((a_dim,), (b_dim,)), ((), ())), preferred_element...]
where the time goes in v2:
time: 463 us; the launch traced here: 457 us
  Pallas kernels  325 us (70%)
  matrix products  64.2 us (14%)
  other arithmetic  41.9 us (9%)
  local copies, waits for them, and re-layouts  18.5 us (4%)
  between operations  7.15 us (2%)
    pallas_call x1, Pallas kernels, front(): pl.pallas_call(front_kernel, out_shape=(jax.ShapeDtypeStruct((4, rows, wi...  90.7 us
    pallas_call x3, Pallas kernels, ring_scatter(): pl.pallas_call(ring_scatter_kernel, out_shape=jax.ShapeDtypeStruct((count...  76.8 us
    dot_general x13, matrix products, product(): lax.dot_general(a, b, (((a_dim,), (b_dim,)), ((), ())), preferred_element...  64.2 us
    pallas_call x1, Pallas kernels, plane_scatter(): pl.pallas_call(functools.partial(plane_scatter_kernel, turns), out_shape=...  56.7 us
    pallas_call x2, Pallas kernels, ring_gather(): pl.pallas_call(ring_gather_kernel, out_shape=jax.ShapeDtypeStruct((4, cou...  48.1 us
    pallas_call x1, Pallas kernels, attend_backward(): pl.pallas_call(attend_back_kernel, out_shape=jax.ShapeDtypeStruct((640, 8...  36.3 us
    pallas_call x1, Pallas kernels, sum_everywhere(): pl.pallas_call(sum_kernel, out_shape=jax.ShapeDtypeStruct(own.shape, jnp....  16.5 us

profile of v2, /device:TPU:0, one launch (start us, length us, event | category | flops | bytes accessed | tf_op | source)
XLA Modules:
  0.0 456.8 jit_solution(16212202312769763404)
XLA Ops:
  16.7 90.7 %shard_map.322 = (bf16[4,224,1536]{2,1,0:T(8,128)(2,1)}, bf16[4,224,1536]{2,1,0:T(8,128)(2,1)}, bf16[2,4,2,2,48,640]{5,4,3,2,1,0:T(8,128)(2,1)}, bf16[2,4,2,2,48...) custom-call(bf16[224,1536]{1,0:T(8,128)(2,1)} %get-tuple-element.92., ...), custom_call_target="tpu_custom_call" | custom-call | tf_op jit(solution)/shard_map/pallas_call | solution.py:809
  110.1 24.2 %shard_map.323 = bf16[4,224,1536]{2,1,0:T(8,128)(2,1)} custom-call(bf16[224,1536]{1,0:T(8,128)(2,1)} %multiply_convert_fusion.4.own), custom_call_target="tpu_custom_call" | custom-call | tf_op jit(solution)/shard_map/pallas_call | solution.py:295
  134.3 6.3 %fusion.31 = f32[896,960]{0,1:T(8,128)S(1)} fusion(bf16[896,1536]{1,0:T(8,128)(2,1)} %bitcast.94, bf16[1536,960]{1,0:T(8,128)(2,1)} %bitcast.109), kind=kOutput, calls=%fused_computation.91 | convolution fusion | flops 2642411520 | bytes 9142272 | tf_op jit(solution)/shard_map/dot_general | solution.py:852
  144.0 6.4 %multiply_convert_fusion = (bf16[896,960]{0,1:T(8,128)(2,1)}, bf16[896,960]{0,1:T(8,128)(2,1)}, bf16[896,960]{0,1:T(8,128)(2,1)S(1)}) fusion(f32[896,960]{0,1:T(8,128)S(1)} %fusion.30, f32[896,960]{0,1:T(8,128)S(1)} %fusion.31, bf16[896,1536]{1,0:T(8,128)(2,1)S(1)} %bitcast.117, bf16[1536,960]{1,0:T(8,128)(2,1)S(1)} %bitcast.113), kind=kOutput, calls=%fused_computation.6 | convolution fusion | flops 2655313920 | bytes 17743872 | tf_op jit(solution)/shard_map/dot_general | solution.py:852
  150.4 4.5 convolution_convert_fusion.4
  154.9 27.2 %shard_map.324 = f32[224,1536]{1,0:T(8,128)} custom-call(bf16[4,224,1536]{2,1,0:T(8,128)(2,1)} %bitcast.100), custom_call_target="tpu_custom_call" | custom-call | tf_op jit(solution)/shard_map/pallas_call | solution.py:395
  182.2 7.2 %convolution_convert_fusion = bf16[1536,960]{0,1:T(8,128)(2,1)} fusion(bf16[896,960]{0,1:T(8,128)(2,1)} %copy-done.28, bf16[896,1536]{1,0:T(8,128)(2,1)} %bitcast.116), kind=kOutput, calls=%fused_computation.1 | convolution fusion | flops 2643886080 | bytes 7421952 | tf_op jit(solution)/shard_map/dot_general | solution.py:852
  189.4 4.7 %copy.43 = bf16[1536,960]{1,0:T(8,128)(2,1)} copy(bf16[1536,960]{0,1:T(8,128)(2,1)} %convolution_convert_fusion) | data formatting | bytes 5898240 | tf_op jit(solution)/shard_map/convert_element_type | solution.py:949
  194.0 5.6 %fusion.32 = f32[896,1536]{1,0:T(8,128)S(1)} fusion(bf16[896,960]{0,1:T(8,128)(2,1)} %get-tuple-element.78, bf16[1536,960]{1,0:T(8,128)(2,1)} %bitcast.111), kind=kOutput, calls=%fused_computation.92 | convolution fusion | flops 2642411520 | bytes 10174464 | tf_op jit(solution)/shard_map/dot_general | solution.py:852
  199.7 4.5 add_convert_fusion
  204.2 26.1 %shard_map.325 = f32[224,1536]{1,0:T(8,128)} custom-call(bf16[4,224,1536]{2,1,0:T(8,128)(2,1)} %bitcast.101), custom_call_target="tpu_custom_call" | custom-call | tf_op jit(solution)/shard_map/pallas_call | solution.py:395
  234.5 4.6 %convolution_convert_fusion.1 = bf16[1536,960]{0,1:T(8,128)(2,1)} fusion(bf16[896,960]{0,1:T(8,128)(2,1)S(1)} %copy-done.27, bf16[896,1536]{1,0:T(8,128)(2,1)S(1)} %bitcast.96), kind=kOutput, calls=%fused_computation.2 | convolution fusion | flops 2643886080 | bytes 7421952 | tf_op jit(solution)/shard_map/dot_general | solution.py:852
  239.2 4.6 %convolution_convert_fusion.2 = bf16[1536,960]{0,1:T(8,128)(2,1)} fusion(bf16[896,960]{0,1:T(8,128)(2,1)S(1)} %copy-done.25, bf16[896,1536]{1,0:T(8,128)(2,1)S(1)} %bitcast.97), kind=kOutput, calls=%fused_computation.3 | convolution fusion | flops 2643886080 | bytes 7421952 | tf_op jit(solution)/shard_map/dot_general | solution.py:852
  243.8 4.6 %copy.41 = bf16[1536,960]{1,0:T(8,128)(2,1)} copy(bf16[1536,960]{0,1:T(8,128)(2,1)} %convolution_convert_fusion.2) | data formatting | bytes 5898240 | tf_op jit(solution)/shard_map/convert_element_type | solution.py:946
  248.4 4.8 %copy.42 = bf16[1536,960]{1,0:T(8,128)(2,1)} copy(bf16[1536,960]{0,1:T(8,128)(2,1)} %convolution_convert_fusion.1) | data formatting | bytes 5898240 | tf_op jit(solution)/shard_map/convert_element_type | solution.py:947
  253.2 23.9 %shard_map.326 = bf16[4,224,1536]{2,1,0:T(8,128)(2,1)} custom-call(bf16[224,1536]{1,0:T(8,128)(2,1)} %multiply_convert_fusion.3.own), custom_call_target="tpu_custom_call" | custom-call | tf_op jit(solution)/shard_map/pallas_call | solution.py:295
  277.1 4.4 convolution_convert_fusion.7.grad_attended
  281.5 36.3 %shard_map.327 = bf16[640,896]{1,0:T(8,128)(2,1)} custom-call(bf16[384,896]{1,0:T(8,128)(2,1)} %get-tuple-element.41.turned, bf16[2,1792,128]{2,1,0:T(8,128)(2,1)} %get-tuple-element.42.kv_rows, bf16[2,128,1792]{2,1,0:T(8,128)(2,1)} %get-tuple-element.43.kv_lines, bf16[384,896]{1,0:T(8,128)(2,1)} %get-tuple-element.44.attended, ...), custom_call_target="tpu_custom_call" | custom-call | tf_op jit(solution)/shard_map/pallas_call | solution.py:213
  317.9 4.9 %convolution_convert_fusion.6 = bf16[1536,384]{1,0:T(8,128)(2,1)} fusion(bf16[896,1536]{1,0:T(8,128)(2,1)} %bitcast.99, bf16[384,896]{1,0:T(8,128)(2,1)} %get-tuple-element.44.attended), kind=kOutput, calls=%fused_computation.12 | convolution fusion | flops 1057554432 | bytes 4620288 | tf_op jit(solution)/shard_map/dot_general | solution.py:852
  326.5 3.9 convolution_convert_fusion.3
  330.4 23.5 %shard_map.328 = f32[224,1536]{1,0:T(8,128)} custom-call(bf16[4,224,1536]{2,1,0:T(8,128)(2,1)} %bitcast.102), custom_call_target="tpu_custom_call" | custom-call | tf_op jit(solution)/shard_map/pallas_call | solution.py:395
  353.9 56.7 %shard_map.329 = (f32[48,960]{1,0:T(8,128)}, f32[48,960]{1,0:T(8,128)}, f32[48,384]{1,0:T(8,128)}, f32[48,960]{1,0:T(8,128)}, f32[48,640]{1,0:T(8,128)}) custom-call(bf16[2,4,2,2,48,960]{5,4,3,2,1,0:T(8,128)(2,1)} %bitcast.92, bf16[2,4,2,2,48,960]{5,4,3,2,1,0:T(8,128)(2,1)} %bitcast.93, bf16[2,4,2,2,48,384]{5,4,3,2,1,0:T(8,128)(2,1)} %bitcast.104, ...), custom_call_target="tpu_custom_call" | custom-call | tf_op jit(solution)/shard_map/pallas_call | solution.py:603
  421.5 4.1 fusion.11
  426.2 16.5 %shard_map.330 = f32[32,128]{1,0:T(8,128)} custom-call(f32[32,128]{1,0:T(8,128)} %concatenate.15.own), custom_call_target="tpu_custom_call" | custom-call | tf_op jit(solution)/shard_map/pallas_call | solution.py:644
  (106 shorter events, 49.5 us)
Async XLA Ops:
  2.8 416.8 %copy-start.17 = (f32[224]{0:T(256)}, f32[224]{0:T(256)S(1)}, u32[]{:S(2)}) copy-start(f32[224]{0:T(256)S(1)} %add_rsqrt_fusion.1) | copy-start | bytes 2692
  12.5 2.9 copy-start.2
  109.0 123.3 %copy-start.16 = (f32[224]{0:T(256)}, f32[224]{0:T(256)S(1)}, u32[]{:S(2)}) copy-start(f32[224]{0:T(256)S(1)} %add_rsqrt_fusion) | copy-start | bytes 2692
  134.3 6.3 %copy-start.4 = (bf16[4,224,1536]{2,1,0:T(8,128)(2,1)S(1)}, bf16[4,224,1536]{2,1,0:T(8,128)(2,1)}, u32[]{:S(2)}) copy-start(bf16[4,224,1536]{2,1,0:T(8,128)(2,1)} %shard_map.323) | copy-start | bytes 8257540
  134.3 6.3 %copy-start.20 = (bf16[2,4,2,2,48,960]{5,4,3,2,1,0:T(8,128)(2,1)S(1)}, bf16[2,4,2,2,48,960]{5,4,3,2,1,0:T(8,128)(2,1)}, u32[]{:S(2)}) copy-start(bf16[2,4,2,2,48,960]{5,4,3,2,1,0:T(8,128)(2,1)} %get-tuple-element.37) | copy-start | bytes 8847364
  140.6 3.4 copy-start.21
  140.6 3.4 copy-start.23
  150.4 4.5 copy-start.28
  194.0 5.6 %copy-start.19 = (bf16[2,4,2,2,48,960]{5,4,3,2,1,0:T(8,128)(2,1)S(1)}, bf16[2,4,2,2,48,960]{5,4,3,2,1,0:T(8,128)(2,1)}, u32[]{:S(2)}) copy-start(bf16[2,4,2,2,48,960]{5,4,3,2,1,0:T(8,128)(2,1)} %get-tuple-element.38) | copy-start | bytes 8847364
  194.0 5.7 %copy-start.26 = (bf16[896,960]{0,1:T(8,128)(2,1)S(1)}, bf16[896,960]{0,1:T(8,128)(2,1)}, u32[]{:S(2)}) copy-start(bf16[896,960]{0,1:T(8,128)(2,1)} %get-tuple-element.77) | copy-start | bytes 5160964
  230.4 3.3 copy-start.27
  234.5 4.6 %copy-start.25 = (bf16[896,960]{0,1:T(8,128)(2,1)S(1)}, bf16[896,960]{0,1:T(8,128)(2,1)}, u32[]{:S(2)}) copy-start(bf16[896,960]{0,1:T(8,128)(2,1)} %get-tuple-element.78) | copy-start | bytes 5160964
  317.8 4.9 %copy-start.7 = (bf16[640,896]{1,0:T(8,128)(2,1)S(1)}, bf16[640,896]{1,0:T(8,128)(2,1)}, u32[]{:S(2)}) copy-start(bf16[640,896]{1,0:T(8,128)(2,1)} %shard_map.327) | copy-start | bytes 3440644
  317.8 4.9 %copy-start.22 = (bf16[4,224,1536]{2,1,0:T(8,128)(2,1)S(1)}, bf16[4,224,1536]{2,1,0:T(8,128)(2,1)}, u32[]{:S(2)}) copy-start(bf16[4,224,1536]{2,1,0:T(8,128)(2,1)} %get-tuple-element.48) | copy-start | bytes 8257540
  322.7 3.8 copy-start.24
  421.5 25.9 %copy-start.15 = (f32[2,1536]{1,0:T(2,128)S(1)}, f32[2,1536]{1,0:T(2,128)}, u32[]{:S(2)}) copy-start(f32[2,1536]{1,0:T(2,128)} %param.23) | copy-start | bytes 36868
  421.5 27.2 %copy-start.14 = (f32[384,48]{0,1:T(8,128)S(1)}, f32[384,48]{0,1:T(8,128)}, u32[]{:S(2)}) copy-start(f32[384,48]{0,1:T(8,128)} %param.29) | copy-start | bytes 221188
  425.6 26.7 %copy-start.8 = (f32[960,48]{0,1:T(8,128)S(1)}, f32[960,48]{0,1:T(8,128)}, u32[]{:S(2)}) copy-start(f32[960,48]{0,1:T(8,128)} %param.35) | copy-start | bytes 552964
  425.6 26.7 %copy-start.11 = (f32[48,960]{1,0:T(8,128)S(1)}, f32[48,960]{1,0:T(8,128)}, u32[]{:S(2)}) copy-start(f32[48,960]{1,0:T(8,128)} %get-tuple-element.53) | copy-start | bytes 552964
  425.6 28.6 %copy-start.6 = (f32[2,48,960]{2,1,0:T(8,128)S(1)}, f32[2,48,960]{2,1,0:T(8,128)}, u32[]{:S(2)}) copy-start(f32[2,48,960]{2,1,0:T(8,128)} %param.32) | copy-start | bytes 1105924
  425.6 28.6 %copy-start.9 = (f32[48,960]{1,0:T(8,128)S(1)}, f32[48,960]{1,0:T(8,128)}, u32[]{:S(2)}) copy-start(f32[48,960]{1,0:T(8,128)} %get-tuple-element.51) | copy-start | bytes 552964
  425.6 28.6 %copy-start.10 = (f32[48,960]{1,0:T(8,128)S(1)}, f32[48,960]{1,0:T(8,128)}, u32[]{:S(2)}) copy-start(f32[48,960]{1,0:T(8,128)} %get-tuple-element.52) | copy-start | bytes 552964
  425.6 28.6 %copy-start.12 = (f32[2,48,960]{2,1,0:T(8,128)S(1)}, f32[2,48,960]{2,1,0:T(8,128)}, u32[]{:S(2)}) copy-start(f32[2,48,960]{2,1,0:T(8,128)} %param.34) | copy-start | bytes 1105924
  425.6 28.6 %copy-start.13 = (f32[2,48,960]{2,1,0:T(8,128)S(1)}, f32[2,48,960]{2,1,0:T(8,128)}, u32[]{:S(2)}) copy-start(f32[2,48,960]{2,1,0:T(8,128)} %param.33) | copy-start | bytes 1105924
  (5 other events, 10.4 us)

commit v3 on v2

--- a/solution.py
+++ b/solution.py
@@ -317,17 +317,31 @@
     lax.fori_loop(0, count // step, body, 0)
 
 
-def ring_scatter_begin(parts, came, send_sem, recv_sem):
+def ring_scatter_near(parts, came, send_sem, recv_sem):
     z, zp, z2, zm, up, down = ring_peers()
     copies = [
-        remote(halves(parts, z2)[1], came.at[0], send_sem.at[0], recv_sem.at[0], up),
-        remote(halves(parts, z2)[0], came.at[1], send_sem.at[1], recv_sem.at[1], down),
         remote(halves(parts, zp)[0], came.at[2], send_sem.at[2], recv_sem.at[2], up),
         remote(halves(parts, zm)[1], came.at[3], send_sem.at[3], recv_sem.at[3], down),
     ]
     for copy in copies:
         copy.start()
     return copies
+
+
+def ring_scatter_far(parts, came, send_sem, recv_sem):
+    z, zp, z2, zm, up, down = ring_peers()
+    copies = [
+        remote(halves(parts, z2)[1], came.at[0], send_sem.at[0], recv_sem.at[0], up),
+        remote(halves(parts, z2)[0], came.at[1], send_sem.at[1], recv_sem.at[1], down),
+    ]
+    for copy in copies:
+        copy.start()
+    return copies
+
+
+def ring_scatter_begin(parts, came, send_sem, recv_sem):
+    far = ring_scatter_far(parts, came, send_sem, recv_sem)
+    return far + ring_scatter_near(parts, came, send_sem, recv_sem)
 
 
 def ring_scatter_forward(parts, came, sums, copies, send_sem, recv_sem):
@@ -842,10 +856,146 @@
     )(first, shrunk, *weights, *tables)
     return (
         outs[0].reshape(4 * rows, width),
-        outs[1].reshape(4 * rows, width),
+        outs[1],
         *(held.reshape(1536, -1) for held in outs[2:7]),
         *outs[7:],
     )
+
+
+def tn(a, b):
+    return lax.dot_general(a, b, (((0,), (0,)), ((), ())), preferred_element_type=jnp.float32)
+
+
+def middle_kernel(*refs):
+    (hidden, cotangent, projected, gain) = refs[:4]
+    (shrunk_from, gate_from, up_from, shrink_from) = refs[4:8]
+    (residual, grad_residual, turned_back, gain_two) = refs[8:12]
+    (grad_gate, grad_up, grad_shrink, out_parts) = refs[12:16]
+    (shrunk_all, w_gate, w_up, w_shrink) = refs[16:20]
+    (second_all, activated_back, gated, gate_back, up_back) = refs[20:25]
+    (parts, came, sums, total) = refs[25:29]
+    (ring_send, ring_recv, load_sem) = refs[29:]
+    z, zp, z2, zm, up, down = ring_peers()
+    greet([up, down])
+    loads = [
+        pltpu.make_async_copy(src, dst, load_sem.at[i])
+        for i, (src, dst) in enumerate(
+            (
+                (shrink_from, w_shrink),
+                (shrunk_from, shrunk_all),
+                (gate_from, w_gate),
+                (up_from, w_up),
+            )
+        )
+    ]
+    for load in loads:
+        load.start()
+    rows = hidden[...].astype(jnp.float32) + RESID * projected[...]
+    residual[...] = rows
+    scaling = lax.rsqrt(jnp.mean(rows * rows, axis=-1, keepdims=True) + EPS)
+    second_all[z] = (rows * scaling * gain[...]).astype(jnp.bfloat16)
+    ring = ring_gather_begin(second_all.at[z], second_all, ring_send.at[0], ring_recv.at[0])
+    loads[0].wait()
+    loads[1].wait()
+    for c in range(4):
+        activated_back[c] = nn(shrunk_all[c], w_shrink[...])
+    loads[2].wait()
+    loads[3].wait()
+
+    def feed(c):
+        gate_value = nn(second_all[c], w_gate[...])
+        up_value = nn(second_all[c], w_up[...])
+        sigmoid_gate = 1.0 / (1.0 + jnp.exp(-gate_value))
+        gate_active = gate_value * sigmoid_gate
+        gated[c] = (gate_active * up_value).astype(jnp.bfloat16)
+        gradient = activated_back[c]
+        gate_back[c] = (
+            gradient * up_value * sigmoid_gate * (1.0 + gate_value * (1.0 - sigmoid_gate))
+        ).astype(jnp.bfloat16)
+        up_back[c] = (gradient * gate_active).astype(jnp.bfloat16)
+        parts[c] = (nt(gate_back[c], w_gate[...]) + nt(up_back[c], w_up[...])).astype(
+            jnp.bfloat16
+        )
+
+    feed(z)
+    ring = ring_gather_forward(second_all, ring, ring_send.at[0], ring_recv.at[0])
+    ring[2].wait_recv()
+    feed(zm)
+    ring[3].wait_recv()
+    feed(zp)
+    near = ring_scatter_near(parts, came, ring_send.at[1], ring_recv.at[1])
+    ring[4].wait_recv()
+    ring[5].wait_recv()
+    feed(z2)
+    far = ring_scatter_far(parts, came, ring_send.at[1], ring_recv.at[1])
+    second_rows = second_all[...].reshape(896, 1536)
+    grad_gate[...] = tn(second_rows, gate_back[...].reshape(896, 960)).astype(jnp.bfloat16)
+    scatter = ring_scatter_forward(
+        parts, came, sums, far + near, ring_send.at[1], ring_recv.at[1]
+    )
+    grad_up[...] = tn(second_rows, up_back[...].reshape(896, 960)).astype(jnp.bfloat16)
+    grad_shrink[...] = tn(
+        shrunk_all[...].reshape(896, 1536), gated[...].reshape(896, 960)
+    ).astype(jnp.bfloat16)
+    for c in range(4):
+        out_parts[c] = nt(gated[c], w_shrink[...]).astype(jnp.bfloat16)
+    for copy in ring:
+        copy.wait_send()
+    ring_scatter_end(parts, came, total, scatter)
+    rows = residual[...]
+    scaling = lax.rsqrt(jnp.mean(rows * rows, axis=-1, keepdims=True) + EPS)
+    normed = rows * scaling
+    gradient = total[...]
+    gain_two[...] = jnp.sum(gradient * normed, axis=0, keepdims=True)
+    gradient = gradient * gain[...]
+    back = cotangent[...].astype(jnp.float32) + scaling * (
+        gradient - normed * jnp.mean(gradient * normed, axis=-1, keepdims=True)
+    )
+    grad_residual[...] = back
+    turned_back[...] = (RESID * back).astype(jnp.bfloat16)
+
+
+def middle(hidden, cotangent, projected, gain, shrunk_all, w_gate, w_up, w_shrink):
+    any_place = pl.BlockSpec(memory_space=pl.ANY)
+    whole = pl.BlockSpec(memory_space=pltpu.VMEM)
+    rows, width = hidden.shape
+    low, full = jnp.bfloat16, jnp.float32
+    return pl.pallas_call(
+        middle_kernel,
+        out_shape=(
+            jax.ShapeDtypeStruct((rows, width), full),
+            jax.ShapeDtypeStruct((rows, width), full),
+            jax.ShapeDtypeStruct((rows, width), low),
+            jax.ShapeDtypeStruct((1, width), full),
+            jax.ShapeDtypeStruct((1536, 960), low),
+            jax.ShapeDtypeStruct((1536, 960), low),
+            jax.ShapeDtypeStruct((1536, 960), low),
+            jax.ShapeDtypeStruct((4, rows, width), low),
+        ),
+        in_specs=[whole] * 4 + [any_place] * 4,
+        out_specs=(whole,) * 8,
+        scratch_shapes=[
+            pltpu.VMEM((4, rows, width), low),
+            pltpu.VMEM((1536, 960), low),
+            pltpu.VMEM((1536, 960), low),
+            pltpu.VMEM((1536, 960), low),
+            pltpu.VMEM((4, rows, width), low),
+            pltpu.VMEM((4, rows, 960), full),
+            pltpu.VMEM((4, rows, 960), low),
+            pltpu.VMEM((4, rows, 960), low),
+            pltpu.VMEM((4, rows, 960), low),
+            pltpu.VMEM((4, rows, width), low),
+            pltpu.VMEM((6, rows // 2, width), low),
+            pltpu.VMEM((2, rows // 2, width), low),
+            pltpu.VMEM((rows, width), full),
+            pltpu.SemaphoreType.DMA((2, 6)),
+            pltpu.SemaphoreType.DMA((2, 6)),
+            pltpu.SemaphoreType.DMA((4,)),
+        ],
+        compiler_params=pltpu.CompilerParams(
+            collective_id=4, has_side_effects=True, vmem_limit_bytes=VMEM_MOST
+        ),
+    )(hidden, cotangent, projected, gain, shrunk_all, w_gate, w_up, w_shrink)
 
 
 def product(a, b, a_dim, b_dim):
@@ -877,10 +1027,9 @@
 ):
     low = jnp.bfloat16
     x_rows = hidden_in[0].astype(jnp.float32)
-    grad_out = cotangent[0].astype(jnp.float32)
     normed_one, scale_one = rms_parts(x_rows)
     first_own = (normed_one * norm_gains[0]).astype(low)
-    shrunk_own = (RESID * grad_out).astype(low)
+    shrunk_own = (RESID * cotangent[0].astype(jnp.float32)).astype(low)
     cos_part, sin_part = angles(positions[0])
     row_index = lax.axis_index("context") * 896 + jnp.arange(896, dtype=jnp.int32)
     limit = jnp.maximum(row_index + 1, prefix[0]).reshape(BLOCKS, 1, 128)
@@ -890,7 +1039,7 @@
     key_sin = jnp.concatenate([-sin_part.T, sin_part.T, 0.0 * still], axis=1)
     (
         first_all,
-        shrunk_gradient,
+        shrunk_all,
         w_in,
         w_gate,
         w_up,
@@ -914,24 +1063,26 @@
         ),
         (cos_part, sin_part, key_cos, key_sin, limit),
     )
-    residual = x_rows + RESID * projected
-    normed_two, scale_two = rms_parts(residual)
-    second_all = ring_gather((normed_two * norm_gains[1]).astype(low), 4)
-    gate_value = product(second_all, w_gate, 1, 0)
-    up_value = product(second_all, w_up, 1, 0)
-    sigmoid_gate = jax.nn.sigmoid(gate_value)
-    gate_active = gate_value * sigmoid_gate
-    gated_hidden = (gate_active * up_value).astype(low)
-    grad_activated = product(shrunk_gradient, w_shrink, 1, 0)
-    gate_gradient = (
-        grad_activated * up_value * sigmoid_gate * (1.0 + gate_value * (1.0 - sigmoid_gate))
-    ).astype(low)
-    up_gradient = (grad_activated * gate_active).astype(low)
-    second_terms = product(gate_gradient, w_gate, 1, 1) + product(up_gradient, w_up, 1, 1)
-    grad_second = ring_scatter(second_terms.astype(low), 5)
-    gain_two = jnp.sum(grad_second * normed_two, axis=0)
-    grad_residual = grad_out + rms_back(grad_second * norm_gains[1], normed_two, scale_two)
-    projected_gradient = ring_gather((RESID * grad_residual).astype(low), 6)
+    (
+        residual,
+        grad_residual,
+        projected_gradient,
+        gain_two,
+        grad_gate,
+        grad_up,
+        grad_shrink,
+        out_parts,
+    ) = middle(
+        hidden_in[0],
+        cotangent[0],
+        projected,
+        norm_gains[1:],
+        shrunk_all,
+        w_gate,
+        w_up,
+        w_shrink,
+    )
+    projected_gradient = ring_gather(projected_gradient, 6)
     grad_attended = product(w_out, projected_gradient, 0, 1).astype(low)
     grad_packed = attend_backward(
         turned, kv_rows, kv_lines, attended, log_total, grad_attended, cos_part, sin_part, limit
@@ -939,14 +1090,14 @@
     grad_first = ring_scatter(product(grad_packed, w_in, 0, 1).astype(low), 7)
     gain_one = jnp.sum(grad_first * normed_one, axis=0)
     input_gradient = grad_residual + rms_back(grad_first * norm_gains[0], normed_one, scale_one)
-    shrunk = ring_scatter(product(gated_hidden, w_shrink, 1, 1).astype(low), 8)
+    shrunk = ring_scatter(out_parts.reshape(896, 1536), 8)
     block_output = (residual + RESID * shrunk).astype(low)
     grad_gate, grad_up, grad_output, grad_shrink, grad_input = plane_scatter(
         (
-            product(second_all, gate_gradient, 0, 0).astype(low),
-            product(second_all, up_gradient, 0, 0).astype(low),
+            grad_gate,
+            grad_up,
             product(projected_gradient, attended, 0, 1).astype(low),
-            product(shrunk_gradient, gated_hidden, 0, 0).astype(low),
+            grad_shrink,
             product(first_all, grad_packed, 0, 1).astype(low),
         ),
         (True, True, False, False, False),
@@ -956,7 +1107,7 @@
     grad_output, grad_shrink = grad_output.T, grad_shrink.T
     reduced = (grad_input, grad_output, grad_expand, grad_shrink)
     local_squares = sum(jnp.sum(g * g) for g in reduced)
-    gains_local = jnp.stack([gain_one, gain_two]).reshape(24, 128)
+    gains_local = jnp.stack([gain_one, gain_two[0]]).reshape(24, 128)
     message = jnp.concatenate([gains_local, jnp.full((8, 128), local_squares)], axis=0)
     message = sum_everywhere(message, 10)
     grad_gains = message[:24].reshape(2, 1536)

time: 463 us -> 390 us (0.84)
  matrix products: 64.2 us -> 14.5 us
  local copies, waits for them, and re-layouts: 18.5 us -> 4.36 us
  other arithmetic: 41.9 us -> 31.2 us
    pallas_call x0 -> x1, Pallas kernels: none -> 61.9 us  [middle(): pl.pallas_call(middle_kernel, out_shape=(jax.ShapeDtypeStruct((rows, widt...]
    dot_general x13 -> x4, matrix products: 64.2 us -> 14.5 us  [product(): lax.dot_general(a, b, (((a_dim,), (b_dim,)), ((), ())), preferred_element...]
    pallas_call x3 -> x2, Pallas kernels: 76.8 us -> 41.4 us  [ring_scatter(): pl.pallas_call(ring_scatter_kernel, out_shape=jax.ShapeDtypeStruct((count...]
    pallas_call x2 -> x1, Pallas kernels: 48.1 us -> 23.8 us  [ring_gather(): pl.pallas_call(ring_gather_kernel, out_shape=jax.ShapeDtypeStruct((4, cou...]
    convert_element_type x3 -> x0, local copies, waits for them, and re-layouts: 14.1 us -> none  [the longest x1 4.8 us: shards(): product(second_all, up_gradient, 0, 0).astype(low)]
where the time goes in v3:
time: 390 us; the launch traced here: 385 us
  Pallas kernels  328 us (84%)
  other arithmetic  31.2 us (8%)
  matrix products  14.5 us (4%)
  between operations  7.18 us (2%)
  local copies, waits for them, and re-layouts  4.36 us (1%)
    pallas_call x1, Pallas kernels, front(): pl.pallas_call(front_kernel, out_shape=(jax.ShapeDtypeStruct((4, rows, wi...  90.8 us
    pallas_call x1, Pallas kernels, middle(): pl.pallas_call(middle_kernel, out_shape=(jax.ShapeDtypeStruct((rows, widt...  61.9 us
    pallas_call x1, Pallas kernels, plane_scatter(): pl.pallas_call(functools.partial(plane_scatter_kernel, turns), out_shape=...  58.4 us
    pallas_call x2, Pallas kernels, ring_scatter(): pl.pallas_call(ring_scatter_kernel, out_shape=jax.ShapeDtypeStruct((count...  41.4 us
    pallas_call x1, Pallas kernels, attend_backward(): pl.pallas_call(attend_back_kernel, out_shape=jax.ShapeDtypeStruct((640, 8...  36.7 us
    pallas_call x1, Pallas kernels, ring_gather(): pl.pallas_call(ring_gather_kernel, out_shape=jax.ShapeDtypeStruct((4, cou...  23.8 us
    pallas_call x1, Pallas kernels, sum_everywhere(): pl.pallas_call(sum_kernel, out_shape=jax.ShapeDtypeStruct(own.shape, jnp....  14.8 us
    dot_general x4, matrix products, product(): lax.dot_general(a, b, (((a_dim,), (b_dim,)), ((), ())), preferred_element...  14.5 us

profile of v3, /device:TPU:0, one launch (start us, length us, event | category | flops | bytes accessed | tf_op | source)
XLA Modules:
  0.0 385.1 jit_solution(601998729292298549)
XLA Ops:
  4.2 1.4 fusion.28
  5.6 1.5 convert_bitcast_fusion.1.refs_5_
  7.1 1.5 convert_element_type.54.refs_2_
  8.6 1.6 convert_bitcast_fusion.refs_6_
  12.1 1.7 fusion.16
  16.5 90.8 %shard_map.322 = (bf16[4,224,1536]{2,1,0:T(8,128)(2,1)}, bf16[4,224,1536]{2,1,0:T(8,128)(2,1)}, bf16[2,4,2,2,48,640]{5,4,3,2,1,0:T(8,128)(2,1)}, bf16[2,4,2,2,48...) custom-call(bf16[224,1536]{1,0:T(8,128)(2,1)} %get-tuple-element.98., ...), custom_call_target="tpu_custom_call" | custom-call | tf_op jit(solution)/shard_map/pallas_call | solution.py:823
  107.4 61.9 %shard_map.323 = (f32[224,1536]{1,0:T(8,128)}, f32[224,1536]{1,0:T(8,128)}, bf16[224,1536]{1,0:T(8,128)(2,1)}, f32[1,1536]{1,0:T(1,128)}, bf16[1536,960]{1,0:T(8...) custom-call(bf16[224,1536]{1,0:T(8,128)(2,1)} %bitcast.60, ...), custom_call_target="tpu_custom_call" | custom-call | tf_op jit(solution)/shard_map/pallas_call | solution.py:963
  169.3 22.3 %shard_map.324 = f32[224,1536]{1,0:T(8,128)} custom-call(bf16[4,224,1536]{2,1,0:T(8,128)(2,1)} %get-tuple-element.50.parts), custom_call_target="tpu_custom_call" | custom-call | tf_op jit(solution)/shard_map/pallas_call | solution.py:409
  191.6 2.4 fusion.12
  194.0 23.8 %shard_map.325 = bf16[4,224,1536]{2,1,0:T(8,128)(2,1)} custom-call(bf16[224,1536]{1,0:T(8,128)(2,1)} %get-tuple-element.58.own), custom_call_target="tpu_custom_call" | custom-call | tf_op jit(solution)/shard_map/pallas_call | solution.py:295
  217.8 4.0 %convolution_convert_fusion.3.grad_attended = bf16[384,896]{1,0:T(8,128)(2,1)} fusion(bf16[1536,384]{1,0:T(8,128)(2,1)S(1)} %bitcast.79, bf16[896,1536]{1,0:T(8,128)(2,1)} %bitcast.68), kind=kOutput, calls=%fused_computation.19 | convolution fusion | flops 1057308672 | bytes 4620288 | tf_op jit(solution)/shard_map/dot_general | solution.py:1002
  221.8 36.7 %shard_map.326 = bf16[640,896]{1,0:T(8,128)(2,1)} custom-call(bf16[384,896]{1,0:T(8,128)(2,1)} %get-tuple-element.52.turned, bf16[2,1792,128]{2,1,0:T(8,128)(2,1)} %get-tuple-element.53.kv_rows, bf16[2,128,1792]{2,1,0:T(8,128)(2,1)} %get-tuple-element.54.kv_lines, bf16[384,896]{1,0:T(8,128)(2,1)} %get-tuple-element.55.attended, ...), custom_call_target="tpu_custom_call" | custom-call | tf_op jit(solution)/shard_map/pallas_call | solution.py:213
  258.6 2.8 convolution_convert_fusion.2
  261.4 3.8 convolution_convert_fusion.1
  265.2 3.9 %convolution_convert_fusion = bf16[896,1536]{1,0:T(8,128)(2,1)} fusion(bf16[640,896]{1,0:T(8,128)(2,1)S(1)} %copy-done.7, bf16[1536,640]{1,0:T(8,128)(2,1)S(1)} %bitcast.78), kind=kOutput, calls=%fused_computation | convolution fusion | flops 1762983936 | bytes 5865472 | tf_op jit(solution)/shard_map/dot_general | solution.py:1002
  269.1 19.1 %shard_map.327 = f32[224,1536]{1,0:T(8,128)} custom-call(bf16[4,224,1536]{2,1,0:T(8,128)(2,1)} %bitcast.70), custom_call_target="tpu_custom_call" | custom-call | tf_op jit(solution)/shard_map/pallas_call | solution.py:409
  288.2 58.4 %shard_map.328 = (f32[48,960]{1,0:T(8,128)}, f32[48,960]{1,0:T(8,128)}, f32[48,384]{1,0:T(8,128)}, f32[48,960]{1,0:T(8,128)}, f32[48,640]{1,0:T(8,128)}) custom-call(bf16[2,4,2,2,48,960]{5,4,3,2,1,0:T(8,128)(2,1)} %bitcast.61, bf16[2,4,2,2,48,960]{5,4,3,2,1,0:T(8,128)(2,1)} %bitcast.62, bf16[2,4,2,2,48,384]{5,4,3,2,1,0:T(8,128)(2,1)} %bitcast.72, ...), custom_call_target="tpu_custom_call" | custom-call | tf_op jit(solution)/shard_map/pallas_call | solution.py:617
  346.6 1.6 multiply_reduce_fusion.1
  348.2 1.5 multiply_reduce_fusion.3
  349.7 1.5 multiply_reduce_fusion.2
  352.5 1.7 multiply_reduce_fusion
  356.2 2.9 fusion.9
  359.8 14.8 %shard_map.329 = f32[32,128]{1,0:T(8,128)} custom-call(f32[32,128]{1,0:T(8,128)} %concatenate.15.own), custom_call_target="tpu_custom_call" | custom-call | tf_op jit(solution)/shard_map/pallas_call | solution.py:658
  374.6 1.3 multiply_reduce_fusion.4
  (93 shorter events, 14.9 us)
Async XLA Ops:
  0.7 9.5 %copy-start.5 = (f32[2,48,960]{2,1,0:T(8,128)S(1)}, f32[2,48,960]{2,1,0:T(8,128)}, u32[]{:S(2)}) copy-start(f32[2,48,960]{2,1,0:T(8,128)} %param.32) | copy-start | bytes 1105924
  169.3 22.3 %copy-start.6 = (f32[224,1536]{1,0:T(8,128)S(1)}, f32[224,1536]{1,0:T(8,128)}, u32[]{:S(2)}) copy-start(f32[224,1536]{1,0:T(8,128)} %get-tuple-element.49) | copy-start | bytes 4128772
  194.0 23.8 %copy-start.31 = (bf16[2,4,2,2,48,384]{5,4,3,2,1,0:T(8,128)(2,1)S(1)}, bf16[2,4,2,2,48,384]{5,4,3,2,1,0:T(8,128)(2,1)}, u32[]{:S(2)}) copy-start(bf16[2,4,2,2,48,384]{5,4,3,2,1,0:T(8,128)(2,1)} %get-tuple-element.57) | copy-start | bytes 3538948
  221.8 36.7 %copy-start.4 = (bf16[4,224,1536]{2,1,0:T(8,128)(2,1)S(1)}, bf16[4,224,1536]{2,1,0:T(8,128)(2,1)}, u32[]{:S(2)}) copy-start(bf16[4,224,1536]{2,1,0:T(8,128)(2,1)} %shard_map.325) | copy-start | bytes 8257540
  221.8 36.7 %copy-start.12 = (bf16[384,896]{1,0:T(8,128)(2,1)S(1)}, bf16[384,896]{1,0:T(8,128)(2,1)}, u32[]{:S(2)}) copy-start(bf16[384,896]{1,0:T(8,128)(2,1)} %get-tuple-element.55.attended) | copy-start | bytes 2064388
  261.4 3.8 copy-start.30
  288.2 67.4 %copy-start.1 = (bf16[1,224,1536]{2,1,0:T(8,128)(2,1)S(1)}, bf16[1,224,1536]{2,1,0:T(8,128)(2,1)}, u32[]{:S(2)}) copy-start(bf16[1,224,1536]{2,1,0:T(8,128)(2,1)} %param.19) | copy-start | bytes 2064388
  288.2 67.4 %copy-start.2 = (f32[224,1536]{1,0:T(8,128)S(1)}, f32[224,1536]{1,0:T(8,128)}, u32[]{:S(2)}) copy-start(f32[224,1536]{1,0:T(8,128)} %shard_map.327) | copy-start | bytes 4128772
  348.1 7.9 %copy-start.28 = (f32[1,1536]{1,0:T(1,128)S(1)}, f32[1,1536]{1,0:T(1,128)}, u32[]{:S(2)}) copy-start(f32[1,1536]{1,0:T(1,128)} %get-tuple-element.60) | copy-start | bytes 18436
  356.1 23.1 %copy-start.25 = (f32[2,1536]{1,0:T(2,128)S(1)}, f32[2,1536]{1,0:T(2,128)}, u32[]{:S(2)}) copy-start(f32[2,1536]{1,0:T(2,128)} %param.23) | copy-start | bytes 36868
  356.1 23.1 %copy-start.26 = (f32[2,1536]{1,0:T(2,128)S(1)}, f32[2,1536]{1,0:T(2,128)}, u32[]{:S(2)}) copy-start(f32[2,1536]{1,0:T(2,128)} %param.25) | copy-start | bytes 36868
  356.1 23.1 %copy-start.27 = (f32[2,1536]{1,0:T(2,128)S(1)}, f32[2,1536]{1,0:T(2,128)}, u32[]{:S(2)}) copy-start(f32[2,1536]{1,0:T(2,128)} %param.24) | copy-start | bytes 36868
  356.1 23.8 %copy-start.17 = (f32[384,48]{0,1:T(8,128)S(1)}, f32[384,48]{0,1:T(8,128)}, u32[]{:S(2)}) copy-start(f32[384,48]{0,1:T(8,128)} %param.29) | copy-start | bytes 221188
  356.2 23.8 %copy-start.18 = (f32[48,384]{1,0:T(8,128)S(1)}, f32[48,384]{1,0:T(8,128)}, u32[]{:S(2)}) copy-start(f32[48,384]{1,0:T(8,128)} %get-tuple-element.66) | copy-start | bytes 221188
  356.2 23.8 %copy-start.23 = (f32[384,48]{0,1:T(8,128)S(1)}, f32[384,48]{0,1:T(8,128)}, u32[]{:S(2)}) copy-start(f32[384,48]{0,1:T(8,128)} %param.31) | copy-start | bytes 221188
  356.2 23.8 %copy-start.24 = (f32[384,48]{0,1:T(8,128)S(1)}, f32[384,48]{0,1:T(8,128)}, u32[]{:S(2)}) copy-start(f32[384,48]{0,1:T(8,128)} %param.30) | copy-start | bytes 221188
  356.2 24.5 %copy-start.13 = (f32[48,640]{1,0:T(8,128)S(1)}, f32[48,640]{1,0:T(8,128)}, u32[]{:S(2)}) copy-start(f32[48,640]{1,0:T(8,128)} %param.26) | copy-start | bytes 368644
  356.2 24.5 %copy-start.14 = (f32[48,640]{1,0:T(8,128)S(1)}, f32[48,640]{1,0:T(8,128)}, u32[]{:S(2)}) copy-start(f32[48,640]{1,0:T(8,128)} %get-tuple-element.65) | copy-start | bytes 368644
  356.2 24.5 %copy-start.21 = (f32[48,640]{1,0:T(8,128)S(1)}, f32[48,640]{1,0:T(8,128)}, u32[]{:S(2)}) copy-start(f32[48,640]{1,0:T(8,128)} %param.28) | copy-start | bytes 368644
  356.2 24.5 %copy-start.22 = (f32[48,640]{1,0:T(8,128)S(1)}, f32[48,640]{1,0:T(8,128)}, u32[]{:S(2)}) copy-start(f32[48,640]{1,0:T(8,128)} %param.27) | copy-start | bytes 368644
  359.2 22.4 %copy-start.8 = (f32[960,48]{0,1:T(8,128)S(1)}, f32[960,48]{0,1:T(8,128)}, u32[]{:S(2)}) copy-start(f32[960,48]{0,1:T(8,128)} %param.35) | copy-start | bytes 552964
  359.2 22.4 %copy-start.11 = (f32[48,960]{1,0:T(8,128)S(1)}, f32[48,960]{1,0:T(8,128)}, u32[]{:S(2)}) copy-start(f32[48,960]{1,0:T(8,128)} %get-tuple-element.69) | copy-start | bytes 552964
  359.2 22.4 %copy-start.19 = (f32[960,48]{0,1:T(8,128)S(1)}, f32[960,48]{0,1:T(8,128)}, u32[]{:S(2)}) copy-start(f32[960,48]{0,1:T(8,128)} %param.37) | copy-start | bytes 552964
  359.2 22.4 %copy-start.20 = (f32[960,48]{0,1:T(8,128)S(1)}, f32[960,48]{0,1:T(8,128)}, u32[]{:S(2)}) copy-start(f32[960,48]{0,1:T(8,128)} %param.36) | copy-start | bytes 552964
  (8 other events, 18.3 us)

commit v4 on v3

--- a/solution.py
+++ b/solution.py
@@ -123,107 +123,6 @@
     @pl.when(jnp.logical_not(near))
     def _():
         run(1792)
-
-
-def attend_back_kernel(
-    turned,
-    kv_rows,
-    kv_lines,
-    attended,
-    log_total,
-    grad_attended,
-    cos_ref,
-    sin_ref,
-    limit,
-    grad_packed,
-    sums,
-    outgoing,
-    incoming,
-    send_sem,
-    recv_sem,
-):
-    xh, y, core, xl, z = place()
-    peer = device(xh, y, core, 1 - xl, z)
-    greet([peer])
-    cos_part, sin_part = cos_ref[...], sin_ref[...]
-    sums[...] = jnp.zeros_like(sums)
-
-    def block(t, carry):
-        b, g = t // HEADS, lax.rem(t, HEADS)
-        columns = pl.ds(pl.multiple_of(b * 128, 128), 128)
-
-        def run(span):
-            head_rows = [
-                pl.ds(pl.multiple_of((g * GROUP + h) * HD, HD), HD) for h in range(GROUP)
-            ]
-            queries = jnp.concatenate([turned[r, columns] for r in head_rows], axis=1)
-            gradient = jnp.concatenate([grad_attended[r, columns] for r in head_rows], axis=1)
-            held = jnp.concatenate([attended[r, columns] for r in head_rows], axis=1)
-            inner = jnp.sum(
-                gradient.astype(jnp.float32) * held.astype(jnp.float32), axis=0, keepdims=True
-            )
-            nothing = jnp.zeros_like(queries)
-            both = jnp.concatenate(
-                [
-                    jnp.concatenate([queries, nothing], axis=1),
-                    jnp.concatenate([nothing, gradient], axis=1),
-                ],
-                axis=0,
-            )
-            products = nn(kv_rows[g, :span], both)
-            key_index = lax.broadcasted_iota(jnp.int32, (span, 384), 0)
-            probs = jnp.exp(
-                jnp.where(key_index < limit[b], products[:, :384], NEG) - log_total[t]
-            )
-            grad_scores = (probs * (products[:, 384:] - inner)).astype(jnp.bfloat16)
-            sums[g, :span] += nt(
-                jnp.concatenate([grad_scores, probs.astype(jnp.bfloat16)], axis=1), both
-            )
-            total = nn(kv_lines[g, :HD, :span], grad_scores) * HD ** (-0.5)
-            cos_here, sin_here = cos_ref[:, columns], sin_ref[:, columns]
-            for h in range(GROUP):
-                lines = pl.ds(pl.multiple_of((g * 5 + h) * HD, HD), HD)
-                grad_packed[lines, columns] = turn_back(
-                    total[:, h * 128 : (h + 1) * 128], cos_here, sin_here
-                ).astype(jnp.bfloat16)
-
-        by_span(xl, b, run)
-        return carry
-
-    lax.fori_loop(0, HEADS * BLOCKS, block, 0)
-    for g in range(HEADS):
-        theirs = sums[g, pl.ds(pl.multiple_of((1 - xl) * 896, 128), 896)]
-        outgoing[g * 128 : (g + 1) * 128] = jnp.transpose(theirs).astype(jnp.bfloat16)
-    copy = remote(outgoing, incoming, send_sem, recv_sem, peer)
-    copy.start()
-    copy.wait()
-    for g in range(HEADS):
-        mine = jnp.transpose(sums[g, pl.ds(pl.multiple_of(xl * 896, 128), 896)])
-        mine = mine + incoming[g * 128 : (g + 1) * 128].astype(jnp.float32)
-        base = g * 5 * HD
-        grad_packed[base + 3 * HD : base + 4 * HD] = turn_back(
-            mine[:HD], cos_part, sin_part
-        ).astype(jnp.bfloat16)
-        grad_packed[base + 4 * HD : base + 5 * HD] = mine[HD:].astype(jnp.bfloat16)
-
-
-def attend_backward(
-    turned, kv_rows, kv_lines, attended, log_total, grad_attended, cos_part, sin_part, limit
-):
-    return pl.pallas_call(
-        attend_back_kernel,
-        out_shape=jax.ShapeDtypeStruct((640, 896), jnp.bfloat16),
-        scratch_shapes=[
-            pltpu.VMEM((HEADS, 1792, 128), jnp.float32),
-            pltpu.VMEM((256, 896), jnp.bfloat16),
-            pltpu.VMEM((256, 896), jnp.bfloat16),
-            pltpu.SemaphoreType.DMA,
-            pltpu.SemaphoreType.DMA,
-        ],
-        compiler_params=pltpu.CompilerParams(
-            collective_id=2, has_side_effects=True, vmem_limit_bytes=VMEM_MOST
-        ),
-    )(turned, kv_rows, kv_lines, attended, log_total, grad_attended, cos_part, sin_part, limit)
 
 
 def ring_peers():
@@ -279,36 +178,6 @@
         copy.wait_recv()
 
 
-def ring_gather_kernel(own, held, send_sem, recv_sem, own_sem):
-    z, zp, z2, zm, up, down = ring_peers()
-    greet([up, down])
-    copies = ring_gather_begin(own, held, send_sem, recv_sem)
-    keep = pltpu.make_async_copy(own, held.at[z], own_sem)
-    keep.start()
-    copies = ring_gather_forward(held, copies, send_sem, recv_sem)
-    keep.wait()
-    ring_gather_end(copies)
-
-
-def ring_gather(rows, identity):
-    count, width = rows.shape
-    held = pl.pallas_call(
-        ring_gather_kernel,
-        out_shape=jax.ShapeDtypeStruct((4, count, width), rows.dtype),
-        in_specs=[pl.BlockSpec(memory_space=pl.ANY)],
-        out_specs=pl.BlockSpec(memory_space=pl.ANY),
-        scratch_shapes=[
-            pltpu.SemaphoreType.DMA((6,)),
-            pltpu.SemaphoreType.DMA((6,)),
-            pltpu.SemaphoreType.DMA,
-        ],
-        compiler_params=pltpu.CompilerParams(
-            collective_id=identity, has_side_effects=True, vmem_limit_bytes=VMEM_MOST
-        ),
-    )(rows)
-    return held.reshape(4 * count, width)
-
-
 def in_rows(count, step, run):
     def body(i, carry):
         run(pl.ds(pl.multiple_of(i * step, step), step))
@@ -395,32 +264,6 @@
     in_rows(count, 16, add)
 
 
-def ring_scatter_kernel(parts, total, came, sums, send_sem, recv_sem):
-    z, zp, z2, zm, up, down = ring_peers()
-    greet([up, down])
-    copies = ring_scatter_begin(parts, came, send_sem, recv_sem)
-    copies = ring_scatter_forward(parts, came, sums, copies, send_sem, recv_sem)
-    ring_scatter_end(parts, came, total, copies)
-
-
-def ring_scatter(parts, identity):
-    rows, width = parts.shape
-    count = rows // 4
-    return pl.pallas_call(
-        ring_scatter_kernel,
-        out_shape=jax.ShapeDtypeStruct((count, width), jnp.float32),
-        scratch_shapes=[
-            pltpu.VMEM((6, count // 2, width), jnp.bfloat16),
-            pltpu.VMEM((2, count // 2, width), jnp.bfloat16),
-            pltpu.SemaphoreType.DMA((6,)),
-            pltpu.SemaphoreType.DMA((6,)),
-        ],
-        compiler_params=pltpu.CompilerParams(
-            collective_id=identity, has_side_effects=True, vmem_limit_bytes=VMEM_MOST
-        ),
-    )(parts.reshape(4, count, width))
-
-
 def plane():
     xh, y, core, xl, z = place()
     ys = [lax.rem(y + d, 4) for d in (1, 3, 2)]
@@ -481,148 +324,6 @@
             copy.wait_recv()
         for copy in self.copies:
             copy.wait_send()
-
-
-class PlaneScatter:
-    def __init__(self, parts, came, halved, across, lined, last, x_first, send_sem, recv_sem):
-        self.parts, self.came, self.halved = parts, came, halved
-        self.across, self.lined, self.last, self.x_first = across, lined, last, x_first
-        self.send_sem, self.recv_sem, self.used, self.copies = send_sem, recv_sem, 0, []
-
-    def send(self, src, dst, peer):
-        copy = remote(src, dst, self.send_sem.at[self.used], self.recv_sem.at[self.used], peer)
-        self.used += 1
-        copy.start()
-        self.copies.append(copy)
-        return copy
-
-    def begin(self):
-        xh, y, core, xl, z = place()
-        ys, xs, y_peers, x_peers, other = plane()
-        self.wheres = (xs[::-1] + [(xh, xl)]) if self.x_first else (ys[::-1] + [y])
-        self.first = []
-        for where in self.wheres:
-            if self.x_first:
-                src = self.parts.at[where[0], :, 1 - core, where[1]]
-                dst = self.came.at[where[0], :, where[1]]
-            else:
-                src, dst = self.parts.at[:, where, 1 - core, :], self.came.at[:, where, :]
-            self.first.append(self.send(src, dst, other))
-
-    def fold(self):
-        xh, y, core, xl, z = place()
-        ys, xs, y_peers, x_peers, other = plane()
-        peers = x_peers[::-1] if self.x_first else y_peers[::-1]
-        self.second = []
-        for k, (where, copy) in enumerate(zip(self.wheres, self.first)):
-            copy.wait_recv()
-
-            def add(i, carry, where=where, k=k):
-                def rows(r):
-                    if self.x_first:
-                        h, l, v = where[0], where[1], i
-                    else:
-                        h, l, v = i // 2, lax.rem(i, 2), where
-                    total = self.parts[h, v, core, l, r].astype(jnp.float32) + self.came[
-                        h, v, l, r
-                    ].astype(jnp.float32)
-                    self.halved[k, i, r] = total.astype(jnp.bfloat16)
-
-                in_rows(48, 16, rows)
-                return carry
-
-            lax.fori_loop(0, 4, add, 0)
-            if k < 3:
-                self.second.append(self.send(self.halved.at[k], self.across.at[k], peers[k]))
-
-    def line(self):
-        xh, y, core, xl, z = place()
-        ys, xs, y_peers, x_peers, other = plane()
-        for copy in self.second:
-            copy.wait_recv()
-
-        def add(i, carry):
-            def rows(r):
-                total = self.halved[3, i, r].astype(jnp.float32)
-                for k in range(3):
-                    total = total + self.across[k, i, r].astype(jnp.float32)
-                self.lined[i, r] = total.astype(jnp.bfloat16)
-
-            in_rows(48, 16, rows)
-            return carry
-
-        lax.fori_loop(0, 4, add, 0)
-        if self.x_first:
-            self.mine, targets, peers = y, ys, y_peers
-        else:
-            self.mine, targets, peers = xh * 2 + xl, [h * 2 + l for h, l in xs], x_peers
-        self.third = [
-            self.send(self.lined.at[target], self.last.at[k], peer)
-            for k, (target, peer) in enumerate(zip(targets, peers))
-        ]
-
-    def end(self, total_ref):
-        for copy in self.third:
-            copy.wait_recv()
-
-        def rows(r):
-            total = self.lined[self.mine, r].astype(jnp.float32)
-            for k in range(3):
-                total = total + self.last[k, r].astype(jnp.float32)
-            total_ref[r] = total
-
-        in_rows(48, 16, rows)
-        for copy in self.copies:
-            copy.wait_send()
-
-
-def scatter_scratch(width):
-    return [
-        pltpu.VMEM((2, 4, 2, 48, width), jnp.bfloat16),
-        pltpu.VMEM((4, 4, 48, width), jnp.bfloat16),
-        pltpu.VMEM((3, 4, 48, width), jnp.bfloat16),
-        pltpu.VMEM((4, 48, width), jnp.bfloat16),
-        pltpu.VMEM((3, 48, width), jnp.bfloat16),
-    ]
-
-
-def plane_scatter_kernel(turns, *refs):
-    n = len(turns)
-    parts, totals, scratch = refs[:n], refs[n : 2 * n], refs[2 * n :]
-    send_sem, recv_sem = scratch[-2:]
-    ys, xs, y_peers, x_peers, other = plane()
-    greet([other] + y_peers + x_peers)
-    scatters = [
-        PlaneScatter(
-            parts[i], *scratch[5 * i : 5 * i + 5], turns[i], send_sem.at[i], recv_sem.at[i]
-        )
-        for i in range(n)
-    ]
-    for scatter in scatters:
-        scatter.begin()
-    for scatter in scatters:
-        scatter.fold()
-    for scatter in scatters:
-        scatter.line()
-    for scatter, total in zip(scatters, totals):
-        scatter.end(total)
-
-
-def plane_scatter(gradients, turns, identity):
-    shaped = [g.reshape(2, 4, 2, 2, 48, g.shape[-1]) for g in gradients]
-    scratch = []
-    for g in gradients:
-        scratch += scatter_scratch(g.shape[-1])
-    n = len(gradients)
-    return pl.pallas_call(
-        functools.partial(plane_scatter_kernel, turns),
-        out_shape=tuple(jax.ShapeDtypeStruct((48, g.shape[-1]), jnp.float32) for g in gradients),
-        scratch_shapes=scratch
-        + [pltpu.SemaphoreType.DMA((n, 10)), pltpu.SemaphoreType.DMA((n, 10))],
-        compiler_params=pltpu.CompilerParams(
-            collective_id=identity, has_side_effects=True, vmem_limit_bytes=VMEM_MOST
-        ),
-    )(*shaped)
 
 
 def sum_kernel(own, total, held, send_sem, recv_sem):
@@ -680,10 +381,10 @@
     (first, shrunk, w_in, w_gate, w_up, w_out, w_shrink) = refs[:7]
     (cos_ref, sin_ref, key_cos, key_sin, limit) = refs[7:12]
     (first_all, shrunk_all, in_all, gate_all, up_all, out_all, shrink_all) = refs[12:19]
-    (turned, kv_rows, kv_lines, attended, log_total, total) = refs[19:25]
-    (packed, held_rows, parts, came, sums) = refs[25:30]
-    (ring_send, ring_recv, plane_send, plane_recv) = refs[30:34]
-    (kv_send, kv_recv, own_sem, out_sem) = refs[34:]
+    (turned, kv_rows, kv_lines, attended, tokens, log_total, total) = refs[19:26]
+    (packed, held_rows, parts, came, sums) = refs[26:31]
+    (ring_send, ring_recv, plane_send, plane_recv) = refs[31:35]
+    (kv_send, kv_recv, own_sem, out_sem) = refs[35:]
     xh, y, core, xl, z = place()
     z, zp, z2, zm, up, down = ring_peers()
     ys, xs, y_peers, x_peers, other = plane()
@@ -794,11 +495,10 @@
     gathers[1].end()
     fetch = pltpu.make_async_copy(out_all, held_rows, out_sem)
     fetch.start()
-    tokens = jnp.transpose(attended[...].astype(jnp.float32)).astype(jnp.bfloat16)
-    packed_low = tokens.reshape(4, 224, 384)
+    tokens[...] = jnp.transpose(attended[...].astype(jnp.float32)).astype(jnp.bfloat16)
     fetch.wait()
     for c in range(4):
-        parts[c] = nt(packed_low[c], held_rows[...].reshape(1536, 384)).astype(jnp.bfloat16)
+        parts[c] = nt(tokens[c * 224 : (c + 1) * 224], held_rows[...].reshape(1536, 384)).astype(jnp.bfloat16)
     scatter = ring_scatter_begin(parts, came, ring_send.at[2], ring_recv.at[2])
     scatter = ring_scatter_forward(
         parts, came, sums, scatter, ring_send.at[2], ring_recv.at[2]
@@ -830,11 +530,12 @@
             jax.ShapeDtypeStruct((HEADS, 1792, 128), jnp.bfloat16),
             jax.ShapeDtypeStruct((HEADS, 128, 1792), jnp.bfloat16),
             jax.ShapeDtypeStruct((384, 896), jnp.bfloat16),
+            jax.ShapeDtypeStruct((896, 384), jnp.bfloat16),
             jax.ShapeDtypeStruct((HEADS * BLOCKS, 1, 384), jnp.float32),
             jax.ShapeDtypeStruct((rows, width), jnp.float32),
         ),
         in_specs=[whole] * 12,
-        out_specs=(whole, any_place, whole) + (any_place,) * 4 + (whole,) * 6,
+        out_specs=(whole, any_place, whole) + (any_place,) * 4 + (whole,) * 7,
         scratch_shapes=[
             pltpu.VMEM((896, 640), jnp.float32),
             pltpu.VMEM((2, 4, 2, 2, 48, 384), jnp.bfloat16),
@@ -855,7 +556,7 @@
         ),
     )(first, shrunk, *weights, *tables)
     return (
-        outs[0].reshape(4 * rows, width),
+        outs[0],
         outs[1],
         *(held.reshape(1536, -1) for held in outs[2:7]),
         *outs[7:],
@@ -998,6 +699,392 @@
     )(hidden, cotangent, projected, gain, shrunk_all, w_gate, w_up, w_shrink)
 
 
+class Scatter:
+    def __init__(self, parts, came, across, lined, last, x_first, send_sem, recv_sem):
+        self.parts, self.came, self.across = parts, came, across
+        self.lined, self.last, self.x_first = lined, last, x_first
+        self.send_sem, self.recv_sem, self.used, self.copies = send_sem, recv_sem, 0, []
+        xh, y, core, xl, z = place()
+        ys, xs, y_peers, x_peers, self.other = plane()
+        if x_first:
+            self.lines, self.peers = xs[::-1] + [(xh, xl)], x_peers[::-1]
+            self.mine, self.targets, self.target_peers = y, ys, y_peers
+        else:
+            self.lines, self.peers = ys[::-1] + [y], y_peers[::-1]
+            self.mine, self.targets, self.target_peers = (xh, xl), xs, x_peers
+
+    def send(self, src, dst, peer):
+        copy = remote(src, dst, self.send_sem.at[self.used], self.recv_sem.at[self.used], peer)
+        self.used += 1
+        copy.start()
+        self.copies.append(copy)
+        return copy
+
+    def in_line(self, line):
+        return (line[0], slice(None), line[1]) if self.x_first else (slice(None), line)
+
+    def begin(self):
+        core = place()[2]
+        self.first = []
+        for line in self.lines:
+            if self.x_first:
+                src = self.parts.at[line[0], :, 1 - core, line[1]]
+            else:
+                src = self.parts.at[:, line, 1 - core]
+            self.first.append(self.send(src, self.came.at[self.in_line(line)], self.other))
+
+    def stage(self, held, sem):
+        copy = pltpu.make_async_copy(self.parts.at[:, :, place()[2]], held, sem)
+        copy.start()
+        return copy
+
+    def at(self, line, i):
+        return (line[0], i, line[1]) if self.x_first else (i // 2, line, lax.rem(i, 2))
+
+    def spot(self, i):
+        if self.x_first:
+            return (i,)
+        return (i[0], i[1]) if isinstance(i, tuple) else (i // 2, lax.rem(i, 2))
+
+    def fold(self, held=None):
+        core = place()[2]
+        self.second = []
+        for k, (line, copy) in enumerate(zip(self.lines, self.first)):
+            copy.wait_recv()
+
+            def add(i, carry, line=line):
+                at = self.at(line, i)
+                if held is None:
+                    own = self.parts[at[0], at[1], core, at[2]]
+                else:
+                    own = held[at]
+                self.came[at] = (
+                    own.astype(jnp.float32) + self.came[at].astype(jnp.float32)
+                ).astype(jnp.bfloat16)
+                return carry
+
+            lax.fori_loop(0, 4, add, 0)
+            if k < 3:
+                self.second.append(
+                    self.send(
+                        self.came.at[self.in_line(line)], self.across.at[k], self.peers[k]
+                    )
+                )
+
+    def line(self):
+        for copy in self.second:
+            copy.wait_recv()
+
+        def add(i, carry):
+            spot = self.spot(i)
+            total = self.came[self.at(self.lines[3], i)].astype(jnp.float32)
+            for k in range(3):
+                total = total + self.across[(k,) + spot].astype(jnp.float32)
+            self.lined[spot] = total.astype(jnp.bfloat16)
+            return carry
+
+        lax.fori_loop(0, 4, add, 0)
+        self.third = [
+            self.send(self.lined.at[self.spot(target)], self.last.at[k], peer)
+            for k, (target, peer) in enumerate(zip(self.targets, self.target_peers))
+        ]
+
+    def end(self, total_ref):
+        for copy in self.third:
+            copy.wait_recv()
+        total = self.lined[self.spot(self.mine)].astype(jnp.float32)
+        for k in range(3):
+            total = total + self.last[k].astype(jnp.float32)
+        total_ref[...] = total
+        for copy in self.copies:
+            copy.wait_send()
+
+
+def scatter_room(width, x_first):
+    line = (4,) if x_first else (2, 2)
+    return [
+        pltpu.VMEM((2, 4, 2, 48, width), jnp.bfloat16),
+        pltpu.VMEM((3,) + line + (48, width), jnp.bfloat16),
+        pltpu.VMEM(line + (48, width), jnp.bfloat16),
+        pltpu.VMEM((3, 48, width), jnp.bfloat16),
+    ]
+
+
+def back_kernel(*refs):
+    (own, out_from, in_from, first_from, out_terms) = refs[:5]
+    gradients = refs[5:8]
+    (turned, kv_rows, kv_lines, attended, tokens, log_total) = refs[8:14]
+    (cos_ref, sin_ref, key_cos, key_sin, limit) = refs[14:19]
+    (shrunk_total, first_total) = refs[19:21]
+    totals = refs[21:26]
+    (proj_all, w_out, w_in, grad_tokens, grad_lines, grad_queries, grad_packed) = refs[26:33]
+    (sums, outgoing, incoming, parts, came_one, came_two, ring_sums) = refs[33:40]
+    stages, out_parts, in_parts = refs[40:42], refs[42], refs[43]
+    rooms = refs[44:64]
+    (ring_send, ring_recv, plane_send, plane_recv, kv_send, kv_recv, load_sem) = refs[64:]
+    xh, y, core, xl, z = place()
+    z, zp, z2, zm, up, down = ring_peers()
+    ys, xs, y_peers, x_peers, other = plane()
+    beside = device(xh, y, core, 1 - xl, z)
+    greet([up, down, other] + y_peers + x_peers)
+    ring = ring_gather_begin(own, proj_all, ring_send.at[0], ring_recv.at[0])
+    every = [
+        Scatter(
+            terms,
+            *rooms[4 * i : 4 * i + 4],
+            SCATTER_TURNS[i],
+            plane_send.at[i],
+            plane_recv.at[i],
+        )
+        for i, terms in enumerate(tuple(gradients) + (out_parts, in_parts))
+    ]
+    feed, out_scatter, in_scatter = every[:3], every[3], every[4]
+    for scatter in feed:
+        scatter.begin()
+
+    def load(src, dst, i):
+        copy = pltpu.make_async_copy(src, dst, load_sem.at[i])
+        copy.start()
+        return copy
+
+    load_out = load(out_from, w_out, 0)
+    keep = load(own, proj_all.at[z], 1)
+    staged = [feed[i].stage(stages[i], load_sem.at[2 + i]) for i in range(2)]
+    load_terms = load(out_terms, parts, 5)
+    load_in = load(in_from, w_in, 6)
+    sums[...] = jnp.zeros_like(sums)
+
+    def give(c):
+        rows = pl.ds(pl.multiple_of(c * 224, 16), 224)
+        grad_tokens[rows] = nn(proj_all[c], w_out[...]).astype(jnp.bfloat16)
+
+    def which(i):
+        shifted = i - 3 + (3 - z) // 3
+        return lax.rem(2 * z + shifted + (shifted + 7) // 7 + 7, 7)
+
+    def lay(b):
+        columns = pl.ds(pl.multiple_of(b * 128, 128), 128)
+        grad_lines[:, columns] = jnp.transpose(
+            grad_tokens[columns].astype(jnp.float32)
+        ).astype(jnp.bfloat16)
+
+    def block(b, g):
+        columns = pl.ds(pl.multiple_of(b * 128, 128), 128)
+
+        def run(span):
+            head_rows = [
+                pl.ds(pl.multiple_of((g * GROUP + h) * HD, HD), HD) for h in range(GROUP)
+            ]
+            queries = jnp.concatenate([turned[r, columns] for r in head_rows], axis=1)
+            gradient = jnp.concatenate([grad_lines[r, columns] for r in head_rows], axis=1)
+            held = jnp.concatenate([attended[r, columns] for r in head_rows], axis=1)
+            inner = jnp.sum(
+                gradient.astype(jnp.float32) * held.astype(jnp.float32), axis=0, keepdims=True
+            )
+            nothing = jnp.zeros_like(queries)
+            both = jnp.concatenate(
+                [
+                    jnp.concatenate([queries, nothing], axis=1),
+                    jnp.concatenate([nothing, gradient], axis=1),
+                ],
+                axis=0,
+            )
+            products = nn(kv_rows[g, :span], both)
+            key_index = lax.broadcasted_iota(jnp.int32, (span, 384), 0)
+            probs = jnp.exp(
+                jnp.where(key_index < limit[b], products[:, :384], NEG)
+                - log_total[b * HEADS + g]
+            )
+            grad_scores = (probs * (products[:, 384:] - inner)).astype(jnp.bfloat16)
+            sums[g, :span] += nt(
+                jnp.concatenate([grad_scores, probs.astype(jnp.bfloat16)], axis=1), both
+            )
+            total = nn(kv_lines[g, :HD, :span], grad_scores) * HD ** (-0.5)
+            cos_here, sin_here = cos_ref[:, columns], sin_ref[:, columns]
+            back = [
+                turn_back(total[:, h * 128 : (h + 1) * 128], cos_here, sin_here)
+                for h in range(GROUP)
+            ]
+            grad_queries[g, columns] = jnp.transpose(jnp.concatenate(back, axis=0)).astype(
+                jnp.bfloat16
+            )
+
+        by_span(xl, b, run)
+
+    def both_heads(t, carry):
+        block(which(lax.div(t, 2)), lax.rem(t, 2))
+        return carry
+
+    keep.wait()
+    load_out.wait()
+    give(z)
+    lay(2 * z)
+
+    def own_block(g, carry):
+        block(2 * z, g)
+        return carry
+
+    lax.fori_loop(0, 2, own_block, 0)
+    ring = ring_gather_forward(proj_all, ring, ring_send.at[0], ring_recv.at[0])
+    staged[0].wait()
+    feed[0].fold(stages[0])
+    staged[0] = feed[2].stage(stages[0], load_sem.at[4])
+    staged[1].wait()
+    feed[1].fold(stages[1])
+    staged[0].wait()
+    feed[2].fold(stages[0])
+    ring[2].wait_recv()
+    give(zm)
+    ring[3].wait_recv()
+    give(zp)
+    for i in range(1, 4):
+        lay(which(i))
+    lax.fori_loop(2, 8, both_heads, 0)
+    ring[4].wait_recv()
+    ring[5].wait_recv()
+    give(z2)
+    for i in range(4, 7):
+        lay(which(i))
+    for copy in ring:
+        copy.wait_send()
+    out_parts[...] = (
+        tn(proj_all[...].reshape(896, 1536), tokens[...])
+        .astype(jnp.bfloat16)
+        .reshape(2, 4, 2, 2, 48, 384)
+    )
+    out_scatter.begin()
+    load_first = load(first_from, proj_all, 7)
+    load_terms.wait()
+    shrunk = ring_scatter_begin(parts, came_one, ring_send.at[1], ring_recv.at[1])
+
+    def exchange(g):
+        theirs = sums[g, pl.ds(pl.multiple_of((1 - xl) * 896, 128), 896)]
+        outgoing[g] = theirs.astype(jnp.bfloat16)
+        copy = remote(outgoing.at[g], incoming.at[g], kv_send.at[g], kv_recv.at[g], beside)
+        copy.start()
+        return copy
+
+    def far_block(g):
+        def body(i, carry):
+            block(which(i), g)
+            return carry
+
+        lax.fori_loop(4, 7, body, 0)
+
+    far_block(0)
+    kv_copies = [exchange(0)]
+    shrunk = ring_scatter_forward(
+        parts, came_one, ring_sums, shrunk, ring_send.at[1], ring_recv.at[1]
+    )
+    out_scatter.fold()
+    far_block(1)
+    kv_copies.append(exchange(1))
+    for scatter in feed:
+        scatter.line()
+    out_scatter.line()
+    load_in.wait()
+    load_first.wait()
+    ring_scatter_end(parts, came_one, shrunk_total, shrunk)
+    for g in range(HEADS):
+        kv_copies[g].wait()
+        mine = sums[g, pl.ds(pl.multiple_of(xl * 896, 128), 896)] + incoming[g].astype(
+            jnp.float32
+        )
+        mine = mine * key_cos[...] - swap_halves(mine) * key_sin[...]
+        grad_packed[:, g * 320 : g * 320 + 192] = grad_queries[g]
+        grad_packed[:, g * 320 + 192 : g * 320 + 320] = mine.astype(jnp.bfloat16)
+
+    def spread(c):
+        rows = pl.ds(pl.multiple_of(c * 224, 16), 224)
+        parts[c] = nt(grad_packed[rows], w_in[...]).astype(jnp.bfloat16)
+
+    spread(z2)
+    far = ring_scatter_far(parts, came_two, ring_send.at[2], ring_recv.at[2])
+    spread(zp)
+    spread(zm)
+    near = ring_scatter_near(parts, came_two, ring_send.at[2], ring_recv.at[2])
+    in_parts[...] = (
+        tn(proj_all[...].reshape(896, 1536), grad_packed[...])
+        .astype(jnp.bfloat16)
+        .reshape(2, 4, 2, 2, 48, 640)
+    )
+    in_scatter.begin()
+    spread(z)
+    in_scatter.fold()
+    ring = ring_scatter_forward(
+        parts, came_two, ring_sums, far + near, ring_send.at[2], ring_recv.at[2]
+    )
+    for i in range(4):
+        every[i].end(totals[i])
+    in_scatter.line()
+    ring_scatter_end(parts, came_two, first_total, ring)
+    in_scatter.end(totals[4])
+
+
+SCATTER_TURNS = (True, True, False, False, False)
+
+
+def back(own, w_out, w_in, first_all, out_terms, gradients, saved, tables):
+    any_place = pl.BlockSpec(memory_space=pl.ANY)
+    whole = pl.BlockSpec(memory_space=pltpu.VMEM)
+    rows, width = own.shape
+    low, full = jnp.bfloat16, jnp.float32
+    widths = [g.shape[-1] for g in gradients] + [384, 640]
+    rooms = []
+    for w, turn_first in zip(widths, SCATTER_TURNS):
+        rooms += scatter_room(w, turn_first)
+    return pl.pallas_call(
+        back_kernel,
+        out_shape=(jax.ShapeDtypeStruct((rows, width), full),) * 2
+        + tuple(jax.ShapeDtypeStruct((48, w), full) for w in widths),
+        in_specs=[whole] + [any_place] * 7 + [whole] * 11,
+        out_specs=(whole,) * 7,
+        scratch_shapes=[
+            pltpu.VMEM((4, rows, width), low),
+            pltpu.VMEM((1536, 384), low),
+            pltpu.VMEM((1536, 640), low),
+            pltpu.VMEM((896, 384), low),
+            pltpu.VMEM((384, 896), low),
+            pltpu.VMEM((HEADS, 896, 192), low),
+            pltpu.VMEM((896, 640), low),
+            pltpu.VMEM((HEADS, 1792, 128), full),
+            pltpu.VMEM((HEADS, 896, 128), low),
+            pltpu.VMEM((HEADS, 896, 128), low),
+            pltpu.VMEM((4, rows, width), low),
+            pltpu.VMEM((6, rows // 2, width), low),
+            pltpu.VMEM((6, rows // 2, width), low),
+            pltpu.VMEM((2, rows // 2, width), low),
+            pltpu.VMEM((2, 4, 2, 48, 960), low),
+            pltpu.VMEM((2, 4, 2, 48, 960), low),
+            pltpu.VMEM((2, 4, 2, 2, 48, 384), low),
+            pltpu.VMEM((2, 4, 2, 2, 48, 640), low),
+            *rooms,
+            pltpu.SemaphoreType.DMA((3, 6)),
+            pltpu.SemaphoreType.DMA((3, 6)),
+            pltpu.SemaphoreType.DMA((5, 10)),
+            pltpu.SemaphoreType.DMA((5, 10)),
+            pltpu.SemaphoreType.DMA((2,)),
+            pltpu.SemaphoreType.DMA((2,)),
+            pltpu.SemaphoreType.DMA((8,)),
+        ],
+        compiler_params=pltpu.CompilerParams(
+            collective_id=2, has_side_effects=True, vmem_limit_bytes=BACK_VMEM
+        ),
+    )(
+        own,
+        w_out,
+        w_in,
+        first_all,
+        out_terms,
+        *(g.reshape(2, 4, 2, 2, 48, g.shape[-1]) for g in gradients),
+        *saved,
+        *tables,
+    )
+
+
+BACK_VMEM = 63 * 2**20
+
+
 def product(a, b, a_dim, b_dim):
     return lax.dot_general(
         a, b, (((a_dim,), (b_dim,)), ((), ())), preferred_element_type=jnp.float32
@@ -1037,6 +1124,7 @@
     still = jnp.ones((896, HD), jnp.float32)
     key_cos = jnp.concatenate([cos_part.T, cos_part.T, still], axis=1)
     key_sin = jnp.concatenate([-sin_part.T, sin_part.T, 0.0 * still], axis=1)
+    tables = (cos_part, sin_part, key_cos, key_sin, limit)
     (
         first_all,
         shrunk_all,
@@ -1049,6 +1137,7 @@
         kv_rows,
         kv_lines,
         attended,
+        tokens,
         log_total,
         projected,
     ) = front(
@@ -1061,7 +1150,7 @@
             output_weight.T.astype(low),
             shrink_weight.T.astype(low),
         ),
-        (cos_part, sin_part, key_cos, key_sin, limit),
+        tables,
     )
     (
         residual,
@@ -1082,27 +1171,19 @@
         w_up,
         w_shrink,
     )
-    projected_gradient = ring_gather(projected_gradient, 6)
-    grad_attended = product(w_out, projected_gradient, 0, 1).astype(low)
-    grad_packed = attend_backward(
-        turned, kv_rows, kv_lines, attended, log_total, grad_attended, cos_part, sin_part, limit
-    )
-    grad_first = ring_scatter(product(grad_packed, w_in, 0, 1).astype(low), 7)
+    shrunk, grad_first, grad_gate, grad_up, grad_shrink, grad_output, grad_input = back(
+        projected_gradient,
+        w_out,
+        w_in,
+        first_all,
+        out_parts,
+        (grad_gate, grad_up, grad_shrink),
+        (turned, kv_rows, kv_lines, attended, tokens, log_total),
+        tables,
+    )
     gain_one = jnp.sum(grad_first * normed_one, axis=0)
     input_gradient = grad_residual + rms_back(grad_first * norm_gains[0], normed_one, scale_one)
-    shrunk = ring_scatter(out_parts.reshape(896, 1536), 8)
     block_output = (residual + RESID * shrunk).astype(low)
-    grad_gate, grad_up, grad_output, grad_shrink, grad_input = plane_scatter(
-        (
-            grad_gate,
-            grad_up,
-            product(projected_gradient, attended, 0, 1).astype(low),
-            grad_shrink,
-            product(first_all, grad_packed, 0, 1).astype(low),
-        ),
-        (True, True, False, False, False),
-        9,
-    )
     grad_expand = jnp.stack([grad_gate, grad_up])
     grad_output, grad_shrink = grad_output.T, grad_shrink.T
     reduced = (grad_input, grad_output, grad_expand, grad_shrink)

time: 390 us -> 306 us (0.78)
  Pallas kernels: 328 us -> 257 us
  matrix products: 14.5 us -> 0 us
    pallas_call x5 -> x1, Pallas kernels: 160 us -> 89.2 us  [back(): pl.pallas_call(back_kernel, out_shape=(jax.ShapeDtypeStruct((rows, width)...]
    dot_general x4 -> x0, matrix products: 14.5 us -> none  [product(): lax.dot_general(a, b, (((a_dim,), (b_dim,)), ((), ())), preferred_element...]
where the time goes in v4:
time: 306 us; the launch traced here: 301 us
  Pallas kernels  257 us (84%)
  other arithmetic  32.1 us (10%)
  between operations  6.93 us (2%)
  local copies, waits for them, and re-layouts  4.39 us (1%)
    pallas_call x1, Pallas kernels, front(): pl.pallas_call(front_kernel, out_shape=(jax.ShapeDtypeStruct((4, rows, wi...  91.1 us
    pallas_call x1, Pallas kernels, back(): pl.pallas_call(back_kernel, out_shape=(jax.ShapeDtypeStruct((rows, width)...  89.2 us
    pallas_call x1, Pallas kernels, middle(): pl.pallas_call(middle_kernel, out_shape=(jax.ShapeDtypeStruct((rows, widt...  61.9 us
    pallas_call x1, Pallas kernels, sum_everywhere(): pl.pallas_call(sum_kernel, out_shape=jax.ShapeDtypeStruct(own.shape, jnp....  15.1 us
    sub x5, other arithmetic, adamw(): weight - step_rate * (momentum_hat / (jnp.sqrt(variance_hat) + ADAM_EPS)...  7.13 us

profile of v4, /device:TPU:0, one launch (start us, length us, event | category | flops | bytes accessed | tf_op | source)
XLA Modules:
  0.0 300.7 jit_solution(10014465410641357838)
XLA Ops:
  1.5 1.3 fusion.11
  4.2 1.4 fusion.28
  5.6 1.5 convert_bitcast_fusion.1.refs_5_
  7.1 1.5 convert_element_type.42.refs_2_
  8.6 1.6 convert_bitcast_fusion.refs_6_
  10.9 1.2 multiply_sine_fusion.1
  12.1 1.7 fusion.16
  13.8 1.2 maximum_maximum_fusion
  15.2 1.3 fusion.4
  16.5 91.1 %shard_map.322 = (bf16[4,224,1536]{2,1,0:T(8,128)(2,1)}, bf16[4,224,1536]{2,1,0:T(8,128)(2,1)}, bf16[2,4,2,2,48,640]{5,4,3,2,1,0:T(8,128)(2,1)}, bf16[2,4,2,2,48...) custom-call(bf16[224,1536]{1,0:T(8,128)(2,1)} %get-tuple-element.104, ...), custom_call_target="tpu_custom_call" | custom-call | tf_op jit(solution)/shard_map/pallas_call | solution.py:523
  107.6 61.9 %shard_map.323 = (f32[224,1536]{1,0:T(8,128)}, f32[224,1536]{1,0:T(8,128)}, bf16[224,1536]{1,0:T(8,128)(2,1)}, f32[1,1536]{1,0:T(1,128)}, bf16[1536,960]{1,0:T(8...) custom-call(bf16[224,1536]{1,0:T(8,128)(2,1)} %bitcast.47, ...), custom_call_target="tpu_custom_call" | custom-call | tf_op jit(solution)/shard_map/pallas_call | solution.py:664
  169.6 89.2 %shard_map.324 = (f32[224,1536]{1,0:T(8,128)}, f32[224,1536]{1,0:T(8,128)}, f32[48,960]{1,0:T(8,128)}, f32[48,960]{1,0:T(8,128)}, f32[48,960]{1,0:T(8,128)}, /*index=5*/f32[48,384]{1,0:T(8,128)}, f32[48,640]{1,0:T(8,128)}) custom-call(bf16[224,1536]{1,0:T(8,128)(2,1)} %get-tuple-element.53.refs_0_, bf16[1536,384]{1,0:T(8,128)(2,1)} %bitcast.56, ...), custom_call_target="tpu_custom_call" | custom-call | tf_op jit(solution)/shard_map/pallas_call | solution.py:1036
  258.7 1.6 multiply_reduce_fusion.1
  260.3 1.5 multiply_reduce_fusion.3
  261.8 1.5 multiply_reduce_fusion.2
  264.7 3.0 fusion.12
  270.3 1.5 fusion.9
  272.4 15.1 %shard_map.325 = f32[32,128]{1,0:T(8,128)} custom-call(f32[32,128]{1,0:T(8,128)} %concatenate.15.own), custom_call_target="tpu_custom_call" | custom-call | tf_op jit(solution)/shard_map/pallas_call | solution.py:359
  287.5 1.3 multiply_reduce_fusion.4
  288.8 1.2 slice.25
  292.1 1.4 add_subtract_fusion
  293.6 1.8 multiply_subtract_fusion.3
  295.3 1.9 multiply_subtract_fusion.2
  298.2 1.2 multiply_subtract_fusion
  (61 shorter events, 6.0 us)
Async XLA Ops:
  0.7 9.5 %copy-start.4 = (f32[2,48,960]{2,1,0:T(8,128)S(1)}, f32[2,48,960]{2,1,0:T(8,128)}, u32[]{:S(2)}) copy-start(f32[2,48,960]{2,1,0:T(8,128)} %param.32) | copy-start | bytes 1105924
  13.8 1.2 copy-start
  13.8 1.5 copy-start.3
  264.7 3.0 %copy-start.8 = (f32[48,960]{1,0:T(8,128)S(1)}, f32[48,960]{1,0:T(8,128)}, u32[]{:S(2)}) copy-start(f32[48,960]{1,0:T(8,128)} %get-tuple-element.73) | copy-start | bytes 552964
  264.7 3.0 %copy-start.10 = (f32[48,960]{1,0:T(8,128)S(1)}, f32[48,960]{1,0:T(8,128)}, u32[]{:S(2)}) copy-start(f32[48,960]{1,0:T(8,128)} %get-tuple-element.74) | copy-start | bytes 552964
  264.7 5.0 %copy-start.1 = (bf16[1,224,1536]{2,1,0:T(8,128)(2,1)S(1)}, bf16[1,224,1536]{2,1,0:T(8,128)(2,1)}, u32[]{:S(2)}) copy-start(bf16[1,224,1536]{2,1,0:T(8,128)(2,1)} %param.19) | copy-start | bytes 2064388
  264.7 5.0 %copy-start.2 = (f32[224,1536]{1,0:T(8,128)S(1)}, f32[224,1536]{1,0:T(8,128)}, u32[]{:S(2)}) copy-start(f32[224,1536]{1,0:T(8,128)} %get-tuple-element.69) | copy-start | bytes 4128772
  267.7 2.5 copy-start.19
  267.7 2.6 copy-start.6
  270.3 21.9 %copy-start.18 = (f32[2,1536]{1,0:T(2,128)S(1)}, f32[2,1536]{1,0:T(2,128)}, u32[]{:S(2)}) copy-start(f32[2,1536]{1,0:T(2,128)} %param.23) | copy-start | bytes 36868
  270.3 23.2 %copy-start.15 = (f32[384,48]{0,1:T(8,128)S(1)}, f32[384,48]{0,1:T(8,128)}, u32[]{:S(2)}) copy-start(f32[384,48]{0,1:T(8,128)} %param.29) | copy-start | bytes 221188
  271.8 25.5 %copy-start.7 = (f32[960,48]{0,1:T(8,128)S(1)}, f32[960,48]{0,1:T(8,128)}, u32[]{:S(2)}) copy-start(f32[960,48]{0,1:T(8,128)} %param.35) | copy-start | bytes 552964
  271.8 25.5 %copy-start.12 = (f32[48,960]{1,0:T(8,128)S(1)}, f32[48,960]{1,0:T(8,128)}, u32[]{:S(2)}) copy-start(f32[48,960]{1,0:T(8,128)} %get-tuple-element.75) | copy-start | bytes 552964
  271.8 25.5 %copy-start.16 = (f32[960,48]{0,1:T(8,128)S(1)}, f32[960,48]{0,1:T(8,128)}, u32[]{:S(2)}) copy-start(f32[960,48]{0,1:T(8,128)} %param.37) | copy-start | bytes 552964
  271.8 25.5 %copy-start.17 = (f32[960,48]{0,1:T(8,128)S(1)}, f32[960,48]{0,1:T(8,128)}, u32[]{:S(2)}) copy-start(f32[960,48]{0,1:T(8,128)} %param.36) | copy-start | bytes 552964
  293.5 4.6 %copy-start.5 = (f32[2,48,960]{2,1,0:T(8,128)S(1)}, f32[2,48,960]{2,1,0:T(8,128)}, u32[]{:S(2)}) copy-start(f32[2,48,960]{2,1,0:T(8,128)} %param.32) | copy-start | bytes 1105924
  293.5 4.6 %copy-start.9 = (f32[48,960]{1,0:T(8,128)S(1)}, f32[48,960]{1,0:T(8,128)}, u32[]{:S(2)}) copy-start(f32[48,960]{1,0:T(8,128)} %get-tuple-element.73) | copy-start | bytes 552964
  293.5 4.6 %copy-start.11 = (f32[48,960]{1,0:T(8,128)S(1)}, f32[48,960]{1,0:T(8,128)}, u32[]{:S(2)}) copy-start(f32[48,960]{1,0:T(8,128)} %get-tuple-element.74) | copy-start | bytes 552964
  293.5 4.6 %copy-start.13 = (f32[2,48,960]{2,1,0:T(8,128)S(1)}, f32[2,48,960]{2,1,0:T(8,128)}, u32[]{:S(2)}) copy-start(f32[2,48,960]{2,1,0:T(8,128)} %param.34) | copy-start | bytes 1105924
  293.5 4.6 %copy-start.14 = (f32[2,48,960]{2,1,0:T(8,128)S(1)}, f32[2,48,960]{2,1,0:T(8,128)}, u32[]{:S(2)}) copy-start(f32[2,48,960]{2,1,0:T(8,128)} %param.33) | copy-start | bytes 1105924

commit v5 on v4

--- a/solution.py
+++ b/solution.py
@@ -37,15 +37,6 @@
     return (jnp.cos(phase_turn), jnp.sin(phase_turn))
 
 
-def rms_parts(values):
-    scaling = lax.rsqrt(jnp.mean(values * values, axis=-1, keepdims=True) + EPS)
-    return (values * scaling, scaling)
-
-
-def rms_back(gradient, normed, scaling):
-    return scaling * (gradient - normed * jnp.mean(gradient * normed, axis=-1, keepdims=True))
-
-
 def adamw(weight, gradient, momentum, variance, step_rate, decay_rate):
     momentum_new = BETA_ONE * momentum + (1.0 - BETA_ONE) * gradient
     variance_new = BETA_TWO * variance + (1.0 - BETA_TWO) * gradient * gradient
@@ -80,11 +71,14 @@
     return {"shard": (xh * 4 + y) * 2 + core, "context": xl, "tensor": z}
 
 
-def greet(peers):
+def hail(peers):
     barrier = pltpu.get_barrier_semaphore()
     for peer in peers:
         pl.semaphore_signal(barrier, inc=1, device_id=peer, device_id_type=MESH)
-    pl.semaphore_wait(barrier, len(peers))
+
+
+def meet(peers):
+    pl.semaphore_wait(pltpu.get_barrier_semaphore(), len(peers))
 
 
 def remote(src, dst, send_sem, recv_sem, peer):
@@ -123,6 +117,24 @@
     @pl.when(jnp.logical_not(near))
     def _():
         run(1792)
+
+
+def limits(prefix, xl, b):
+    lane = lax.broadcasted_iota(jnp.int32, (1, GROUP * 128), 1)
+    row = xl * 896 + b * 128 + lax.rem(lane, 128)
+    return jnp.maximum(row + 1, prefix[0])
+
+
+def key_tables(cos_ref, sin_ref, key_cos, key_sin):
+    cos_part, sin_part = jnp.transpose(cos_ref[...]), jnp.transpose(sin_ref[...])
+    still = jnp.ones((896, HD), jnp.float32)
+    key_cos[...] = jnp.concatenate([cos_part, cos_part, still], axis=1)
+    key_sin[...] = jnp.concatenate([-sin_part, sin_part, 0.0 * still], axis=1)
+
+
+def arrival(z, i):
+    shifted = i - 3 + (3 - z) // 3
+    return lax.rem(2 * z + shifted + (shifted + 7) // 7 + 7, 7)
 
 
 def ring_peers():
@@ -326,50 +338,6 @@
             copy.wait_send()
 
 
-def sum_kernel(own, total, held, send_sem, recv_sem):
-    xh, y, core, xl, z = place()
-    ys, xs, y_peers, x_peers, other = plane()
-    z_peers = [device(xh, y, core, xl, lax.rem(z + d, 4)) for d in (1, 3, 2)]
-    greet([other] + z_peers + x_peers + y_peers)
-    total[...] = own[...]
-    groups = ((z_peers, z, 4), (x_peers, xh * 2 + xl, 4), (y_peers, y, 4), ([other], core, 2))
-    for axis, (group, here, count) in enumerate(groups):
-        held[axis, here] = total[...]
-        copies = [
-            remote(
-                held.at[axis, here],
-                held.at[axis, here],
-                send_sem.at[axis * 3 + k],
-                recv_sem.at[axis * 3 + k],
-                peer,
-            )
-            for k, peer in enumerate(group)
-        ]
-        for copy in copies:
-            copy.start()
-        for copy in copies:
-            copy.wait()
-        order = held[axis, 0]
-        for k in range(1, count):
-            order = order + held[axis, k]
-        total[...] = order
-
-
-def sum_everywhere(own, identity):
-    return pl.pallas_call(
-        sum_kernel,
-        out_shape=jax.ShapeDtypeStruct(own.shape, jnp.float32),
-        scratch_shapes=[
-            pltpu.VMEM((4, 4) + own.shape, jnp.float32),
-            pltpu.SemaphoreType.DMA((12,)),
-            pltpu.SemaphoreType.DMA((12,)),
-        ],
-        compiler_params=pltpu.CompilerParams(
-            collective_id=identity, has_side_effects=True, vmem_limit_bytes=VMEM_MOST
-        ),
-    )(own)
-
-
 def swap_halves(block):
     lane = lax.broadcasted_iota(jnp.int32, block.shape, 1)
     return jnp.where(
@@ -378,19 +346,30 @@
 
 
 def front_kernel(*refs):
-    (first, shrunk, w_in, w_gate, w_up, w_out, w_shrink) = refs[:7]
-    (cos_ref, sin_ref, key_cos, key_sin, limit) = refs[7:12]
-    (first_all, shrunk_all, in_all, gate_all, up_all, out_all, shrink_all) = refs[12:19]
-    (turned, kv_rows, kv_lines, attended, tokens, log_total, total) = refs[19:26]
-    (packed, held_rows, parts, came, sums) = refs[26:31]
-    (ring_send, ring_recv, plane_send, plane_recv) = refs[31:35]
-    (kv_send, kv_recv, own_sem, out_sem) = refs[35:]
+    (hidden, cotangent, gain, m_in, m_expand, m_out, m_shrink) = refs[:7]
+    (cos_ref, sin_ref, prefix) = refs[7:10]
+    (first_to, shrunk_all, in_to, gate_all, up_all, out_all, shrink_all) = refs[10:17]
+    (turned_to, rows_to, lines_to, attended, tokens, log_total, total) = refs[17:24]
+    (first_all, shrunk, in_all, w_gate, w_up, w_out, w_shrink) = refs[24:31]
+    (turned, kv_rows, kv_lines, key_cos, key_sin) = refs[31:36]
+    (packed, held_rows, parts, came, sums) = refs[36:41]
+    (ring_send, ring_recv, plane_send, plane_recv) = refs[41:45]
+    (kv_send, kv_recv, own_sem, out_sem) = refs[45:]
     xh, y, core, xl, z = place()
     z, zp, z2, zm, up, down = ring_peers()
     ys, xs, y_peers, x_peers, other = plane()
     beside = device(xh, y, core, 1 - xl, z)
-    greet([up, down, other] + y_peers + x_peers)
-    owns = (w_in, w_out, w_gate, w_up, w_shrink)
+    peers = [up, down, other] + y_peers + x_peers
+    hail(peers)
+    low = jnp.bfloat16
+    in_own = in_all.at[xh, y, core, xl]
+    in_own[...] = m_in[...].astype(low)
+    w_out[...] = m_out[...].astype(low)
+    rows = hidden[...].astype(jnp.float32)
+    scaling = lax.rsqrt(jnp.mean(rows * rows, axis=-1, keepdims=True) + EPS)
+    first_all[z] = (rows * scaling * gain[...]).astype(low)
+    meet(peers)
+    owns = (in_own, w_out, w_gate, w_up, w_shrink)
     helds = (in_all, out_all, gate_all, up_all, shrink_all)
     gathers = [
         PlaneGather(own, held, i in (2, 3), plane_send.at[i], plane_recv.at[i])
@@ -398,19 +377,23 @@
     ]
     for gather in gathers[:2]:
         gather.begin()
-    ring = ring_gather_begin(first, first_all, ring_send.at[0], ring_recv.at[0])
+    ring = ring_gather_begin(first_all.at[z], first_all, ring_send.at[0], ring_recv.at[0])
+    w_gate[...] = m_expand[0].astype(low)
+    w_up[...] = m_expand[1].astype(low)
+    w_shrink[...] = m_shrink[...].astype(low)
+    shrunk[...] = (RESID * cotangent[...].astype(jnp.float32)).astype(low)
     keeps = [
         pltpu.make_async_copy(own, held.at[xh, y, core, xl], own_sem.at[i])
-        for i, (own, held) in enumerate(zip(owns, helds))
+        for i, (own, held) in enumerate(zip(owns[1:], helds[1:]))
     ]
-    keeps.append(pltpu.make_async_copy(first, first_all.at[z], own_sem.at[5]))
-    keeps.append(pltpu.make_async_copy(shrunk, shrunk_all.at[z], own_sem.at[6]))
+    keeps.append(pltpu.make_async_copy(shrunk, shrunk_all.at[z], own_sem.at[4]))
     for keep in keeps:
         keep.start()
     for keep in keeps:
         keep.wait()
     for gather in gathers[:2]:
         gather.spread()
+    key_tables(cos_ref, sin_ref, key_cos, key_sin)
     ring = ring_gather_forward(first_all, ring, ring_send.at[0], ring_recv.at[0])
     gathers[0].share()
     gathers[1].share()
@@ -426,7 +409,7 @@
             mine = pl.ds(pl.multiple_of(xl * 896 + c * 224, 16), 224)
             kv_rows[g, mine] = (
                 block * key_cos[rows] + swap_halves(block) * key_sin[rows]
-            ).astype(jnp.bfloat16)
+            ).astype(low)
 
     kv_copies = []
     for i, c in enumerate((z, zm, zp, z2)):
@@ -442,6 +425,14 @@
         kv_copies.append(remote(mine, mine, kv_send.at[i], kv_recv.at[i], beside))
         kv_copies[-1].start()
     later = ring_gather_begin(shrunk, shrunk_all, ring_send.at[1], ring_recv.at[1])
+    saves = []
+
+    def save(src, dst):
+        saves.append(pltpu.make_async_copy(src, dst, own_sem.at[5 + len(saves)]))
+        saves[-1].start()
+
+    save(first_all, first_to)
+    save(in_all, in_to)
 
     def turn_block(b, carry):
         columns = pl.ds(pl.multiple_of(b * 128, 128), 128)
@@ -452,19 +443,21 @@
                 at = (g * 5 + h) * HD
                 turned[(g * GROUP + h) * HD : (g * GROUP + h + 1) * HD, columns] = (
                     turn(lines[at : at + HD], cos_here, sin_here) * HD ** (-0.5)
-                ).astype(jnp.bfloat16)
+                ).astype(low)
         return carry
 
     lax.fori_loop(0, BLOCKS, turn_block, 0)
+    save(turned, turned_to)
     for copy in kv_copies:
         copy.wait_recv()
     for gather in gathers[2:]:
         gather.spread()
     for g in range(HEADS):
-        kv_lines[g] = jnp.transpose(kv_rows[g].astype(jnp.float32)).astype(jnp.bfloat16)
-
-    def block(t, carry):
-        b, g = t // HEADS, lax.rem(t, HEADS)
+        kv_lines[g] = jnp.transpose(kv_rows[g].astype(jnp.float32)).astype(low)
+    save(kv_rows, rows_to)
+    save(kv_lines, lines_to)
+
+    def block(b, g):
         columns = pl.ds(pl.multiple_of(b * 128, 128), 128)
 
         def run(span):
@@ -475,34 +468,55 @@
             queries = jnp.concatenate([queries, jnp.zeros_like(queries)], axis=0)
             scores = nn(kv_rows[g, :span], queries)
             key_index = lax.broadcasted_iota(jnp.int32, (span, 384), 0)
-            scores = jnp.where(key_index < limit[b], scores, NEG)
+            scores = jnp.where(key_index < limits(prefix, xl, b), scores, NEG)
             row_max = jnp.max(scores, axis=0, keepdims=True)
             shifted = jnp.exp(scores - row_max)
             exp_total = jnp.sum(shifted, axis=0, keepdims=True)
-            out = nn(kv_lines[g, HD:, :span], shifted.astype(jnp.bfloat16)) * (1.0 / exp_total)
+            out = nn(kv_lines[g, HD:, :span], shifted.astype(low)) * (1.0 / exp_total)
             for h in range(GROUP):
-                attended[head_rows[h], columns] = out[:, h * 128 : (h + 1) * 128].astype(
-                    jnp.bfloat16
-                )
-            log_total[t] = row_max + jnp.log(exp_total)
+                attended[head_rows[h], columns] = out[:, h * 128 : (h + 1) * 128].astype(low)
+            log_total[b * HEADS + g] = row_max + jnp.log(exp_total)
 
         by_span(xl, b, run)
+
+    def both_heads(t, carry):
+        block(arrival(z, lax.div(t, 2)), lax.rem(t, 2))
         return carry
 
-    lax.fori_loop(0, 6, block, 0)
+    def own_block(g, carry):
+        block(2 * z, g)
+        return carry
+
+    def lay(b):
+        columns = pl.ds(pl.multiple_of(b * 128, 128), 128)
+        tokens[columns] = jnp.transpose(attended[:, columns].astype(jnp.float32)).astype(low)
+
+    def apply(c):
+        mine = pl.ds(pl.multiple_of(c * 224, 16), 224)
+        parts[c] = nt(tokens[mine], held_rows[...].reshape(1536, 384)).astype(low)
+
+    lax.fori_loop(8, 14, both_heads, 0)
     later = ring_gather_forward(shrunk_all, later, ring_send.at[1], ring_recv.at[1])
-    lax.fori_loop(6, HEADS * BLOCKS, block, 0)
     gathers[1].end()
     fetch = pltpu.make_async_copy(out_all, held_rows, out_sem)
     fetch.start()
-    tokens[...] = jnp.transpose(attended[...].astype(jnp.float32)).astype(jnp.bfloat16)
+    for i in range(4, 7):
+        lay(arrival(z, i))
     fetch.wait()
-    for c in range(4):
-        parts[c] = nt(tokens[c * 224 : (c + 1) * 224], held_rows[...].reshape(1536, 384)).astype(jnp.bfloat16)
-    scatter = ring_scatter_begin(parts, came, ring_send.at[2], ring_recv.at[2])
+    apply(z2)
+    far = ring_scatter_far(parts, came, ring_send.at[2], ring_recv.at[2])
+    lax.fori_loop(2, 8, both_heads, 0)
+    for i in range(1, 4):
+        lay(arrival(z, i))
+    apply(zp)
+    apply(zm)
+    near = ring_scatter_near(parts, came, ring_send.at[2], ring_recv.at[2])
     scatter = ring_scatter_forward(
-        parts, came, sums, scatter, ring_send.at[2], ring_recv.at[2]
-    )
+        parts, came, sums, far + near, ring_send.at[2], ring_recv.at[2]
+    )
+    lax.fori_loop(0, 2, own_block, 0)
+    lay(2 * z)
+    apply(z)
     for gather in gathers[2:]:
         gather.share()
     for gather in gathers[2:]:
@@ -510,57 +524,64 @@
     ring_gather_end(later)
     for copy in kv_copies + ring:
         copy.wait_send()
+    for copy in saves:
+        copy.wait()
     ring_scatter_end(parts, came, total, scatter)
 
 
-def front(first, shrunk, weights, tables):
+def front(hidden, cotangent, gain, weights, tables, prefix):
     any_place = pl.BlockSpec(memory_space=pl.ANY)
     whole = pl.BlockSpec(memory_space=pltpu.VMEM)
-    rows, width = first.shape
-    gathered = [
-        jax.ShapeDtypeStruct((2, 4, 2, 2) + w.shape, jnp.bfloat16) for w in weights
-    ]
+    rows, width = hidden.shape
+    low, full = jnp.bfloat16, jnp.float32
+    block = (2, 4, 2, 2, 48)
+    first_shape, in_shape = (4, rows, width), block + (640,)
+    turned_shape, rows_shape, lines_shape = (384, 896), (HEADS, 1792, 128), (HEADS, 128, 1792)
+    kept = (first_shape, (4, rows, width), in_shape) + (block + (960,),) * 2
+    kept += (block + (384,), block + (960,), turned_shape, rows_shape, lines_shape)
     outs = pl.pallas_call(
         front_kernel,
         out_shape=(
-            jax.ShapeDtypeStruct((4, rows, width), jnp.bfloat16),
-            jax.ShapeDtypeStruct((4, rows, width), jnp.bfloat16),
-            *gathered,
-            jax.ShapeDtypeStruct((384, 896), jnp.bfloat16),
-            jax.ShapeDtypeStruct((HEADS, 1792, 128), jnp.bfloat16),
-            jax.ShapeDtypeStruct((HEADS, 128, 1792), jnp.bfloat16),
-            jax.ShapeDtypeStruct((384, 896), jnp.bfloat16),
-            jax.ShapeDtypeStruct((896, 384), jnp.bfloat16),
-            jax.ShapeDtypeStruct((HEADS * BLOCKS, 1, 384), jnp.float32),
-            jax.ShapeDtypeStruct((rows, width), jnp.float32),
+            *(jax.ShapeDtypeStruct(shape, low) for shape in kept),
+            jax.ShapeDtypeStruct((384, 896), low),
+            jax.ShapeDtypeStruct((896, 384), low),
+            jax.ShapeDtypeStruct((HEADS * BLOCKS, 1, 384), full),
+            jax.ShapeDtypeStruct((rows, width), full),
         ),
-        in_specs=[whole] * 12,
-        out_specs=(whole, any_place, whole) + (any_place,) * 4 + (whole,) * 7,
+        in_specs=[whole] * 9 + [pl.BlockSpec(memory_space=pltpu.SMEM)],
+        out_specs=(any_place,) * 10 + (whole,) * 4,
         scratch_shapes=[
-            pltpu.VMEM((896, 640), jnp.float32),
-            pltpu.VMEM((2, 4, 2, 2, 48, 384), jnp.bfloat16),
-            pltpu.VMEM((4, rows, width), jnp.bfloat16),
-            pltpu.VMEM((6, rows // 2, width), jnp.bfloat16),
-            pltpu.VMEM((2, rows // 2, width), jnp.bfloat16),
+            pltpu.VMEM(first_shape, low),
+            pltpu.VMEM((rows, width), low),
+            pltpu.VMEM(in_shape, low),
+            pltpu.VMEM((48, 960), low),
+            pltpu.VMEM((48, 960), low),
+            pltpu.VMEM((48, 384), low),
+            pltpu.VMEM((48, 960), low),
+            pltpu.VMEM(turned_shape, low),
+            pltpu.VMEM(rows_shape, low),
+            pltpu.VMEM(lines_shape, low),
+            pltpu.VMEM((896, 128), full),
+            pltpu.VMEM((896, 128), full),
+            pltpu.VMEM((896, 640), full),
+            pltpu.VMEM(block + (384,), low),
+            pltpu.VMEM((4, rows, width), low),
+            pltpu.VMEM((6, rows // 2, width), low),
+            pltpu.VMEM((2, rows // 2, width), low),
             pltpu.SemaphoreType.DMA((3, 6)),
             pltpu.SemaphoreType.DMA((3, 6)),
             pltpu.SemaphoreType.DMA((5, 10)),
             pltpu.SemaphoreType.DMA((5, 10)),
             pltpu.SemaphoreType.DMA((4,)),
             pltpu.SemaphoreType.DMA((4,)),
-            pltpu.SemaphoreType.DMA((7,)),
+            pltpu.SemaphoreType.DMA((10,)),
             pltpu.SemaphoreType.DMA,
         ],
         compiler_params=pltpu.CompilerParams(
             collective_id=0, has_side_effects=True, vmem_limit_bytes=VMEM_MOST
         ),
-    )(first, shrunk, *weights, *tables)
-    return (
-        outs[0],
-        outs[1],
-        *(held.reshape(1536, -1) for held in outs[2:7]),
-        *outs[7:],
-    )
+    )(hidden, cotangent, gain, *weights, *tables, prefix)
+    return outs[:2] + tuple(held.reshape(1536, -1) for held in outs[2:7]) + outs[7:]
 
 
 def tn(a, b):
@@ -571,13 +592,14 @@
     (hidden, cotangent, projected, gain) = refs[:4]
     (shrunk_from, gate_from, up_from, shrink_from) = refs[4:8]
     (residual, grad_residual, turned_back, gain_two) = refs[8:12]
-    (grad_gate, grad_up, grad_shrink, out_parts) = refs[12:16]
+    (gate_to, up_to, shrink_to, out_to) = refs[12:16]
     (shrunk_all, w_gate, w_up, w_shrink) = refs[16:20]
     (second_all, activated_back, gated, gate_back, up_back) = refs[20:25]
     (parts, came, sums, total) = refs[25:29]
-    (ring_send, ring_recv, load_sem) = refs[29:]
+    (grad_gate, grad_up, grad_shrink, out_parts) = refs[29:33]
+    (ring_send, ring_recv, load_sem) = refs[33:]
     z, zp, z2, zm, up, down = ring_peers()
-    greet([up, down])
+    hail([up, down])
     loads = [
         pltpu.make_async_copy(src, dst, load_sem.at[i])
         for i, (src, dst) in enumerate(
@@ -595,6 +617,7 @@
     residual[...] = rows
     scaling = lax.rsqrt(jnp.mean(rows * rows, axis=-1, keepdims=True) + EPS)
     second_all[z] = (rows * scaling * gain[...]).astype(jnp.bfloat16)
+    meet([up, down])
     ring = ring_gather_begin(second_all.at[z], second_all, ring_send.at[0], ring_recv.at[0])
     loads[0].wait()
     loads[1].wait()
@@ -630,16 +653,26 @@
     feed(z2)
     far = ring_scatter_far(parts, came, ring_send.at[1], ring_recv.at[1])
     second_rows = second_all[...].reshape(896, 1536)
+    saves = []
+
+    def save(src, dst):
+        saves.append(pltpu.make_async_copy(src, dst, load_sem.at[4 + len(saves)]))
+        saves[-1].start()
+
     grad_gate[...] = tn(second_rows, gate_back[...].reshape(896, 960)).astype(jnp.bfloat16)
+    save(grad_gate, gate_to)
     scatter = ring_scatter_forward(
         parts, came, sums, far + near, ring_send.at[1], ring_recv.at[1]
     )
     grad_up[...] = tn(second_rows, up_back[...].reshape(896, 960)).astype(jnp.bfloat16)
+    save(grad_up, up_to)
     grad_shrink[...] = tn(
         shrunk_all[...].reshape(896, 1536), gated[...].reshape(896, 960)
     ).astype(jnp.bfloat16)
+    save(grad_shrink, shrink_to)
     for c in range(4):
         out_parts[c] = nt(gated[c], w_shrink[...]).astype(jnp.bfloat16)
+    save(out_parts, out_to)
     for copy in ring:
         copy.wait_send()
     ring_scatter_end(parts, came, total, scatter)
@@ -654,6 +687,8 @@
     )
     grad_residual[...] = back
     turned_back[...] = (RESID * back).astype(jnp.bfloat16)
+    for copy in saves:
+        copy.wait()
 
 
 def middle(hidden, cotangent, projected, gain, shrunk_all, w_gate, w_up, w_shrink):
@@ -674,7 +709,7 @@
             jax.ShapeDtypeStruct((4, rows, width), low),
         ),
         in_specs=[whole] * 4 + [any_place] * 4,
-        out_specs=(whole,) * 8,
+        out_specs=(whole,) * 4 + (any_place,) * 4,
         scratch_shapes=[
             pltpu.VMEM((4, rows, width), low),
             pltpu.VMEM((1536, 960), low),
@@ -689,9 +724,13 @@
             pltpu.VMEM((6, rows // 2, width), low),
             pltpu.VMEM((2, rows // 2, width), low),
             pltpu.VMEM((rows, width), full),
+            pltpu.VMEM((1536, 960), low),
+            pltpu.VMEM((1536, 960), low),
+            pltpu.VMEM((1536, 960), low),
+            pltpu.VMEM((4, rows, width), low),
             pltpu.SemaphoreType.DMA((2, 6)),
             pltpu.SemaphoreType.DMA((2, 6)),
-            pltpu.SemaphoreType.DMA((4,)),
+            pltpu.SemaphoreType.DMA((8,)),
         ],
         compiler_params=pltpu.CompilerParams(
             collective_id=4, has_side_effects=True, vmem_limit_bytes=VMEM_MOST
@@ -814,19 +853,24 @@
     (own, out_from, in_from, first_from, out_terms) = refs[:5]
     gradients = refs[5:8]
     (turned, kv_rows, kv_lines, attended, tokens, log_total) = refs[8:14]
-    (cos_ref, sin_ref, key_cos, key_sin, limit) = refs[14:19]
-    (shrunk_total, first_total) = refs[19:21]
-    totals = refs[21:26]
-    (proj_all, w_out, w_in, grad_tokens, grad_lines, grad_queries, grad_packed) = refs[26:33]
-    (sums, outgoing, incoming, parts, came_one, came_two, ring_sums) = refs[33:40]
-    stages, out_parts, in_parts = refs[40:42], refs[42], refs[43]
-    rooms = refs[44:64]
+    (cos_ref, sin_ref, prefix) = refs[14:17]
+    (shrunk_total, first_total) = refs[17:19]
+    totals = refs[19:24]
+    (proj_all, w_out, w_in, grad_tokens, grad_lines, grad_queries, grad_packed) = refs[24:31]
+    (sums, outgoing, incoming, parts, came_one, came_two, ring_sums) = refs[31:38]
+    stages, out_parts, in_parts = refs[38:40], refs[40], refs[41]
+    rooms = refs[42:62]
+    (key_cos, key_sin) = refs[62:64]
     (ring_send, ring_recv, plane_send, plane_recv, kv_send, kv_recv, load_sem) = refs[64:]
     xh, y, core, xl, z = place()
     z, zp, z2, zm, up, down = ring_peers()
     ys, xs, y_peers, x_peers, other = plane()
     beside = device(xh, y, core, 1 - xl, z)
-    greet([up, down, other] + y_peers + x_peers)
+    peers = [up, down, other] + y_peers + x_peers
+    hail(peers)
+    sums[...] = jnp.zeros_like(sums)
+    key_tables(cos_ref, sin_ref, key_cos, key_sin)
+    meet(peers)
     ring = ring_gather_begin(own, proj_all, ring_send.at[0], ring_recv.at[0])
     every = [
         Scatter(
@@ -852,15 +896,10 @@
     staged = [feed[i].stage(stages[i], load_sem.at[2 + i]) for i in range(2)]
     load_terms = load(out_terms, parts, 5)
     load_in = load(in_from, w_in, 6)
-    sums[...] = jnp.zeros_like(sums)
 
     def give(c):
         rows = pl.ds(pl.multiple_of(c * 224, 16), 224)
         grad_tokens[rows] = nn(proj_all[c], w_out[...]).astype(jnp.bfloat16)
-
-    def which(i):
-        shifted = i - 3 + (3 - z) // 3
-        return lax.rem(2 * z + shifted + (shifted + 7) // 7 + 7, 7)
 
     def lay(b):
         columns = pl.ds(pl.multiple_of(b * 128, 128), 128)
@@ -892,7 +931,7 @@
             products = nn(kv_rows[g, :span], both)
             key_index = lax.broadcasted_iota(jnp.int32, (span, 384), 0)
             probs = jnp.exp(
-                jnp.where(key_index < limit[b], products[:, :384], NEG)
+                jnp.where(key_index < limits(prefix, xl, b), products[:, :384], NEG)
                 - log_total[b * HEADS + g]
             )
             grad_scores = (probs * (products[:, 384:] - inner)).astype(jnp.bfloat16)
@@ -912,7 +951,7 @@
         by_span(xl, b, run)
 
     def both_heads(t, carry):
-        block(which(lax.div(t, 2)), lax.rem(t, 2))
+        block(arrival(z, lax.div(t, 2)), lax.rem(t, 2))
         return carry
 
     keep.wait()
@@ -938,13 +977,13 @@
     ring[3].wait_recv()
     give(zp)
     for i in range(1, 4):
-        lay(which(i))
+        lay(arrival(z, i))
     lax.fori_loop(2, 8, both_heads, 0)
     ring[4].wait_recv()
     ring[5].wait_recv()
     give(z2)
     for i in range(4, 7):
-        lay(which(i))
+        lay(arrival(z, i))
     for copy in ring:
         copy.wait_send()
     out_parts[...] = (
@@ -966,7 +1005,7 @@
 
     def far_block(g):
         def body(i, carry):
-            block(which(i), g)
+            block(arrival(z, i), g)
             return carry
 
         lax.fori_loop(4, 7, body, 0)
@@ -1024,7 +1063,7 @@
 SCATTER_TURNS = (True, True, False, False, False)
 
 
-def back(own, w_out, w_in, first_all, out_terms, gradients, saved, tables):
+def back(own, w_out, w_in, first_all, out_terms, gradients, saved, tables, prefix):
     any_place = pl.BlockSpec(memory_space=pl.ANY)
     whole = pl.BlockSpec(memory_space=pltpu.VMEM)
     rows, width = own.shape
@@ -1037,7 +1076,10 @@
         back_kernel,
         out_shape=(jax.ShapeDtypeStruct((rows, width), full),) * 2
         + tuple(jax.ShapeDtypeStruct((48, w), full) for w in widths),
-        in_specs=[whole] + [any_place] * 7 + [whole] * 11,
+        in_specs=[whole]
+        + [any_place] * 7
+        + [whole] * 8
+        + [pl.BlockSpec(memory_space=pltpu.SMEM)],
         out_specs=(whole,) * 7,
         scratch_shapes=[
             pltpu.VMEM((4, rows, width), low),
@@ -1059,6 +1101,8 @@
             pltpu.VMEM((2, 4, 2, 2, 48, 384), low),
             pltpu.VMEM((2, 4, 2, 2, 48, 640), low),
             *rooms,
+            pltpu.VMEM((896, 128), full),
+            pltpu.VMEM((896, 128), full),
             pltpu.SemaphoreType.DMA((3, 6)),
             pltpu.SemaphoreType.DMA((3, 6)),
             pltpu.SemaphoreType.DMA((5, 10)),
@@ -1079,16 +1123,131 @@
         *(g.reshape(2, 4, 2, 2, 48, g.shape[-1]) for g in gradients),
         *saved,
         *tables,
+        prefix,
     )
 
 
 BACK_VMEM = 63 * 2**20
 
 
-def product(a, b, a_dim, b_dim):
-    return lax.dot_general(
-        a, b, (((a_dim,), (b_dim,)), ((), ())), preferred_element_type=jnp.float32
-    )
+def finish_kernel(*refs):
+    (grad_first, hidden, grad_residual, gain_two) = refs[:4]
+    (gains, gains_first, gains_second) = refs[4:7]
+    (grad_gate, grad_up, grad_shrink, grad_output, grad_input) = refs[7:12]
+    masters = [refs[12 + 3 * i : 15 + 3 * i] for i in range(4)]
+    (input_gradient, norm_ref) = refs[24:26]
+    gains_new = refs[26:29]
+    news = [refs[29 + 3 * i : 32 + 3 * i] for i in range(4)]
+    own, held, sems_out, sems_in = refs[41:]
+    xh, y, core, xl, z = place()
+    ys, xs, y_peers, x_peers, other = plane()
+    groups = (
+        (
+            [
+                device(xh, y, c, xl, lax.rem(z + d, 4))
+                for d, c in ((1, core), (3, core), (0, 1 - core), (2, core))
+                + ((1, 1 - core), (3, 1 - core), (2, 1 - core))
+            ],
+            z * 2 + core,
+            8,
+        ),
+        (x_peers, xh * 2 + xl, 4),
+        (y_peers, y, 4),
+    )
+    peers = [peer for group in groups for peer in group[0]]
+    hail(peers)
+    rows = hidden[...].astype(jnp.float32)
+    scaling = lax.rsqrt(jnp.mean(rows * rows, axis=-1, keepdims=True) + EPS)
+    normed = rows * scaling
+    gradient = grad_first[...]
+    gain_one = jnp.sum(gradient * normed, axis=0, keepdims=True)
+    squares = jnp.zeros((1, 1), jnp.float32)
+    for terms in (grad_gate, grad_up, grad_shrink, grad_output, grad_input):
+        held_terms = terms[...]
+        squares = squares + jnp.sum(
+            jnp.sum(held_terms * held_terms, axis=0, keepdims=True), axis=1, keepdims=True
+        )
+    for k in range(3):
+        own[k : k + 1] = gain_one[:, k * 512 : (k + 1) * 512]
+        own[3 + k : 4 + k] = gain_two[:, k * 512 : (k + 1) * 512]
+    own[6:8] = jnp.broadcast_to(squares, (2, 512))
+    meet(peers)
+    used = 0
+    for axis, (group, here, count) in enumerate(groups):
+        held[axis, here] = own[...]
+        spot = held.at[axis, here]
+        copies = []
+        for peer in group:
+            copies.append(remote(spot, spot, sems_out.at[used], sems_in.at[used], peer))
+            copies[-1].start()
+            used += 1
+        if axis == 0:
+            gradient = gradient * gains[0:1]
+            input_gradient[...] = grad_residual[...] + scaling * (
+                gradient - normed * jnp.mean(gradient * normed, axis=-1, keepdims=True)
+            )
+        for copy in copies:
+            copy.wait()
+        order = held[axis, 0]
+        for k in range(1, count):
+            order = order + held[axis, k]
+        own[...] = order
+    grad_gains = jnp.concatenate(
+        [
+            jnp.concatenate([own[3 * r + k : 3 * r + k + 1] for k in range(3)], axis=1)
+            for r in range(2)
+        ],
+        axis=0,
+    )
+    gain_squares = jnp.sum(
+        jnp.sum(grad_gains * grad_gains, axis=0, keepdims=True), axis=1, keepdims=True
+    )
+    gradient_norm = jnp.sqrt(own[6:7, 0:1] + gain_squares)
+    norm_ref[...] = gradient_norm
+    factor = jnp.minimum(1.0, MAX_NORM / (gradient_norm + 1e-06))
+
+    def put(targets, results):
+        for target, result in zip(targets, results):
+            target[...] = result
+
+    put(
+        gains_new,
+        adamw(
+            gains[...], factor * grad_gains, gains_first[...], gains_second[...], GAIN_RATE, 0.0
+        ),
+    )
+    for i, terms in ((0, grad_input), (1, grad_output), (3, grad_shrink)):
+        weight, first, second = masters[i]
+        put(news[i], adamw(weight[...], factor * terms[...], first[...], second[...], RATE, DECAY))
+    for k, terms in enumerate((grad_gate, grad_up)):
+        weight, first, second = masters[2]
+        results = adamw(weight[k], factor * terms[...], first[k], second[k], RATE, DECAY)
+        for target, result in zip(news[2], results):
+            target[k] = result
+
+
+def finish(grad_first, hidden, grad_residual, gain_two, gains, gradients, masters):
+    rows, width = hidden.shape
+    full = jnp.float32
+    flat = [array for group in masters for array in group]
+    return pl.pallas_call(
+        finish_kernel,
+        out_shape=(
+            jax.ShapeDtypeStruct((rows, width), full),
+            jax.ShapeDtypeStruct((1, 1), full),
+            *(jax.ShapeDtypeStruct((2, width), full) for _ in range(3)),
+            *(jax.ShapeDtypeStruct(array.shape, full) for array in flat),
+        ),
+        scratch_shapes=[
+            pltpu.VMEM((8, 512), full),
+            pltpu.VMEM((3, 8, 8, 512), full),
+            pltpu.SemaphoreType.DMA((13,)),
+            pltpu.SemaphoreType.DMA((13,)),
+        ],
+        compiler_params=pltpu.CompilerParams(
+            collective_id=10, has_side_effects=True, vmem_limit_bytes=VMEM_MOST
+        ),
+    )(grad_first, hidden, grad_residual, gain_two, *gains, *gradients, *flat)
 
 
 def shards(
@@ -1113,18 +1272,14 @@
     shrink_second,
 ):
     low = jnp.bfloat16
-    x_rows = hidden_in[0].astype(jnp.float32)
-    normed_one, scale_one = rms_parts(x_rows)
-    first_own = (normed_one * norm_gains[0]).astype(low)
-    shrunk_own = (RESID * cotangent[0].astype(jnp.float32)).astype(low)
-    cos_part, sin_part = angles(positions[0])
-    row_index = lax.axis_index("context") * 896 + jnp.arange(896, dtype=jnp.int32)
-    limit = jnp.maximum(row_index + 1, prefix[0]).reshape(BLOCKS, 1, 128)
-    limit = jnp.concatenate([limit] * GROUP, axis=2)
-    still = jnp.ones((896, HD), jnp.float32)
-    key_cos = jnp.concatenate([cos_part.T, cos_part.T, still], axis=1)
-    key_sin = jnp.concatenate([-sin_part.T, sin_part.T, 0.0 * still], axis=1)
-    tables = (cos_part, sin_part, key_cos, key_sin, limit)
+    hidden, upstream = hidden_in[0], cotangent[0]
+    masters = (
+        (input_weight, input_first, input_second),
+        (output_weight.T, output_first.T, output_second.T),
+        (expand_weight, expand_first, expand_second),
+        (shrink_weight.T, shrink_first.T, shrink_second.T),
+    )
+    tables = angles(positions[0])
     (
         first_all,
         shrunk_all,
@@ -1141,16 +1296,12 @@
         log_total,
         projected,
     ) = front(
-        first_own,
-        shrunk_own,
-        (
-            input_weight.astype(low),
-            expand_weight[0].astype(low),
-            expand_weight[1].astype(low),
-            output_weight.T.astype(low),
-            shrink_weight.T.astype(low),
-        ),
+        hidden,
+        upstream,
+        norm_gains[:1],
+        (input_weight, expand_weight, output_weight.T, shrink_weight.T),
         tables,
+        prefix,
     )
     (
         residual,
@@ -1162,16 +1313,9 @@
         grad_shrink,
         out_parts,
     ) = middle(
-        hidden_in[0],
-        cotangent[0],
-        projected,
-        norm_gains[1:],
-        shrunk_all,
-        w_gate,
-        w_up,
-        w_shrink,
-    )
-    shrunk, grad_first, grad_gate, grad_up, grad_shrink, grad_output, grad_input = back(
+        hidden, upstream, projected, norm_gains[1:], shrunk_all, w_gate, w_up, w_shrink
+    )
+    shrunk, grad_first, *gradients = back(
         projected_gradient,
         w_out,
         w_in,
@@ -1180,35 +1324,31 @@
         (grad_gate, grad_up, grad_shrink),
         (turned, kv_rows, kv_lines, attended, tokens, log_total),
         tables,
-    )
-    gain_one = jnp.sum(grad_first * normed_one, axis=0)
-    input_gradient = grad_residual + rms_back(grad_first * norm_gains[0], normed_one, scale_one)
+        prefix,
+    )
     block_output = (residual + RESID * shrunk).astype(low)
-    grad_expand = jnp.stack([grad_gate, grad_up])
-    grad_output, grad_shrink = grad_output.T, grad_shrink.T
-    reduced = (grad_input, grad_output, grad_expand, grad_shrink)
-    local_squares = sum(jnp.sum(g * g) for g in reduced)
-    gains_local = jnp.stack([gain_one, gain_two[0]]).reshape(24, 128)
-    message = jnp.concatenate([gains_local, jnp.full((8, 128), local_squares)], axis=0)
-    message = sum_everywhere(message, 10)
-    grad_gains = message[:24].reshape(2, 1536)
-    squares = message[24, 0] + jnp.sum(grad_gains * grad_gains)
-    gradient_norm = jnp.sqrt(squares)
-    factor = jnp.minimum(1.0, MAX_NORM / (gradient_norm + 1e-06))
-    gains_new = adamw(norm_gains, factor * grad_gains, gains_first, gains_second, GAIN_RATE, 0.0)
-    input_new = adamw(input_weight, factor * reduced[0], input_first, input_second, RATE, DECAY)
-    output_new = adamw(output_weight, factor * reduced[1], output_first, output_second, RATE, DECAY)
-    expand_new = adamw(expand_weight, factor * reduced[2], expand_first, expand_second, RATE, DECAY)
-    shrink_new = adamw(shrink_weight, factor * reduced[3], shrink_first, shrink_second, RATE, DECAY)
+    outs = finish(
+        grad_first,
+        hidden,
+        grad_residual,
+        gain_two,
+        (norm_gains, gains_first, gains_second),
+        gradients,
+        masters,
+    )
+    input_gradient, gradient_norm = outs[0], outs[1].reshape(())
+    gains_new, input_new, output_new, expand_new, shrink_new = (
+        outs[2 + 3 * i : 5 + 3 * i] for i in range(5)
+    )
     return (
         block_output[None],
         input_gradient[None],
         gradient_norm,
         *gains_new,
         *input_new,
-        *output_new,
+        *(array.T for array in output_new),
         *expand_new,
-        *shrink_new,
+        *(array.T for array in shrink_new),
     )
 
 

time: 306 us -> 279 us (0.912)
  other arithmetic: 32.1 us -> 4.69 us
  local copies, waits for them, and re-layouts: 4.39 us -> 14 us
  Pallas kernels: 257 us -> 253 us
  between operations: 6.93 us -> 3.51 us
    unnamed x40 -> x46, local copies, waits for them, and re-layouts: 0.32 us -> 12.6 us
    reduce_sum x7 -> x0, other arithmetic: 8.45 us -> none  [the longest x4 5.33 us: shards(): local_squares = sum((jnp.sum(g * g) for g in reduced))]
    sub x5 -> x0, other arithmetic: 7.13 us -> none  [adamw(): weight - step_rate * (momentum_hat / (jnp.sqrt(variance_hat) + ADAM_EPS)...]
    convert_element_type x4 -> x0, other arithmetic: 5.91 us -> none  [the longest x1 1.58 us: shards(): shrink_weight.T.astype(low)]
where the time goes in v5:
time: 279 us; the launch traced here: 275 us
  Pallas kernels  253 us (91%)
  local copies, waits for them, and re-layouts  14 us (5%)
  other arithmetic  4.69 us (2%)
  between operations  3.51 us (1%)
    pallas_call x1, Pallas kernels, back(): pl.pallas_call(back_kernel, out_shape=(jax.ShapeDtypeStruct((rows, width)...  89.9 us
    pallas_call x1, Pallas kernels, front(): pl.pallas_call(front_kernel, out_shape=(*(jax.ShapeDtypeStruct(shape, low...  86.3 us
    pallas_call x1, Pallas kernels, middle(): pl.pallas_call(middle_kernel, out_shape=(jax.ShapeDtypeStruct((rows, widt...  58.9 us
    pallas_call x1, Pallas kernels, finish(): pl.pallas_call(finish_kernel, out_shape=(jax.ShapeDtypeStruct((rows, widt...  17.9 us
    unnamed x46, local copies, waits for them, and re-layouts  12.6 us

profile of v5, /device:TPU:0, one launch (start us, length us, event | category | flops | bytes accessed | tf_op | source)
XLA Modules:
  0.0 275.1 jit_solution(11408398843345630653)
XLA Ops:
  1.3 0.7 convert_reduce_fusion
  2.0 1.4 fusion.1
  3.4 1.2 multiply_sine_fusion
  4.6 86.3 %shard_map.322 = (bf16[4,224,1536]{2,1,0:T(8,128)(2,1)}, bf16[4,224,1536]{2,1,0:T(8,128)(2,1)}, bf16[2,4,2,2,48,640]{5,4,3,2,1,0:T(8,128)(2,1)}, bf16[2,4,2,2,48...) custom-call(bf16[224,1536]{1,0:T(8,128)(2,1)} %bitcast.26, ...), custom_call_target="tpu_custom_call" | custom-call | tf_op jit(solution)/shard_map/pallas_call | solution.py:542
  90.9 58.9 %shard_map.323 = (f32[224,1536]{1,0:T(8,128)}, f32[224,1536]{1,0:T(8,128)}, bf16[224,1536]{1,0:T(8,128)(2,1)}, f32[1,1536]{1,0:T(1,128)}, bf16[1536,960]{1,0:T(8...) custom-call(bf16[224,1536]{1,0:T(8,128)(2,1)} %bitcast.27, ...), custom_call_target="tpu_custom_call" | custom-call | tf_op jit(solution)/shard_map/pallas_call | solution.py:699
  149.7 89.9 %shard_map.324 = (f32[224,1536]{1,0:T(8,128)}, f32[224,1536]{1,0:T(8,128)}, f32[48,960]{1,0:T(8,128)}, f32[48,960]{1,0:T(8,128)}, f32[48,960]{1,0:T(8,128)}, /*index=5*/f32[48,384]{1,0:T(8,128)}, f32[48,640]{1,0:T(8,128)}) custom-call(bf16[224,1536]{1,0:T(8,128)(2,1)} %get-tuple-element.70.refs_0_, bf16[1536,384]{1,0:T(8,128)(2,1)} %bitcast.39, ...), custom_call_target="tpu_custom_call" | custom-call | tf_op jit(solution)/shard_map/pallas_call | solution.py:1075
  239.6 2.8 %fusion = bf16[1,224,1536]{2,1,0:T(8,128)(2,1)} fusion(f32[224,1536]{1,0:T(8,128)} %get-tuple-element.69, f32[224,1536]{1,0:T(8,128)} %get-tuple-element.84), kind=kLoop, calls=%fused_computation.1 | loop fusion | flops 1032192 | bytes 3440640 | tf_op jit(solution)/shard_map/broadcast_in_dim | solution.py:1344
  242.5 17.9 %shard_map.325 = (f32[224,1536]{1,0:T(8,128)}, f32[1,1]{1,0:T(1,128)}, f32[2,1536]{1,0:T(2,128)}, f32[2,1536]{1,0:T(2,128)}, f32[2,1536]{1,0:T(2,128)}, /*index=...) custom-call(f32[224,1536]{1,0:T(8,128)} %get-tuple-element.85.refs_0, ...), custom_call_target="tpu_custom_call" | custom-call | tf_op jit(solution)/shard_map/pallas_call | solution.py:1233
  260.4 2.6 copy.55
  263.8 0.6 copy.57
  264.4 0.6 copy.58
  265.0 0.6 copy.59
  265.6 0.6 copy.60
  266.3 0.6 copy.61
  266.9 0.6 copy.62
  267.6 0.6 copy.63
  268.2 0.6 copy.64
  268.9 0.6 copy.65
  269.5 0.7 copy.66
  270.3 0.7 copy.67
  271.0 0.7 copy.68
  271.8 0.7 copy.69
  272.4 0.7 copy.70
  273.1 0.7 copy.71
  (31 shorter events, 0.1 us)
Async XLA Ops:
  260.3 3.5 %copy-start.14 = (f32[2,1536]{1,0:T(2,128)S(1)}, f32[2,1536]{1,0:T(2,128)}, u32[]{:S(2)}) copy-start(f32[2,1536]{1,0:T(2,128)} %get-tuple-element.135) | copy-start | bytes 36868
  260.4 4.1 %copy-start.13 = (f32[2,1536]{1,0:T(2,128)S(1)}, f32[2,1536]{1,0:T(2,128)}, u32[]{:S(2)}) copy-start(f32[2,1536]{1,0:T(2,128)} %get-tuple-element.136) | copy-start | bytes 36868
  260.4 4.7 %copy-start.12 = (f32[2,1536]{1,0:T(2,128)S(1)}, f32[2,1536]{1,0:T(2,128)}, u32[]{:S(2)}) copy-start(f32[2,1536]{1,0:T(2,128)} %get-tuple-element.137) | copy-start | bytes 36868
  260.4 5.3 %copy-start.8 = (f32[48,640]{1,0:T(8,128)S(1)}, f32[48,640]{1,0:T(8,128)}, u32[]{:S(2)}) copy-start(f32[48,640]{1,0:T(8,128)} %get-tuple-element.138) | copy-start | bytes 368644
  260.4 5.9 %copy-start.7 = (f32[48,640]{1,0:T(8,128)S(1)}, f32[48,640]{1,0:T(8,128)}, u32[]{:S(2)}) copy-start(f32[48,640]{1,0:T(8,128)} %get-tuple-element.139) | copy-start | bytes 368644
  260.4 6.5 %copy-start.6 = (f32[48,640]{1,0:T(8,128)S(1)}, f32[48,640]{1,0:T(8,128)}, u32[]{:S(2)}) copy-start(f32[48,640]{1,0:T(8,128)} %get-tuple-element.140) | copy-start | bytes 368644
  260.4 7.2 %copy-start.11 = (f32[48,384]{1,0:T(8,128)S(1)}, f32[48,384]{1,0:T(8,128)}, u32[]{:S(2)}) copy-start(f32[48,384]{1,0:T(8,128)} %get-tuple-element.101) | copy-start | bytes 221188
  260.4 7.8 %copy-start.10 = (f32[48,384]{1,0:T(8,128)S(1)}, f32[48,384]{1,0:T(8,128)}, u32[]{:S(2)}) copy-start(f32[48,384]{1,0:T(8,128)} %get-tuple-element.102) | copy-start | bytes 221188
  260.4 8.4 %copy-start.9 = (f32[48,384]{1,0:T(8,128)S(1)}, f32[48,384]{1,0:T(8,128)}, u32[]{:S(2)}) copy-start(f32[48,384]{1,0:T(8,128)} %get-tuple-element.103) | copy-start | bytes 221188
  260.4 9.1 %copy-start.2 = (f32[2,48,960]{2,1,0:T(8,128)S(1)}, f32[2,48,960]{2,1,0:T(8,128)}, u32[]{:S(2)}) copy-start(f32[2,48,960]{2,1,0:T(8,128)} %get-tuple-element.144) | copy-start | bytes 1105924
  263.1 7.2 %copy-start.1 = (f32[2,48,960]{2,1,0:T(8,128)S(1)}, f32[2,48,960]{2,1,0:T(8,128)}, u32[]{:S(2)}) copy-start(f32[2,48,960]{2,1,0:T(8,128)} %get-tuple-element.145) | copy-start | bytes 1105924
  265.6 5.4 %copy-start = (f32[2,48,960]{2,1,0:T(8,128)S(1)}, f32[2,48,960]{2,1,0:T(8,128)}, u32[]{:S(2)}) copy-start(f32[2,48,960]{2,1,0:T(8,128)} %get-tuple-element.146) | copy-start | bytes 1105924
  267.6 4.2 %copy-start.5 = (f32[48,960]{1,0:T(8,128)S(1)}, f32[48,960]{1,0:T(8,128)}, u32[]{:S(2)}) copy-start(f32[48,960]{1,0:T(8,128)} %get-tuple-element.107) | copy-start | bytes 552964
  269.5 2.9 %copy-start.4 = (f32[48,960]{1,0:T(8,128)S(1)}, f32[48,960]{1,0:T(8,128)}, u32[]{:S(2)}) copy-start(f32[48,960]{1,0:T(8,128)} %get-tuple-element.108) | copy-start | bytes 552964
  270.3 2.9 %copy-start.3 = (f32[48,960]{1,0:T(8,128)S(1)}, f32[48,960]{1,0:T(8,128)}, u32[]{:S(2)}) copy-start(f32[48,960]{1,0:T(8,128)} %get-tuple-element.109) | copy-start | bytes 552964

commit v6 on v5

--- a/solution.py
+++ b/solution.py
@@ -133,8 +133,18 @@
 
 
 def arrival(z, i):
-    shifted = i - 3 + (3 - z) // 3
-    return lax.rem(2 * z + shifted + (shifted + 7) // 7 + 7, 7)
+    edge = (3 - z) // 3
+    if isinstance(i, int) and i < 2:
+        shift = i * (2 * edge - 1)
+    elif isinstance(i, int) and i > 3:
+        shift = i - 2 + edge
+    else:
+        shift = 3 * i - 8 + edge
+    return lax.rem(2 * z + shift + 7, 7)
+
+
+def arrival_far(z, i):
+    return lax.rem(2 * z + i + 5 + (3 - z) // 3, 7)
 
 
 def ring_peers():
@@ -160,10 +170,10 @@
     first, second = own.at[pl.ds(0, rows)], own.at[pl.ds(rows, rows)]
     first_to, second_to = halves(held, z)
     copies = [
-        remote(first, first_to, send_sem.at[0], recv_sem.at[0], up),
-        remote(second, second_to, send_sem.at[1], recv_sem.at[1], down),
-        remote(second, second_to, send_sem.at[2], recv_sem.at[2], up),
-        remote(first, first_to, send_sem.at[3], recv_sem.at[3], down),
+        remote(second, second_to, send_sem.at[0], recv_sem.at[0], up),
+        remote(first, first_to, send_sem.at[1], recv_sem.at[1], down),
+        remote(first, first_to, send_sem.at[2], recv_sem.at[2], up),
+        remote(second, second_to, send_sem.at[3], recv_sem.at[3], down),
     ]
     for copy in copies:
         copy.start()
@@ -173,11 +183,11 @@
 def ring_gather_forward(held, copies, send_sem, recv_sem):
     z, zp, z2, zm, up, down = ring_peers()
     copies[0].wait_recv()
-    below = halves(held, zm)[0]
+    below = halves(held, zm)[1]
     on_up = remote(below, below, send_sem.at[4], recv_sem.at[4], up)
     on_up.start()
     copies[1].wait_recv()
-    above = halves(held, zp)[1]
+    above = halves(held, zp)[0]
     on_down = remote(above, above, send_sem.at[5], recv_sem.at[5], down)
     on_down.start()
     return copies + [on_up, on_down]
@@ -288,8 +298,8 @@
 
 
 class PlaneGather:
-    def __init__(self, own, held, y_first, send_sem, recv_sem):
-        self.own, self.held, self.y_first = own, held, y_first
+    def __init__(self, own, held, y_first, shared, send_sem, recv_sem):
+        self.own, self.held, self.y_first, self.shared = own, held, y_first, shared
         self.send_sem, self.recv_sem, self.used = send_sem, recv_sem, 0
         self.copies, self.first, self.second, self.third = [], [], [], []
 
@@ -321,7 +331,7 @@
         mine = self.line((xh, xl) if self.y_first else y)
         peers = x_peers if self.y_first else y_peers
         self.second = [self.send(mine, mine, peer) for peer in peers]
-        self.third = [self.send(mine, mine, other)]
+        self.third = [self.send(mine, mine, other)] if self.shared else []
 
     def share(self):
         ys, xs, y_peers, x_peers, other = plane()
@@ -332,7 +342,7 @@
             self.third.append(self.send(line, line, other))
 
     def end(self):
-        for copy in self.third:
+        for copy in self.third if self.shared else self.second:
             copy.wait_recv()
         for copy in self.copies:
             copy.wait_send()
@@ -372,7 +382,7 @@
     owns = (in_own, w_out, w_gate, w_up, w_shrink)
     helds = (in_all, out_all, gate_all, up_all, shrink_all)
     gathers = [
-        PlaneGather(own, held, i in (2, 3), plane_send.at[i], plane_recv.at[i])
+        PlaneGather(own, held, i == 4, i < 2, plane_send.at[i], plane_recv.at[i])
         for i, (own, held) in enumerate(zip(owns, helds))
     ]
     for gather in gathers[:2]:
@@ -393,13 +403,16 @@
         keep.wait()
     for gather in gathers[:2]:
         gather.spread()
+    for gather in gathers[2:4]:
+        gather.begin()
     key_tables(cos_ref, sin_ref, key_cos, key_sin)
     ring = ring_gather_forward(first_all, ring, ring_send.at[0], ring_recv.at[0])
     gathers[0].share()
     gathers[1].share()
+    gathers[4].begin()
+    for gather in gathers[2:4]:
+        gather.spread()
     gathers[0].end()
-    for gather in gathers[2:]:
-        gather.begin()
 
     def project(c, rows):
         out = nn(first_all[c], in_all[...].reshape(1536, 640))
@@ -450,8 +463,7 @@
     save(turned, turned_to)
     for copy in kv_copies:
         copy.wait_recv()
-    for gather in gathers[2:]:
-        gather.spread()
+    gathers[4].spread()
     for g in range(HEADS):
         kv_lines[g] = jnp.transpose(kv_rows[g].astype(jnp.float32)).astype(low)
     save(kv_rows, rows_to)
@@ -479,8 +491,16 @@
 
         by_span(xl, b, run)
 
-    def both_heads(t, carry):
+    def near_heads(t, carry):
         block(arrival(z, lax.div(t, 2)), lax.rem(t, 2))
+        return carry
+
+    def far_heads(t, carry):
+        block(arrival_far(z, lax.div(t, 2)), lax.rem(t, 2))
+        return carry
+
+    def beside_block(g, carry):
+        block(arrival(z, 1), g)
         return carry
 
     def own_block(g, carry):
@@ -495,7 +515,7 @@
         mine = pl.ds(pl.multiple_of(c * 224, 16), 224)
         parts[c] = nt(tokens[mine], held_rows[...].reshape(1536, 384)).astype(low)
 
-    lax.fori_loop(8, 14, both_heads, 0)
+    lax.fori_loop(8, 14, far_heads, 0)
     later = ring_gather_forward(shrunk_all, later, ring_send.at[1], ring_recv.at[1])
     gathers[1].end()
     fetch = pltpu.make_async_copy(out_all, held_rows, out_sem)
@@ -505,7 +525,8 @@
     fetch.wait()
     apply(z2)
     far = ring_scatter_far(parts, came, ring_send.at[2], ring_recv.at[2])
-    lax.fori_loop(2, 8, both_heads, 0)
+    lax.fori_loop(0, 2, beside_block, 0)
+    lax.fori_loop(4, 8, near_heads, 0)
     for i in range(1, 4):
         lay(arrival(z, i))
     apply(zp)
@@ -517,8 +538,6 @@
     lax.fori_loop(0, 2, own_block, 0)
     lay(2 * z)
     apply(z)
-    for gather in gathers[2:]:
-        gather.share()
     for gather in gathers[2:]:
         gather.end()
     ring_gather_end(later)
@@ -581,7 +600,7 @@
             collective_id=0, has_side_effects=True, vmem_limit_bytes=VMEM_MOST
         ),
     )(hidden, cotangent, gain, *weights, *tables, prefix)
-    return outs[:2] + tuple(held.reshape(1536, -1) for held in outs[2:7]) + outs[7:]
+    return outs
 
 
 def tn(a, b):
@@ -597,17 +616,23 @@
     (second_all, activated_back, gated, gate_back, up_back) = refs[20:25]
     (parts, came, sums, total) = refs[25:29]
     (grad_gate, grad_up, grad_shrink, out_parts) = refs[29:33]
-    (ring_send, ring_recv, load_sem) = refs[33:]
+    (ring_send, ring_recv, load_sem, share_send, share_recv) = refs[33:]
     z, zp, z2, zm, up, down = ring_peers()
-    hail([up, down])
+    xh, y, core, xl, z = place()
+
+    def flat(weight):
+        return weight[...].reshape(1536, 960)
+
+    other = device(xh, y, 1 - core, xl, z)
+    hail([up, down, other])
     loads = [
         pltpu.make_async_copy(src, dst, load_sem.at[i])
         for i, (src, dst) in enumerate(
             (
-                (shrink_from, w_shrink),
+                (shrink_from.at[:, :, core], w_shrink.at[:, :, core]),
                 (shrunk_from, shrunk_all),
-                (gate_from, w_gate),
-                (up_from, w_up),
+                (gate_from.at[:, :, core], w_gate.at[:, :, core]),
+                (up_from.at[:, :, core], w_up.at[:, :, core]),
             )
         )
     ]
@@ -617,18 +642,31 @@
     residual[...] = rows
     scaling = lax.rsqrt(jnp.mean(rows * rows, axis=-1, keepdims=True) + EPS)
     second_all[z] = (rows * scaling * gain[...]).astype(jnp.bfloat16)
-    meet([up, down])
+    meet([up, down, other])
     ring = ring_gather_begin(second_all.at[z], second_all, ring_send.at[0], ring_recv.at[0])
+    shares = [
+        remote(
+            src.at[:, :, core], dst.at[:, :, core], share_send.at[i], share_recv.at[i], other
+        )
+        for i, (src, dst) in enumerate(
+            ((shrink_from, w_shrink), (gate_from, w_gate), (up_from, w_up))
+        )
+    ]
+    for share in shares:
+        share.start()
     loads[0].wait()
     loads[1].wait()
+    shares[0].wait_recv()
     for c in range(4):
-        activated_back[c] = nn(shrunk_all[c], w_shrink[...])
+        activated_back[c] = nn(shrunk_all[c], flat(w_shrink))
     loads[2].wait()
     loads[3].wait()
+    shares[1].wait_recv()
+    shares[2].wait_recv()
 
     def feed(c):
-        gate_value = nn(second_all[c], w_gate[...])
-        up_value = nn(second_all[c], w_up[...])
+        gate_value = nn(second_all[c], flat(w_gate))
+        up_value = nn(second_all[c], flat(w_up))
         sigmoid_gate = 1.0 / (1.0 + jnp.exp(-gate_value))
         gate_active = gate_value * sigmoid_gate
         gated[c] = (gate_active * up_value).astype(jnp.bfloat16)
@@ -637,7 +675,7 @@
             gradient * up_value * sigmoid_gate * (1.0 + gate_value * (1.0 - sigmoid_gate))
         ).astype(jnp.bfloat16)
         up_back[c] = (gradient * gate_active).astype(jnp.bfloat16)
-        parts[c] = (nt(gate_back[c], w_gate[...]) + nt(up_back[c], w_up[...])).astype(
+        parts[c] = (nt(gate_back[c], flat(w_gate)) + nt(up_back[c], flat(w_up))).astype(
             jnp.bfloat16
         )
 
@@ -671,9 +709,9 @@
     ).astype(jnp.bfloat16)
     save(grad_shrink, shrink_to)
     for c in range(4):
-        out_parts[c] = nt(gated[c], w_shrink[...]).astype(jnp.bfloat16)
+        out_parts[c] = nt(gated[c], flat(w_shrink)).astype(jnp.bfloat16)
     save(out_parts, out_to)
-    for copy in ring:
+    for copy in ring + shares:
         copy.wait_send()
     ring_scatter_end(parts, came, total, scatter)
     rows = residual[...]
@@ -712,9 +750,9 @@
         out_specs=(whole,) * 4 + (any_place,) * 4,
         scratch_shapes=[
             pltpu.VMEM((4, rows, width), low),
-            pltpu.VMEM((1536, 960), low),
-            pltpu.VMEM((1536, 960), low),
-            pltpu.VMEM((1536, 960), low),
+            pltpu.VMEM((2, 4, 2, 2, 48, 960), low),
+            pltpu.VMEM((2, 4, 2, 2, 48, 960), low),
+            pltpu.VMEM((2, 4, 2, 2, 48, 960), low),
             pltpu.VMEM((4, rows, width), low),
             pltpu.VMEM((4, rows, 960), full),
             pltpu.VMEM((4, rows, 960), low),
@@ -731,6 +769,8 @@
             pltpu.SemaphoreType.DMA((2, 6)),
             pltpu.SemaphoreType.DMA((2, 6)),
             pltpu.SemaphoreType.DMA((8,)),
+            pltpu.SemaphoreType.DMA((3,)),
+            pltpu.SemaphoreType.DMA((3,)),
         ],
         compiler_params=pltpu.CompilerParams(
             collective_id=4, has_side_effects=True, vmem_limit_bytes=VMEM_MOST
@@ -853,20 +893,27 @@
     (own, out_from, in_from, first_from, out_terms) = refs[:5]
     gradients = refs[5:8]
     (turned, kv_rows, kv_lines, attended, tokens, log_total) = refs[8:14]
-    (cos_ref, sin_ref, prefix) = refs[14:17]
-    (shrunk_total, first_total) = refs[17:19]
-    totals = refs[19:24]
-    (proj_all, w_out, w_in, grad_tokens, grad_lines, grad_queries, grad_packed) = refs[24:31]
-    (sums, outgoing, incoming, parts, came_one, came_two, ring_sums) = refs[31:38]
-    stages, out_parts, in_parts = refs[38:40], refs[40], refs[41]
-    rooms = refs[42:62]
-    (key_cos, key_sin) = refs[62:64]
-    (ring_send, ring_recv, plane_send, plane_recv, kv_send, kv_recv, load_sem) = refs[64:]
+    (cos_ref, sin_ref, hidden, gain_two, prefix) = refs[14:19]
+    (shrunk_total, first_total) = refs[19:21]
+    totals = refs[21:26]
+    everywhere = refs[26]
+    (proj_all, w_out, w_in, grad_tokens, grad_lines, grad_queries, grad_packed) = refs[27:34]
+    (sums, outgoing, incoming, parts, came_one, came_two, ring_sums) = refs[34:41]
+    stages, out_parts, in_parts = refs[41:43], refs[43], refs[44]
+    rooms = refs[45:65]
+    (key_cos, key_sin, gathered) = refs[65:68]
+    (ring_send, ring_recv, plane_send, plane_recv, kv_send, kv_recv, load_sem) = refs[68:75]
+    (sum_send, sum_recv) = refs[75:]
     xh, y, core, xl, z = place()
     z, zp, z2, zm, up, down = ring_peers()
     ys, xs, y_peers, x_peers, other = plane()
     beside = device(xh, y, core, 1 - xl, z)
-    peers = [up, down, other] + y_peers + x_peers
+    column = [
+        device(xh, y, c, xl, lax.rem(z + d, 4))
+        for d, c in ((1, core), (3, core), (0, 1 - core), (2, core))
+        + ((1, 1 - core), (3, 1 - core), (2, 1 - core))
+    ]
+    peers = column + y_peers + x_peers
     hail(peers)
     sums[...] = jnp.zeros_like(sums)
     key_tables(cos_ref, sin_ref, key_cos, key_sin)
@@ -897,9 +944,11 @@
     load_terms = load(out_terms, parts, 5)
     load_in = load(in_from, w_in, 6)
 
-    def give(c):
-        rows = pl.ds(pl.multiple_of(c * 224, 16), 224)
-        grad_tokens[rows] = nn(proj_all[c], w_out[...]).astype(jnp.bfloat16)
+    def give(c, start=0, count=224):
+        rows = pl.ds(pl.multiple_of(c * 224 + start, 16), count)
+        grad_tokens[rows] = nn(proj_all[c, start : start + count], w_out[...]).astype(
+            jnp.bfloat16
+        )
 
     def lay(b):
         columns = pl.ds(pl.multiple_of(b * 128, 128), 128)
@@ -965,6 +1014,14 @@
 
     lax.fori_loop(0, 2, own_block, 0)
     ring = ring_gather_forward(proj_all, ring, ring_send.at[0], ring_recv.at[0])
+    give(zm, 112, 112)
+    give(zp, 0, 112)
+    lay(arrival(z, 1))
+
+    def beside_block(g, carry):
+        block(arrival(z, 1), g)
+        return carry
+
     staged[0].wait()
     feed[0].fold(stages[0])
     staged[0] = feed[2].stage(stages[0], load_sem.at[4])
@@ -972,13 +1029,14 @@
     feed[1].fold(stages[1])
     staged[0].wait()
     feed[2].fold(stages[0])
+    lax.fori_loop(0, 2, beside_block, 0)
     ring[2].wait_recv()
-    give(zm)
+    give(zm, 0, 112)
     ring[3].wait_recv()
-    give(zp)
-    for i in range(1, 4):
+    give(zp, 112, 112)
+    for i in range(2, 4):
         lay(arrival(z, i))
-    lax.fori_loop(2, 8, both_heads, 0)
+    lax.fori_loop(4, 8, both_heads, 0)
     ring[4].wait_recv()
     ring[5].wait_recv()
     give(z2)
@@ -1005,7 +1063,7 @@
 
     def far_block(g):
         def body(i, carry):
-            block(arrival(z, i), g)
+            block(arrival_far(z, i), g)
             return carry
 
         lax.fori_loop(4, 7, body, 0)
@@ -1057,13 +1115,44 @@
         every[i].end(totals[i])
     in_scatter.line()
     ring_scatter_end(parts, came_two, first_total, ring)
+    rows = hidden[...].astype(jnp.float32)
+    scaling = lax.rsqrt(jnp.mean(rows * rows, axis=-1, keepdims=True) + EPS)
+    gain_one = jnp.sum(first_total[...] * rows * scaling, axis=0, keepdims=True)
     in_scatter.end(totals[4])
-
-
-SCATTER_TURNS = (True, True, False, False, False)
-
-
-def back(own, w_out, w_in, first_all, out_terms, gradients, saved, tables, prefix):
+    squares = jnp.zeros((1, 1), jnp.float32)
+    for total in totals:
+        terms = total[...]
+        squares = squares + jnp.sum(
+            jnp.sum(terms * terms, axis=0, keepdims=True), axis=1, keepdims=True
+        )
+    for k in range(3):
+        everywhere[k : k + 1] = gain_one[:, k * 512 : (k + 1) * 512]
+        everywhere[3 + k : 4 + k] = gain_two[:, k * 512 : (k + 1) * 512]
+    everywhere[6:8] = jnp.broadcast_to(squares, (2, 512))
+    used = 0
+    groups = ((column, z * 2 + core, 8), (x_peers, xh * 2 + xl, 4), (y_peers, y, 4))
+    for axis, (group, here, count) in enumerate(groups):
+        gathered[axis, here] = everywhere[...]
+        spot = gathered.at[axis, here]
+        copies = []
+        for peer in group:
+            copies.append(remote(spot, spot, sum_send.at[used], sum_recv.at[used], peer))
+            copies[-1].start()
+            used += 1
+        for copy in copies:
+            copy.wait()
+        order = gathered[axis, 0]
+        for k in range(1, count):
+            order = order + gathered[axis, k]
+        everywhere[...] = order
+
+
+SCATTER_TURNS = (False, False, True, True, False)
+
+
+def back(
+    own, w_out, w_in, first_all, out_terms, gradients, saved, tables, hidden, gain_two, prefix
+):
     any_place = pl.BlockSpec(memory_space=pl.ANY)
     whole = pl.BlockSpec(memory_space=pltpu.VMEM)
     rows, width = own.shape
@@ -1075,12 +1164,13 @@
     return pl.pallas_call(
         back_kernel,
         out_shape=(jax.ShapeDtypeStruct((rows, width), full),) * 2
-        + tuple(jax.ShapeDtypeStruct((48, w), full) for w in widths),
+        + tuple(jax.ShapeDtypeStruct((48, w), full) for w in widths)
+        + (jax.ShapeDtypeStruct((8, 512), full),),
         in_specs=[whole]
         + [any_place] * 7
-        + [whole] * 8
+        + [whole] * 10
         + [pl.BlockSpec(memory_space=pltpu.SMEM)],
-        out_specs=(whole,) * 7,
+        out_specs=(whole,) * 8,
         scratch_shapes=[
             pltpu.VMEM((4, rows, width), low),
             pltpu.VMEM((1536, 384), low),
@@ -1103,6 +1193,7 @@
             *rooms,
             pltpu.VMEM((896, 128), full),
             pltpu.VMEM((896, 128), full),
+            pltpu.VMEM((3, 8, 8, 512), full),
             pltpu.SemaphoreType.DMA((3, 6)),
             pltpu.SemaphoreType.DMA((3, 6)),
             pltpu.SemaphoreType.DMA((5, 10)),
@@ -1110,6 +1201,8 @@
             pltpu.SemaphoreType.DMA((2,)),
             pltpu.SemaphoreType.DMA((2,)),
             pltpu.SemaphoreType.DMA((8,)),
+            pltpu.SemaphoreType.DMA((13,)),
+            pltpu.SemaphoreType.DMA((13,)),
         ],
         compiler_params=pltpu.CompilerParams(
             collective_id=2, has_side_effects=True, vmem_limit_bytes=BACK_VMEM
@@ -1123,6 +1216,8 @@
         *(g.reshape(2, 4, 2, 2, 48, g.shape[-1]) for g in gradients),
         *saved,
         *tables,
+        hidden,
+        gain_two,
         prefix,
     )
 
@@ -1131,70 +1226,24 @@
 
 
 def finish_kernel(*refs):
-    (grad_first, hidden, grad_residual, gain_two) = refs[:4]
-    (gains, gains_first, gains_second) = refs[4:7]
-    (grad_gate, grad_up, grad_shrink, grad_output, grad_input) = refs[7:12]
-    masters = [refs[12 + 3 * i : 15 + 3 * i] for i in range(4)]
-    (input_gradient, norm_ref) = refs[24:26]
-    gains_new = refs[26:29]
-    news = [refs[29 + 3 * i : 32 + 3 * i] for i in range(4)]
-    own, held, sems_out, sems_in = refs[41:]
-    xh, y, core, xl, z = place()
-    ys, xs, y_peers, x_peers, other = plane()
-    groups = (
-        (
-            [
-                device(xh, y, c, xl, lax.rem(z + d, 4))
-                for d, c in ((1, core), (3, core), (0, 1 - core), (2, core))
-                + ((1, 1 - core), (3, 1 - core), (2, 1 - core))
-            ],
-            z * 2 + core,
-            8,
-        ),
-        (x_peers, xh * 2 + xl, 4),
-        (y_peers, y, 4),
-    )
-    peers = [peer for group in groups for peer in group[0]]
-    hail(peers)
+    (sums, grad_first, hidden, grad_residual, residual, shrunk) = refs[:6]
+    (gains, gains_first, gains_second) = refs[6:9]
+    (grad_gate, grad_up, grad_shrink, grad_output, grad_input) = refs[9:14]
+    masters = [refs[14 + 3 * i : 17 + 3 * i] for i in range(4)]
+    (block_output, input_gradient, norm_ref) = refs[26:29]
+    gains_new = refs[29:32]
+    news = [refs[32 + 3 * i : 35 + 3 * i] for i in range(4)]
+    block_output[...] = (residual[...] + RESID * shrunk[...]).astype(jnp.bfloat16)
     rows = hidden[...].astype(jnp.float32)
     scaling = lax.rsqrt(jnp.mean(rows * rows, axis=-1, keepdims=True) + EPS)
     normed = rows * scaling
-    gradient = grad_first[...]
-    gain_one = jnp.sum(gradient * normed, axis=0, keepdims=True)
-    squares = jnp.zeros((1, 1), jnp.float32)
-    for terms in (grad_gate, grad_up, grad_shrink, grad_output, grad_input):
-        held_terms = terms[...]
-        squares = squares + jnp.sum(
-            jnp.sum(held_terms * held_terms, axis=0, keepdims=True), axis=1, keepdims=True
-        )
-    for k in range(3):
-        own[k : k + 1] = gain_one[:, k * 512 : (k + 1) * 512]
-        own[3 + k : 4 + k] = gain_two[:, k * 512 : (k + 1) * 512]
-    own[6:8] = jnp.broadcast_to(squares, (2, 512))
-    meet(peers)
-    used = 0
-    for axis, (group, here, count) in enumerate(groups):
-        held[axis, here] = own[...]
-        spot = held.at[axis, here]
-        copies = []
-        for peer in group:
-            copies.append(remote(spot, spot, sems_out.at[used], sems_in.at[used], peer))
-            copies[-1].start()
-            used += 1
-        if axis == 0:
-            gradient = gradient * gains[0:1]
-            input_gradient[...] = grad_residual[...] + scaling * (
-                gradient - normed * jnp.mean(gradient * normed, axis=-1, keepdims=True)
-            )
-        for copy in copies:
-            copy.wait()
-        order = held[axis, 0]
-        for k in range(1, count):
-            order = order + held[axis, k]
-        own[...] = order
+    gradient = grad_first[...] * gains[0:1]
+    input_gradient[...] = grad_residual[...] + scaling * (
+        gradient - normed * jnp.mean(gradient * normed, axis=-1, keepdims=True)
+    )
     grad_gains = jnp.concatenate(
         [
-            jnp.concatenate([own[3 * r + k : 3 * r + k + 1] for k in range(3)], axis=1)
+            jnp.concatenate([sums[3 * r + k : 3 * r + k + 1] for k in range(3)], axis=1)
             for r in range(2)
         ],
         axis=0,
@@ -1202,7 +1251,7 @@
     gain_squares = jnp.sum(
         jnp.sum(grad_gains * grad_gains, axis=0, keepdims=True), axis=1, keepdims=True
     )
-    gradient_norm = jnp.sqrt(own[6:7, 0:1] + gain_squares)
+    gradient_norm = jnp.sqrt(sums[6:7, 0:1] + gain_squares)
     norm_ref[...] = gradient_norm
     factor = jnp.minimum(1.0, MAX_NORM / (gradient_norm + 1e-06))
 
@@ -1226,28 +1275,40 @@
             target[k] = result
 
 
-def finish(grad_first, hidden, grad_residual, gain_two, gains, gradients, masters):
-    rows, width = hidden.shape
+def finish(sums, rows_in, gains, gradients, masters):
     full = jnp.float32
     flat = [array for group in masters for array in group]
+
+    def cut(array):
+        shape = array.shape[:-2] + (array.shape[-2] // 2, array.shape[-1])
+        lead = (0,) * (array.ndim - 2)
+        return pl.BlockSpec(shape, lambda i: lead + (i, 0))
+
+    def kept(shape):
+        return pl.BlockSpec(shape, lambda i: (0, 0))
+
+    width = rows_in[0].shape[1]
+    rows = jax.ShapeDtypeStruct(rows_in[0].shape, full)
     return pl.pallas_call(
         finish_kernel,
+        grid=(2,),
         out_shape=(
-            jax.ShapeDtypeStruct((rows, width), full),
+            jax.ShapeDtypeStruct(rows.shape, jnp.bfloat16),
+            rows,
             jax.ShapeDtypeStruct((1, 1), full),
             *(jax.ShapeDtypeStruct((2, width), full) for _ in range(3)),
             *(jax.ShapeDtypeStruct(array.shape, full) for array in flat),
         ),
-        scratch_shapes=[
-            pltpu.VMEM((8, 512), full),
-            pltpu.VMEM((3, 8, 8, 512), full),
-            pltpu.SemaphoreType.DMA((13,)),
-            pltpu.SemaphoreType.DMA((13,)),
-        ],
-        compiler_params=pltpu.CompilerParams(
-            collective_id=10, has_side_effects=True, vmem_limit_bytes=VMEM_MOST
-        ),
-    )(grad_first, hidden, grad_residual, gain_two, *gains, *gradients, *flat)
+        in_specs=[kept(sums.shape)]
+        + [cut(array) for array in rows_in]
+        + [kept(array.shape) for array in gains]
+        + [cut(array) for array in gradients]
+        + [cut(array) for array in flat],
+        out_specs=(cut(rows), cut(rows), kept((1, 1)))
+        + (kept((2, width)),) * 3
+        + tuple(cut(array) for array in flat),
+        compiler_params=pltpu.CompilerParams(vmem_limit_bytes=VMEM_MOST),
+    )(sums, *rows_in, *gains, *gradients, *flat)
 
 
 def shards(
@@ -1315,30 +1376,29 @@
     ) = middle(
         hidden, upstream, projected, norm_gains[1:], shrunk_all, w_gate, w_up, w_shrink
     )
-    shrunk, grad_first, *gradients = back(
+    shrunk, grad_first, *gradients, sums = back(
         projected_gradient,
-        w_out,
-        w_in,
+        w_out.reshape(1536, 384),
+        w_in.reshape(1536, 640),
         first_all,
         out_parts,
         (grad_gate, grad_up, grad_shrink),
         (turned, kv_rows, kv_lines, attended, tokens, log_total),
         tables,
+        hidden,
+        gain_two,
         prefix,
     )
-    block_output = (residual + RESID * shrunk).astype(low)
     outs = finish(
-        grad_first,
-        hidden,
-        grad_residual,
-        gain_two,
+        sums,
+        (grad_first, hidden, grad_residual, residual, shrunk),
         (norm_gains, gains_first, gains_second),
         gradients,
         masters,
     )
-    input_gradient, gradient_norm = outs[0], outs[1].reshape(())
+    block_output, input_gradient, gradient_norm = outs[0], outs[1], outs[2].reshape(())
     gains_new, input_new, output_new, expand_new, shrink_new = (
-        outs[2 + 3 * i : 5 + 3 * i] for i in range(5)
+        outs[3 + 3 * i : 6 + 3 * i] for i in range(5)
     )
     return (
         block_output[None],

time: 279 us -> 253 us (0.907)
  local copies, waits for them, and re-layouts: 14 us -> 1.39 us
  Pallas kernels: 253 us -> 244 us
  other arithmetic: 4.69 us -> 1.88 us
    unnamed x46 -> x0, local copies, waits for them, and re-layouts: 12.6 us -> none
    pallas_call x1, Pallas kernels: 17.9 us -> 5.87 us  [finish(): pl.pallas_call(finish_kernel, grid=(2,), out_shape=(jax.ShapeDtypeStruct(...]
    pallas_call x1, Pallas kernels: 89.9 us -> 98.7 us  [back(): pl.pallas_call(back_kernel, out_shape=(jax.ShapeDtypeStruct((rows, width)...]
    pallas_call x1, Pallas kernels: 86.3 us -> 82.6 us  [front(): pl.pallas_call(front_kernel, out_shape=(*(jax.ShapeDtypeStruct(shape, low...]
    broadcast_in_dim x1 -> x0, other arithmetic: 2.82 us -> none  [shards(): block_output[None]]
where the time goes in v6:
time: 253 us; the launch traced here: 249 us
  Pallas kernels  244 us (96%)
    pallas_call x1, Pallas kernels, back(): pl.pallas_call(back_kernel, out_shape=(jax.ShapeDtypeStruct((rows, width)...  98.7 us
    pallas_call x1, Pallas kernels, front(): pl.pallas_call(front_kernel, out_shape=(*(jax.ShapeDtypeStruct(shape, low...  82.6 us
    pallas_call x1, Pallas kernels, middle(): pl.pallas_call(middle_kernel, out_shape=(jax.ShapeDtypeStruct((rows, widt...  57.3 us
    pallas_call x1, Pallas kernels, finish(): pl.pallas_call(finish_kernel, grid=(2,), out_shape=(jax.ShapeDtypeStruct(...  5.87 us

profile of v6, /device:TPU:0, one launch (start us, length us, event | category | flops | bytes accessed | tf_op | source)
XLA Modules:
  0.0 249.3 jit_solution(10616257265394692479)
XLA Ops:
  1.3 0.7 convert_reduce_fusion
  2.0 1.4 fusion
  3.4 1.2 multiply_sine_fusion
  4.6 82.6 %shard_map.322 = (bf16[4,224,1536]{2,1,0:T(8,128)(2,1)}, bf16[4,224,1536]{2,1,0:T(8,128)(2,1)}, bf16[2,4,2,2,48,640]{5,4,3,2,1,0:T(8,128)(2,1)}, bf16[2,4,2,2,48...) custom-call(bf16[224,1536]{1,0:T(8,128)(2,1)} %bitcast.22, ...), custom_call_target="tpu_custom_call" | custom-call | tf_op jit(solution)/shard_map/pallas_call | solution.py:561
  87.2 57.3 %shard_map.323 = (f32[224,1536]{1,0:T(8,128)}, f32[224,1536]{1,0:T(8,128)}, bf16[224,1536]{1,0:T(8,128)(2,1)}, f32[1,1536]{1,0:T(1,128)}, bf16[1536,960]{1,0:T(8...) custom-call(bf16[224,1536]{1,0:T(8,128)(2,1)} %bitcast.23, ...), custom_call_target="tpu_custom_call" | custom-call | tf_op jit(solution)/shard_map/pallas_call | solution.py:737
  144.5 98.7 %shard_map.324 = (f32[224,1536]{1,0:T(8,128)}, f32[224,1536]{1,0:T(8,128)}, f32[48,960]{1,0:T(8,128)}, f32[48,960]{1,0:T(8,128)}, f32[48,960]{1,0:T(8,128)}, /*i...) custom-call(bf16[224,1536]{1,0:T(8,128)(2,1)} %get-tuple-element.71.refs_0_, bf16[1536,384]{1,0:T(8,128)(2,1)} %bitcast.32, ...), custom_call_target="tpu_custom_call" | custom-call | tf_op jit(solution)/shard_map/pallas_call | solution.py:1164
  243.2 5.9 %shard_map.325 = (bf16[224,1536]{1,0:T(8,128)(2,1)}, f32[224,1536]{1,0:T(8,128)}, f32[1,1]{1,0:T(1,128)}, f32[2,1536]{1,0:T(2,128)}, f32[2,1536]{1,0:T(2,128)}, ...) custom-call(f32[8,512]{1,0:T(8,128)} %get-tuple-element.86.refs_0_, ...), custom_call_target="tpu_custom_call" | custom-call | tf_op jit(solution)/shard_map/pallas_call | solution.py:1292
  (1 shorter events, 0.0 us)

commit v7 on v6

--- a/solution.py
+++ b/solution.py
@@ -302,6 +302,13 @@
         self.own, self.held, self.y_first, self.shared = own, held, y_first, shared
         self.send_sem, self.recv_sem, self.used = send_sem, recv_sem, 0
         self.copies, self.first, self.second, self.third = [], [], [], []
+        xh, y, core, xl, z = place()
+        ys, xs, self.y_peers, self.x_peers, self.other = plane()
+        self.core = core
+        if y_first:
+            self.mine, self.wheres, self.peers = (xh, xl), xs, self.x_peers
+        else:
+            self.mine, self.wheres, self.peers = y, ys, self.y_peers
 
     def send(self, src, dst, peer):
         copy = remote(src, dst, self.send_sem.at[self.used], self.recv_sem.at[self.used], peer)
@@ -312,37 +319,58 @@
 
     def begin(self):
         xh, y, core, xl, z = place()
-        ys, xs, y_peers, x_peers, other = plane()
         target = self.held.at[xh, y, core, xl]
-        peers = y_peers if self.y_first else x_peers
+        peers = self.y_peers if self.y_first else self.x_peers
         self.first = [self.send(self.own, target, peer) for peer in peers]
 
+    def half(self, where, k):
+        if self.y_first:
+            return self.held.at[where[0], pl.ds(2 * k, 2), self.core, where[1]]
+        return self.held.at[k, where, self.core]
+
     def line(self, where):
-        xh, y, core, xl, z = place()
         if self.y_first:
-            return self.held.at[where[0], :, core, where[1]]
-        return self.held.at[:, where, core, :]
+            return self.held.at[where[0], :, self.core, where[1]]
+        return self.held.at[:, where, self.core]
+
+    def give(self, where):
+        line = self.line(where)
+        self.third.append(self.send(line, line, self.other))
 
     def spread(self):
-        xh, y, core, xl, z = place()
-        ys, xs, y_peers, x_peers, other = plane()
         for copy in self.first:
             copy.wait_recv()
-        mine = self.line((xh, xl) if self.y_first else y)
-        peers = x_peers if self.y_first else y_peers
-        self.second = [self.send(mine, mine, peer) for peer in peers]
-        self.third = [self.send(mine, mine, other)] if self.shared else []
+        low_half, high_half = self.half(self.mine, 0), self.half(self.mine, 1)
+        ahead, behind = self.peers[:2]
+        self.second = [
+            self.send(high_half, high_half, ahead),
+            self.send(low_half, low_half, behind),
+            self.send(low_half, low_half, ahead),
+            self.send(high_half, high_half, behind),
+        ]
+        if self.shared:
+            self.give(self.mine)
+
+    def relay(self):
+        ahead, behind = self.peers[:2]
+        self.second[0].wait_recv()
+        part = self.half(self.wheres[1], 1)
+        self.second.append(self.send(part, part, ahead))
+        self.second[1].wait_recv()
+        part = self.half(self.wheres[0], 0)
+        self.second.append(self.send(part, part, behind))
 
     def share(self):
-        ys, xs, y_peers, x_peers, other = plane()
-        wheres = xs if self.y_first else ys
-        for copy, where in zip(self.second, (wheres[1], wheres[0], wheres[2])):
-            copy.wait_recv()
-            line = self.line(where)
-            self.third.append(self.send(line, line, other))
+        self.second[2].wait_recv()
+        self.give(self.wheres[1])
+        self.second[3].wait_recv()
+        self.give(self.wheres[0])
+        self.second[4].wait_recv()
+        self.second[5].wait_recv()
+        self.give(self.wheres[2])
 
     def end(self):
-        for copy in self.third if self.shared else self.second:
+        for copy in self.third if self.shared else self.second[2:]:
             copy.wait_recv()
         for copy in self.copies:
             copy.wait_send()
@@ -358,35 +386,45 @@
 def front_kernel(*refs):
     (hidden, cotangent, gain, m_in, m_expand, m_out, m_shrink) = refs[:7]
     (cos_ref, sin_ref, prefix) = refs[7:10]
-    (first_to, shrunk_all, in_to, gate_all, up_all, out_all, shrink_all) = refs[10:17]
-    (turned_to, rows_to, lines_to, attended, tokens, log_total, total) = refs[17:24]
-    (first_all, shrunk, in_all, w_gate, w_up, w_out, w_shrink) = refs[24:31]
-    (turned, kv_rows, kv_lines, key_cos, key_sin) = refs[31:36]
-    (packed, held_rows, parts, came, sums) = refs[36:41]
-    (ring_send, ring_recv, plane_send, plane_recv) = refs[41:45]
-    (kv_send, kv_recv, own_sem, out_sem) = refs[45:]
+    (first_to, shrunk_all, query_to, rest_to) = refs[10:14]
+    (gate_all, up_all, out_all, shrink_all) = refs[14:18]
+    (turned_to, rows_to, lines_to, attended, tokens, log_total, total) = refs[18:25]
+    (first_all, shrunk, in_query, in_rest, w_gate, w_up, w_out, w_shrink) = refs[25:33]
+    (turned, kv_rows, kv_lines, key_cos, key_sin) = refs[33:38]
+    (packed, held_rows, own_tokens) = refs[38:41]
+    (ring_send, ring_recv, plane_send, plane_recv, out_send, out_recv) = refs[41:47]
+    (kv_send, kv_recv, token_send, token_recv, own_sem, out_sem) = refs[47:]
     xh, y, core, xl, z = place()
     z, zp, z2, zm, up, down = ring_peers()
     ys, xs, y_peers, x_peers, other = plane()
     beside = device(xh, y, core, 1 - xl, z)
-    peers = [up, down, other] + y_peers + x_peers
+    across = device(xh, y, core, xl, z2)
+    peers = [up, down, across, other] + y_peers + x_peers
     hail(peers)
     low = jnp.bfloat16
-    in_own = in_all.at[xh, y, core, xl]
-    in_own[...] = m_in[...].astype(low)
-    w_out[...] = m_out[...].astype(low)
+    query_own, rest_own = in_query.at[xh, y, core, xl], in_rest.at[xh, y, core, xl]
+    query_own[...] = m_in[:, :384].astype(low)
+    rest_own[...] = m_in[:, 384:].astype(low)
+    w_out[z] = m_out[...].astype(low)
     rows = hidden[...].astype(jnp.float32)
     scaling = lax.rsqrt(jnp.mean(rows * rows, axis=-1, keepdims=True) + EPS)
     first_all[z] = (rows * scaling * gain[...]).astype(low)
     meet(peers)
-    owns = (in_own, w_out, w_gate, w_up, w_shrink)
-    helds = (in_all, out_all, gate_all, up_all, shrink_all)
+    out_copies = [
+        remote(w_out.at[z], w_out.at[z], out_send.at[i], out_recv.at[i], peer)
+        for i, peer in enumerate((up, down, across))
+    ]
+    for copy in out_copies:
+        copy.start()
+    owns = (query_own, rest_own, w_out, w_gate, w_up, w_shrink)
+    helds = (in_query, in_rest, out_all, gate_all, up_all, shrink_all)
     gathers = [
-        PlaneGather(own, held, i == 4, i < 2, plane_send.at[i], plane_recv.at[i])
-        for i, (own, held) in enumerate(zip(owns, helds))
+        PlaneGather(own, held, y_first, i < 3, plane_send.at[i], plane_recv.at[i])
+        for i, (own, held, y_first) in enumerate(zip(owns, helds, GATHER_TURNS))
     ]
-    for gather in gathers[:2]:
-        gather.begin()
+    query_gather, rest_gather, out_gather, *feed_gathers = gathers
+    query_gather.begin()
+    rest_gather.begin()
     ring = ring_gather_begin(first_all.at[z], first_all, ring_send.at[0], ring_recv.at[0])
     w_gate[...] = m_expand[0].astype(low)
     w_up[...] = m_expand[1].astype(low)
@@ -394,28 +432,40 @@
     shrunk[...] = (RESID * cotangent[...].astype(jnp.float32)).astype(low)
     keeps = [
         pltpu.make_async_copy(own, held.at[xh, y, core, xl], own_sem.at[i])
-        for i, (own, held) in enumerate(zip(owns[1:], helds[1:]))
+        for i, (own, held) in enumerate(zip(owns[3:], helds[3:]))
     ]
-    keeps.append(pltpu.make_async_copy(shrunk, shrunk_all.at[z], own_sem.at[4]))
+    keeps.append(pltpu.make_async_copy(shrunk, shrunk_all.at[z], own_sem.at[3]))
     for keep in keeps:
         keep.start()
+    for copy in out_copies:
+        copy.wait_recv()
+    out_gather.begin()
+    keeps.append(pltpu.make_async_copy(w_out, out_all.at[xh, y, core, xl], own_sem.at[4]))
+    keeps[-1].start()
+    query_gather.spread()
+    rest_gather.spread()
     for keep in keeps:
         keep.wait()
-    for gather in gathers[:2]:
-        gather.spread()
-    for gather in gathers[2:4]:
+    for gather in feed_gathers:
         gather.begin()
     key_tables(cos_ref, sin_ref, key_cos, key_sin)
+    query_gather.relay()
+    rest_gather.relay()
     ring = ring_gather_forward(first_all, ring, ring_send.at[0], ring_recv.at[0])
-    gathers[0].share()
-    gathers[1].share()
-    gathers[4].begin()
-    for gather in gathers[2:4]:
-        gather.spread()
-    gathers[0].end()
+    out_gather.spread()
+    query_gather.share()
+    rest_gather.share()
+    query_gather.end()
+    rest_gather.end()
 
     def project(c, rows):
-        out = nn(first_all[c], in_all[...].reshape(1536, 640))
+        out = jnp.concatenate(
+            [
+                nn(first_all[c], in_query[...].reshape(1536, 384)),
+                nn(first_all[c], in_rest[...].reshape(1536, 256)),
+            ],
+            axis=1,
+        )
         packed[rows] = out
         for g in range(HEADS):
             block = out[:, g * 320 + 192 : g * 320 + 320]
@@ -437,6 +487,9 @@
         mine = kv_rows.at[:, pl.ds(pl.multiple_of(xl * 896 + c * 224, 16), 224)]
         kv_copies.append(remote(mine, mine, kv_send.at[i], kv_recv.at[i], beside))
         kv_copies[-1].start()
+    out_gather.relay()
+    for gather in feed_gathers:
+        gather.spread()
     later = ring_gather_begin(shrunk, shrunk_all, ring_send.at[1], ring_recv.at[1])
     saves = []
 
@@ -445,7 +498,8 @@
         saves[-1].start()
 
     save(first_all, first_to)
-    save(in_all, in_to)
+    save(in_query, query_to)
+    save(in_rest, rest_to)
 
     def turn_block(b, carry):
         columns = pl.ds(pl.multiple_of(b * 128, 128), 128)
@@ -463,7 +517,6 @@
     save(turned, turned_to)
     for copy in kv_copies:
         copy.wait_recv()
-    gathers[4].spread()
     for g in range(HEADS):
         kv_lines[g] = jnp.transpose(kv_rows[g].astype(jnp.float32)).astype(low)
     save(kv_rows, rows_to)
@@ -511,41 +564,48 @@
         columns = pl.ds(pl.multiple_of(b * 128, 128), 128)
         tokens[columns] = jnp.transpose(attended[:, columns].astype(jnp.float32)).astype(low)
 
-    def apply(c):
-        mine = pl.ds(pl.multiple_of(c * 224, 16), 224)
-        parts[c] = nt(tokens[mine], held_rows[...].reshape(1536, 384)).astype(low)
+    def post(c, i, peer):
+        mine = tokens.at[pl.ds(pl.multiple_of(c * 224, 16), 224)]
+        copy = remote(mine, own_tokens.at[z], token_send.at[i], token_recv.at[i], peer)
+        copy.start()
+        return copy
 
     lax.fori_loop(8, 14, far_heads, 0)
+    for gather in feed_gathers:
+        gather.relay()
     later = ring_gather_forward(shrunk_all, later, ring_send.at[1], ring_recv.at[1])
-    gathers[1].end()
-    fetch = pltpu.make_async_copy(out_all, held_rows, out_sem)
-    fetch.start()
     for i in range(4, 7):
         lay(arrival(z, i))
-    fetch.wait()
-    apply(z2)
-    far = ring_scatter_far(parts, came, ring_send.at[2], ring_recv.at[2])
+    token_copies = [post(z2, 0, across)]
+    out_gather.share()
     lax.fori_loop(0, 2, beside_block, 0)
     lax.fori_loop(4, 8, near_heads, 0)
     for i in range(1, 4):
         lay(arrival(z, i))
-    apply(zp)
-    apply(zm)
-    near = ring_scatter_near(parts, came, ring_send.at[2], ring_recv.at[2])
-    scatter = ring_scatter_forward(
-        parts, came, sums, far + near, ring_send.at[2], ring_recv.at[2]
-    )
+    token_copies += [post(zp, 1, up), post(zm, 2, down)]
+    out_gather.end()
+    fetch = pltpu.make_async_copy(out_all, held_rows, out_sem)
+    fetch.start()
     lax.fori_loop(0, 2, own_block, 0)
     lay(2 * z)
-    apply(z)
-    for gather in gathers[2:]:
+    own_tokens[z] = tokens[pl.ds(pl.multiple_of(z * 224, 16), 224)]
+    fetch.wait()
+    for copy in token_copies:
+        copy.wait_recv()
+    projected = jnp.zeros(total.shape, jnp.float32)
+    for c in range(4):
+        projected = projected + nt(own_tokens[c], held_rows[:, :, :, :, c].reshape(1536, 384))
+    total[...] = projected
+    for gather in feed_gathers:
         gather.end()
     ring_gather_end(later)
-    for copy in kv_copies + ring:
+    for copy in kv_copies + ring + token_copies + out_copies:
         copy.wait_send()
     for copy in saves:
         copy.wait()
-    ring_scatter_end(parts, came, total, scatter)
+
+
+GATHER_TURNS = (True, False, False, True, True, False)
 
 
 def front(hidden, cotangent, gain, weights, tables, prefix):
@@ -554,10 +614,11 @@
     rows, width = hidden.shape
     low, full = jnp.bfloat16, jnp.float32
     block = (2, 4, 2, 2, 48)
-    first_shape, in_shape = (4, rows, width), block + (640,)
+    first_shape, in_shapes = (4, rows, width), (block + (384,), block + (256,))
+    out_shape = block[:4] + (4, 48, 384)
     turned_shape, rows_shape, lines_shape = (384, 896), (HEADS, 1792, 128), (HEADS, 128, 1792)
-    kept = (first_shape, (4, rows, width), in_shape) + (block + (960,),) * 2
-    kept += (block + (384,), block + (960,), turned_shape, rows_shape, lines_shape)
+    kept = (first_shape, (4, rows, width)) + in_shapes + (block + (960,),) * 2
+    kept += (out_shape, block + (960,), turned_shape, rows_shape, lines_shape)
     outs = pl.pallas_call(
         front_kernel,
         out_shape=(
@@ -568,14 +629,15 @@
             jax.ShapeDtypeStruct((rows, width), full),
         ),
         in_specs=[whole] * 9 + [pl.BlockSpec(memory_space=pltpu.SMEM)],
-        out_specs=(any_place,) * 10 + (whole,) * 4,
+        out_specs=(any_place,) * 11 + (whole,) * 4,
         scratch_shapes=[
             pltpu.VMEM(first_shape, low),
             pltpu.VMEM((rows, width), low),
-            pltpu.VMEM(in_shape, low),
+            pltpu.VMEM(in_shapes[0], low),
+            pltpu.VMEM(in_shapes[1], low),
             pltpu.VMEM((48, 960), low),
             pltpu.VMEM((48, 960), low),
-            pltpu.VMEM((48, 384), low),
+            pltpu.VMEM((4, 48, 384), low),
             pltpu.VMEM((48, 960), low),
             pltpu.VMEM(turned_shape, low),
             pltpu.VMEM(rows_shape, low),
@@ -583,17 +645,19 @@
             pltpu.VMEM((896, 128), full),
             pltpu.VMEM((896, 128), full),
             pltpu.VMEM((896, 640), full),
-            pltpu.VMEM(block + (384,), low),
-            pltpu.VMEM((4, rows, width), low),
-            pltpu.VMEM((6, rows // 2, width), low),
-            pltpu.VMEM((2, rows // 2, width), low),
-            pltpu.SemaphoreType.DMA((3, 6)),
-            pltpu.SemaphoreType.DMA((3, 6)),
-            pltpu.SemaphoreType.DMA((5, 10)),
-            pltpu.SemaphoreType.DMA((5, 10)),
+            pltpu.VMEM(out_shape, low),
+            pltpu.VMEM((4, rows, 384), low),
+            pltpu.SemaphoreType.DMA((2, 6)),
+            pltpu.SemaphoreType.DMA((2, 6)),
+            pltpu.SemaphoreType.DMA((6, 13)),
+            pltpu.SemaphoreType.DMA((6, 13)),
+            pltpu.SemaphoreType.DMA((3,)),
+            pltpu.SemaphoreType.DMA((3,)),
             pltpu.SemaphoreType.DMA((4,)),
             pltpu.SemaphoreType.DMA((4,)),
-            pltpu.SemaphoreType.DMA((10,)),
+            pltpu.SemaphoreType.DMA((3,)),
+            pltpu.SemaphoreType.DMA((3,)),
+            pltpu.SemaphoreType.DMA((11,)),
             pltpu.SemaphoreType.DMA,
         ],
         compiler_params=pltpu.CompilerParams(
@@ -890,8 +954,8 @@
 
 
 def back_kernel(*refs):
-    (own, out_from, in_from, first_from, out_terms) = refs[:5]
-    gradients = refs[5:8]
+    (own, out_from, query_from, rest_from, first_from, out_terms) = refs[:6]
+    gradients, refs = refs[6:9], refs[1:]
     (turned, kv_rows, kv_lines, attended, tokens, log_total) = refs[8:14]
     (cos_ref, sin_ref, hidden, gain_two, prefix) = refs[14:19]
     (shrunk_total, first_total) = refs[19:21]
@@ -938,17 +1002,18 @@
         copy.start()
         return copy
 
-    load_out = load(out_from, w_out, 0)
+    load_out = load(out_from.at[:, :, :, :, z], w_out, 0)
     keep = load(own, proj_all.at[z], 1)
     staged = [feed[i].stage(stages[i], load_sem.at[2 + i]) for i in range(2)]
     load_terms = load(out_terms, parts, 5)
-    load_in = load(in_from, w_in, 6)
+    load_query = load(query_from, w_in.at[:, pl.ds(0, 384)], 6)
+    load_rest = load(rest_from, w_in.at[:, pl.ds(384, 256)], 8)
 
     def give(c, start=0, count=224):
         rows = pl.ds(pl.multiple_of(c * 224 + start, 16), count)
-        grad_tokens[rows] = nn(proj_all[c, start : start + count], w_out[...]).astype(
-            jnp.bfloat16
-        )
+        grad_tokens[rows] = nn(
+            proj_all[c, start : start + count], w_out[...].reshape(1536, 384)
+        ).astype(jnp.bfloat16)
 
     def lay(b):
         columns = pl.ds(pl.multiple_of(b * 128, 128), 128)
@@ -1079,7 +1144,8 @@
     for scatter in feed:
         scatter.line()
     out_scatter.line()
-    load_in.wait()
+    load_query.wait()
+    load_rest.wait()
     load_first.wait()
     ring_scatter_end(parts, came_one, shrunk_total, shrunk)
     for g in range(HEADS):
@@ -1151,7 +1217,7 @@
 
 
 def back(
-    own, w_out, w_in, first_all, out_terms, gradients, saved, tables, hidden, gain_two, prefix
+    own, w_out, w_query, w_rest, first_all, out_terms, gradients, saved, tables, hidden, gain_two, prefix
 ):
     any_place = pl.BlockSpec(memory_space=pl.ANY)
     whole = pl.BlockSpec(memory_space=pltpu.VMEM)
@@ -1167,13 +1233,13 @@
         + tuple(jax.ShapeDtypeStruct((48, w), full) for w in widths)
         + (jax.ShapeDtypeStruct((8, 512), full),),
         in_specs=[whole]
-        + [any_place] * 7
+        + [any_place] * 8
         + [whole] * 10
         + [pl.BlockSpec(memory_space=pltpu.SMEM)],
         out_specs=(whole,) * 8,
         scratch_shapes=[
             pltpu.VMEM((4, rows, width), low),
-            pltpu.VMEM((1536, 384), low),
+            pltpu.VMEM((2, 4, 2, 2, 48, 384), low),
             pltpu.VMEM((1536, 640), low),
             pltpu.VMEM((896, 384), low),
             pltpu.VMEM((384, 896), low),
@@ -1200,7 +1266,7 @@
             pltpu.SemaphoreType.DMA((5, 10)),
             pltpu.SemaphoreType.DMA((2,)),
             pltpu.SemaphoreType.DMA((2,)),
-            pltpu.SemaphoreType.DMA((8,)),
+            pltpu.SemaphoreType.DMA((9,)),
             pltpu.SemaphoreType.DMA((13,)),
             pltpu.SemaphoreType.DMA((13,)),
         ],
@@ -1210,7 +1276,8 @@
     )(
         own,
         w_out,
-        w_in,
+        w_query,
+        w_rest,
         first_all,
         out_terms,
         *(g.reshape(2, 4, 2, 2, 48, g.shape[-1]) for g in gradients),
@@ -1344,7 +1411,8 @@
     (
         first_all,
         shrunk_all,
-        w_in,
+        w_query,
+        w_rest,
         w_gate,
         w_up,
         w_out,
@@ -1378,8 +1446,9 @@
     )
     shrunk, grad_first, *gradients, sums = back(
         projected_gradient,
-        w_out.reshape(1536, 384),
-        w_in.reshape(1536, 640),
+        w_out,
+        w_query.reshape(1536, 384),
+        w_rest.reshape(1536, 256),
         first_all,
         out_parts,
         (grad_gate, grad_up, grad_shrink),

time: 253 us -> 251 us (level)
    pallas_call x1, Pallas kernels: 82.6 us -> 77.5 us  [front(): pl.pallas_call(front_kernel, out_shape=(*(jax.ShapeDtypeStruct(shape, low...]
where the time goes in v7:
time: 251 us; the launch traced here: 246 us
  Pallas kernels  242 us (96%)
    pallas_call x1, Pallas kernels, back(): pl.pallas_call(back_kernel, out_shape=(jax.ShapeDtypeStruct((rows, width)...  100 us
    pallas_call x1, Pallas kernels, front(): pl.pallas_call(front_kernel, out_shape=(*(jax.ShapeDtypeStruct(shape, low...  77.5 us
    pallas_call x1, Pallas kernels, middle(): pl.pallas_call(middle_kernel, out_shape=(jax.ShapeDtypeStruct((rows, widt...  58 us
    pallas_call x1, Pallas kernels, finish(): pl.pallas_call(finish_kernel, grid=(2,), out_shape=(jax.ShapeDtypeStruct(...  5.96 us

profile of v7, /device:TPU:0, one launch (start us, length us, event | category | flops | bytes accessed | tf_op | source)
XLA Modules:
  0.0 246.4 jit_solution(10305110767502307204)
XLA Ops:
  1.3 0.7 convert_reduce_fusion
  2.0 1.4 fusion
  3.4 1.2 multiply_sine_fusion
  4.6 77.5 %shard_map.322 = (bf16[4,224,1536]{2,1,0:T(8,128)(2,1)}, bf16[4,224,1536]{2,1,0:T(8,128)(2,1)}, bf16[2,4,2,2,48,384]{5,4,3,2,1,0:T(8,128)(2,1)}, bf16[2,4,2,2,48...) custom-call(bf16[224,1536]{1,0:T(8,128)(2,1)} %bitcast.22, ...), custom_call_target="tpu_custom_call" | custom-call | tf_op jit(solution)/shard_map/pallas_call | solution.py:622
  82.1 58.0 %shard_map.323 = (f32[224,1536]{1,0:T(8,128)}, f32[224,1536]{1,0:T(8,128)}, bf16[224,1536]{1,0:T(8,128)(2,1)}, f32[1,1536]{1,0:T(1,128)}, bf16[1536,960]{1,0:T(8...) custom-call(bf16[224,1536]{1,0:T(8,128)(2,1)} %bitcast.23, ...), custom_call_target="tpu_custom_call" | custom-call | tf_op jit(solution)/shard_map/pallas_call | solution.py:801
  140.1 100.1 %shard_map.324 = (f32[224,1536]{1,0:T(8,128)}, f32[224,1536]{1,0:T(8,128)}, f32[48,960]{1,0:T(8,128)}, f32[48,960]{1,0:T(8,128)}, f32[48,960]{1,0:T(8,128)}, /*i...) custom-call(bf16[224,1536]{1,0:T(8,128)(2,1)} %get-tuple-element.72.refs_0_, ...), custom_call_target="tpu_custom_call" | custom-call | tf_op jit(solution)/shard_map/pallas_call | solution.py:1230
  240.2 6.0 %shard_map.325 = (bf16[224,1536]{1,0:T(8,128)(2,1)}, f32[224,1536]{1,0:T(8,128)}, f32[1,1]{1,0:T(1,128)}, f32[2,1536]{1,0:T(2,128)}, f32[2,1536]{1,0:T(2,128)}, ...) custom-call(f32[8,512]{1,0:T(8,128)} %get-tuple-element.88.refs_0_, ...), custom_call_target="tpu_custom_call" | custom-call | tf_op jit(solution)/shard_map/pallas_call | solution.py:1359
  (1 shorter events, 0.0 us)

commit v8 on v7

--- a/solution.py
+++ b/solution.py
@@ -7,6 +7,7 @@
 from jax.experimental import pallas as pl
 from jax.experimental.pallas import tpu as pltpu
 from jax.sharding import PartitionSpec as P
+import numpy as np
 
 HD = 64
 GROUP = 3
@@ -31,9 +32,8 @@
 
 
 def angles(places):
-    half_width = HD // 2
-    frequency = ROPE_BASE ** (-2.0 * jnp.arange(half_width, dtype=jnp.float32) / HD)
-    phase_turn = places.astype(jnp.float32)[None, :] * frequency[:, None]
+    frequency = (ROPE_BASE ** (-2.0 * np.arange(HD // 2) / HD)).astype(np.float32)
+    phase_turn = places.astype(jnp.float32) * frequency[:, None]
     return (jnp.cos(phase_turn), jnp.sin(phase_turn))
 
 
@@ -408,7 +408,7 @@
     w_out[z] = m_out[...].astype(low)
     rows = hidden[...].astype(jnp.float32)
     scaling = lax.rsqrt(jnp.mean(rows * rows, axis=-1, keepdims=True) + EPS)
-    first_all[z] = (rows * scaling * gain[...]).astype(low)
+    first_all[z] = (rows * scaling * gain[0:1]).astype(low)
     meet(peers)
     out_copies = [
         remote(w_out.at[z], w_out.at[z], out_send.at[i], out_recv.at[i], peer)
@@ -705,7 +705,7 @@
     rows = hidden[...].astype(jnp.float32) + RESID * projected[...]
     residual[...] = rows
     scaling = lax.rsqrt(jnp.mean(rows * rows, axis=-1, keepdims=True) + EPS)
-    second_all[z] = (rows * scaling * gain[...]).astype(jnp.bfloat16)
+    second_all[z] = (rows * scaling * gain[1:2]).astype(jnp.bfloat16)
     meet([up, down, other])
     ring = ring_gather_begin(second_all.at[z], second_all, ring_send.at[0], ring_recv.at[0])
     shares = [
@@ -783,7 +783,7 @@
     normed = rows * scaling
     gradient = total[...]
     gain_two[...] = jnp.sum(gradient * normed, axis=0, keepdims=True)
-    gradient = gradient * gain[...]
+    gradient = gradient * gain[1:2]
     back = cotangent[...].astype(jnp.float32) + scaling * (
         gradient - normed * jnp.mean(gradient * normed, axis=-1, keepdims=True)
     )
@@ -1407,7 +1407,7 @@
         (expand_weight, expand_first, expand_second),
         (shrink_weight.T, shrink_first.T, shrink_second.T),
     )
-    tables = angles(positions[0])
+    tables = angles(positions)
     (
         first_all,
         shrunk_all,
@@ -1427,7 +1427,7 @@
     ) = front(
         hidden,
         upstream,
-        norm_gains[:1],
+        norm_gains,
         (input_weight, expand_weight, output_weight.T, shrink_weight.T),
         tables,
         prefix,
@@ -1442,7 +1442,7 @@
         grad_shrink,
         out_parts,
     ) = middle(
-        hidden, upstream, projected, norm_gains[1:], shrunk_all, w_gate, w_up, w_shrink
+        hidden, upstream, projected, norm_gains, shrunk_all, w_gate, w_up, w_shrink
     )
     shrunk, grad_first, *gradients, sums = back(
         projected_gradient,

time: 251 us -> 251 us (level)
  no operation moved by 1% of the time
where the time goes in v8:
time: 251 us; the launch traced here: 246 us
  Pallas kernels  241 us (96%)
  other arithmetic  2.52 us (1%)
    pallas_call x1, Pallas kernels, back(): pl.pallas_call(back_kernel, out_shape=(jax.ShapeDtypeStruct((rows, width)...  99.8 us
    pallas_call x1, Pallas kernels, front(): pl.pallas_call(front_kernel, out_shape=(*(jax.ShapeDtypeStruct(shape, low...  77.5 us
    pallas_call x1, Pallas kernels, middle(): pl.pallas_call(middle_kernel, out_shape=(jax.ShapeDtypeStruct((rows, widt...  58.1 us
    pallas_call x1, Pallas kernels, finish(): pl.pallas_call(finish_kernel, grid=(2,), out_shape=(jax.ShapeDtypeStruct(...  5.96 us

profile of v8, /device:TPU:0, one launch (start us, length us, event | category | flops | bytes accessed | tf_op | source)
XLA Modules:
  0.0 245.5 jit_solution(7849084946482080077)
XLA Ops:
  1.3 0.7 convert_reduce_fusion
  2.0 1.8 multiply_sine_fusion
  3.8 77.5 %shard_map.331 = (bf16[4,224,1536]{2,1,0:T(8,128)(2,1)}, bf16[4,224,1536]{2,1,0:T(8,128)(2,1)}, bf16[2,4,2,2,48,384]{5,4,3,2,1,0:T(8,128)(2,1)}, bf16[2,4,2,2,48...) custom-call(bf16[224,1536]{1,0:T(8,128)(2,1)} %bitcast.22, ...), custom_call_target="tpu_custom_call" | custom-call | tf_op jit(solution)/shard_map/pallas_call | solution.py:622
  81.4 58.1 %shard_map.332 = (f32[224,1536]{1,0:T(8,128)}, f32[224,1536]{1,0:T(8,128)}, bf16[224,1536]{1,0:T(8,128)(2,1)}, f32[1,1536]{1,0:T(1,128)}, bf16[1536,960]{1,0:T(8...) custom-call(bf16[224,1536]{1,0:T(8,128)(2,1)} %bitcast.23, ...), custom_call_target="tpu_custom_call" | custom-call | tf_op jit(solution)/shard_map/pallas_call | solution.py:801
  139.5 99.8 %shard_map.333 = (f32[224,1536]{1,0:T(8,128)}, f32[224,1536]{1,0:T(8,128)}, f32[48,960]{1,0:T(8,128)}, f32[48,960]{1,0:T(8,128)}, f32[48,960]{1,0:T(8,128)}, /*i...) custom-call(bf16[224,1536]{1,0:T(8,128)(2,1)} %get-tuple-element.72.refs_0_, ...), custom_call_target="tpu_custom_call" | custom-call | tf_op jit(solution)/shard_map/pallas_call | solution.py:1230
  239.3 6.0 %shard_map.334 = (bf16[224,1536]{1,0:T(8,128)(2,1)}, f32[224,1536]{1,0:T(8,128)}, f32[1,1]{1,0:T(1,128)}, f32[2,1536]{1,0:T(2,128)}, f32[2,1536]{1,0:T(2,128)}, ...) custom-call(f32[8,512]{1,0:T(8,128)} %get-tuple-element.88.refs_0_, ...), custom_call_target="tpu_custom_call" | custom-call | tf_op jit(solution)/shard_map/pallas_call | solution.py:1359
